TPU v7x, 32 devices: a whole 2x2x4 slice. The times are simulated.
32 devices in a mesh: ctx: 4 (over x, core), tp: 4 (over z), fsdp: 2 (over y).
Axes of the slice: x: 2, y: 2, z: 4, core: 2. Of those that a mesh axis runs over, the one named last changes fastest.
Arguments:
- tokens: bfloat16 [8192, 8192], P(('ctx', 'fsdp'), 'tp'), may hold values from -6 to 6
- weight: bfloat16 [8192, 3, 4096], P('fsdp', None, 'tp'), may hold values from -0.0625 to 0.0625
- rate: float32 [4096, 16], P(('tp', 'fsdp')), may hold values from 1.2207031e-06 to 0.1
- residue: float32 [4096, 16], P(('tp', 'fsdp')), may hold values from -3 to 3
- skip: float32 [4096], P(('tp', 'fsdp')), may hold values from 0.5 to 1.5
- order: int32 [8], replicated, may hold values from 0 to 7, each once
Outputs:
- gated: bfloat16 [4096, 8192], P(('tp', 'fsdp'), 'ctx')
Inputs may be any that keep to these rules, and one draw needn't show every extreme that they name: order is a permutation: every segment number appears once.
All inputs are finite; a program needn't handle non-finite values.
Results may differ from a plain program's by a relative error of at most 0.006.
Values may be sent and summed in bfloat16 or wider, within the bound.
No kernel may reach another device: no remote copies, remote signals or barrier semaphores. Data moves between devices by JAX's collectives and lax.ppermute only.
A program may use at most 256 MiB of HBM per device.

v0:
```python
import jax
import jax.numpy as jnp
from jax import lax
from jax.sharding import PartitionSpec as P


def swapped(block, axis, distance):
    count = lax.axis_size(axis)
    route = []
    for low in range(count):
        high = low | 1 << distance
        if high != low and high < count:
            route += [(low, high), (high, low)]
    return lax.ppermute(block, axis, route)


def pole_gain(rate, residue, length):
    return residue * jnp.sqrt(jnp.maximum(-jnp.expm1(-2.0 * rate), 1.0 / length))


def carry_states(pieces, seg_ids, mine, rate, seg_len):
    distance = mine[:, None] - 1 - seg_ids[None, :]
    earlier = distance >= 0
    span = jnp.maximum(distance, 0).astype(jnp.float32) * seg_len
    factor = jnp.where(
        earlier[:, :, None, None], jnp.exp(-rate[None, None, :, :] * span[:, :, None, None]), 0.0
    )
    return jnp.sum(factor * pieces[None], axis=1)


def per_device(tokens, weight, rate, residue, skip, order):
    seg_len = tokens.shape[0]
    n_ctx = lax.axis_size("ctx")
    seq_len = 2 * n_ctx * seg_len
    pair_index = lax.axis_index("fsdp")
    ctx_index = lax.axis_index("ctx")
    whole = lax.all_gather(tokens, "tp", axis=1, tiled=True)
    half = weight.shape[0]
    kept = lax.dynamic_slice_in_dim(whole, pair_index * half, half, 1)
    given = lax.dynamic_slice_in_dim(whole, (1 - pair_index) * half, half, 1)
    partner = swapped(given, "fsdp", 0)
    both_rows = jnp.where(
        pair_index == 0,
        jnp.concatenate([kept, partner], axis=0),
        jnp.concatenate([partner, kept], axis=0),
    )
    projected = lax.psum_scatter(
        jnp.einsum("dkc,td->ckt", weight, both_rows, preferred_element_type=jnp.float32),
        "fsdp",
        scatter_dimension=0,
        tiled=True,
    ).astype(jnp.bfloat16)
    channels = projected.shape[0]
    query = projected[:, 0].astype(jnp.float32)
    product = projected[:, 1].astype(jnp.float32) * projected[:, 2].astype(jnp.float32)
    gain = pole_gain(rate, residue, float(seq_len))
    block_len = min(128, seg_len)
    block_count = seg_len // block_len
    highest = lax.Precision.HIGHEST
    lags = jnp.arange(block_len)
    lag_float = lags.astype(jnp.float32)
    lag_filter = jnp.einsum(
        "cr,crl->cl", gain, jnp.exp(-rate[:, :, None] * lag_float[None, None, :]), precision=highest
    )
    offsets = lags[:, None] - lags[None, :]
    toeplitz = jnp.where(
        (offsets >= 0)[None], jnp.take(lag_filter, jnp.maximum(offsets, 0), axis=1), 0.0
    )
    prod_blocks = product.reshape(channels, 2, block_count, block_len)
    inside = jnp.einsum("cij,cmbj->cmbi", toeplitz, prod_blocks, precision=highest)
    tail = jnp.exp(-rate[:, :, None] * (block_len - 1 - lag_float)[None, None, :])
    block_ends = jnp.einsum("crj,cmbj->crmb", tail, prod_blocks, precision=highest)
    block_ids = jnp.arange(block_count)
    block_gap = block_ids[:, None] - 1 - block_ids[None, :]
    block_mask = block_gap >= 0
    within = jnp.where(
        block_mask[None, None],
        jnp.exp(
            -rate[:, :, None, None]
            * (block_len * jnp.maximum(block_gap, 0).astype(jnp.float32))[None, None]
        ),
        0.0,
    )
    local_in = jnp.einsum("crab,crmb->crma", within, block_ends, precision=highest)
    to_end = jnp.exp(
        -rate[:, :, None]
        * (block_len * (block_count - 1 - block_ids).astype(jnp.float32))[None, None, :]
    )
    seg_end = jnp.einsum("crb,crmb->crm", to_end, block_ends, precision=highest)
    ends = seg_end.transpose(2, 0, 1)
    mine = lax.dynamic_slice_in_dim(order, 2 * ctx_index, 2)
    every_seg = jnp.arange(2 * n_ctx)
    placing = (mine[:, None] == every_seg[None, :]).astype(jnp.float32)
    slots = jnp.sum(placing[:, :, None, None] * ends[:, None], axis=0)
    totals = lax.psum(slots, "ctx")
    incoming = carry_states(totals, every_seg, mine, rate, seg_len)
    from_start = jnp.exp(
        -rate[:, :, None] * (block_len * block_ids.astype(jnp.float32))[None, None, :]
    )
    state_in = local_in + from_start[:, :, None, :] * incoming.transpose(1, 2, 0)[:, :, :, None]
    head = gain[:, :, None] * jnp.exp(-rate[:, :, None] * (lag_float + 1.0)[None, None, :])
    from_state = jnp.einsum("cri,crmb->cmbi", head, state_in, precision=highest)
    conv = (inside + from_state).reshape(channels, 2 * seg_len)
    return (query * (conv + skip[:, None] * product)).astype(jnp.bfloat16)


def solution(mesh):
    placed = (
        P(("ctx", "fsdp"), "tp"),
        P("fsdp", None, "tp"),
        P(("tp", "fsdp"), None),
        P(("tp", "fsdp"), None),
        P(("tp", "fsdp")),
        P(),
    )
    return jax.shard_map(
        per_device, mesh=mesh, in_specs=placed, out_specs=P(("tp", "fsdp"), "ctx"), check_vma=False
    )
```

profile of v0, /device:TPU:9, one launch (start us, length us, event | category | flops | bytes accessed | tf_op | source)
XLA Modules:
  0.0 1229.2 jit_solution(5580976601258650257)
XLA Ops:
  6.5 0.7 all-gather.2.cloned.1.call-update
  7.3 0.0 reduce-scatter.2.cloned.1.call-start
  7.3 286.8 %all-gather.2.cloned.1.call-done = bf16[1024,8192]{1,0:T(8,128)(2,1)} async-done(((bf16[1024,2048]{1,0:T(8,128)(2,1)}), bf16[1024,8192]{1,0:T(8,128)(2,1)}) %all-gather.2.cloned.1.call-update) | async-done | bytes 16777232 | tf_op jit(solution)/shard_map/all_gather | solution.py:37
  294.1 11.7 constant_dynamic-slice_fusion.1
  305.8 1.3 collective-permute-start
  307.0 180.5 %collective-permute-done = bf16[1024,4096]{1,0:T(8,128)(2,1)} collective-permute-done((bf16[1024,4096]{1,0:T(8,128)(2,1)}, bf16[1024,4096]{1,0:T(8,128)(2,1)}, u32[]{:S(2)}, u32[]{:S(2)}) %collective-permute-start) | collective-permute-done | bytes 8388640 | tf_op jit(solution)/shard_map/ppermute | solution.py:14
  487.6 70.5 %fusion.17 = f32[1024,3,2048]{0,2,1:T(8,128)} fusion(bf16[4096,3,1024]{2,0,1:T(8,128)(2,1)} %param.7, bf16[1024,4096]{1,0:T(8,128)(2,1)} %collective-permute-done, bf16[1024,4096]{1,0:T(8,128)(2,1)} %get-tuple-element.7, pred[]{:T(512)S(6)} %eq.18), kind=kOutput, calls=%fused_computation.18 | convolution fusion | flops 51615105024 | bytes 67108864 | tf_op jit(solution)/shard_map/dkc,td->ckt/dot_general | solution.py:48
  558.1 0.0 copy-start.11
  558.1 0.0 reduce-scatter.2.cloned.1.call-update
  558.1 0.3 all-reduce.2.cloned.1.call-start
  558.4 0.5 copy-done.8
  558.8 0.0 copy-done.9
  558.9 0.1 copy.27
  559.0 0.1 copy.48
  559.2 0.1 broadcast_add_fusion.1
  559.3 0.1 fusion.42
  559.4 0.1 convert_multiply_fusion.3
  559.4 0.1 compare_convert_fusion
  559.5 0.1 fusion.41
  559.6 0.1 convert_multiply_fusion.2
  559.7 1.7 exponential_select_fusion
  561.3 6.7 multiply_reduce_fusion
  568.0 4.4 multiply_exponential_fusion.1
  572.4 267.0 %reduce-scatter.2.cloned.1.call-done = f32[512,3,2048]{0,2,1:T(8,128)} async-done(((f32[1024,3,2048]{0,2,1:T(8,128)}), f32[512,3,2048]{0,2,1:T(8,128)}) %reduce-scatter.2.cloned.1.call-update) | async-done | bytes 12582928 | tf_op jit(solution)/shard_map/reduce_scatter | solution.py:47
  839.4 5.4 convert_element_type.76
  844.8 2.9 convert_multiply_fusion.1
  847.8 1.0 copy-done.1
  848.8 5.4 copy.29
  854.2 10.1 fusion.23
  864.3 10.9 copy.31
  875.2 58.8 %fusion.46 = f32[512,16,1,2]{3,2,1,0:T(1,128)} fusion(f32[512,16,8,1]{2,3,1,0:T(1,128)} %bitcast.68, f32[512,16,2,8]{3,2,1,0:T(2,128)} %copy.31), kind=kOutput, calls=%fused_computation.72 | convolution fusion | flops 1572864 | bytes 851968 | tf_op jit(solution)/shard_map/crb,crmb->crm/dot_general | solution.py:89
  934.0 5.4 copy.46
  939.4 0.8 multiply_reduce_fusion.2
  940.2 0.0 all-reduce.2.cloned.1.call-update
  940.3 25.6 %copy.32 = f32[512,16,8,8]{3,2,1,0:T(8,128)} copy(f32[512,16,8,8]{0,3,2,1:T(8,128)S(1)} %copy-done.2) | data formatting | bytes 4194304 | tf_op jit(solution)/shard_map/jit(_where)/select_n | solution.py:76
  965.9 0.1 copy.42
  966.1 64.3 %gather_fusion = f32[16384,512]{1,0:T(8,128)} fusion(f32[512,128]{0,1:T(8,128)S(1)} %copy.42, s32[16384]{0:T(1024)S(1)} %bitcast_clamp_fusion), kind=kCustom, calls=%fused_computation | custom fusion | bytes 67174400 | tf_op jit(solution)/shard_map/jit(_take)/gather | solution.py:67
  1030.3 35.7 %copy.28 = f32[128,128,512]{1,0,2:T(8,128)} copy(f32[128,128,512]{2,1,0:T(8,128)} %bitcast.66) | data formatting | bytes 67108864 | tf_op jit(solution)/shard_map/jit(_take)/gather | solution.py:67
  1066.1 0.0 all-reduce.2.cloned.1.call-done
  1066.1 1.1 multiply_reduce_fusion.1
  1067.3 3.5 copy.34
  1070.8 62.6 %multiply_add_fusion = f32[512,16,2,8]{3,2,1,0:T(2,128)} fusion(f32[512,16,2,8]{3,2,1,0:T(2,128)} %copy.31, f32[512,16,8,8]{3,2,1,0:T(8,128)} %copy.32, f32[512,16,2]{2,1,0:T(8,128)} %copy.34, f32[512,16,8]{2,1,0:T(8,128)} %get-tuple-element.9), kind=kOutput, calls=%fused_computation.21 | convolution fusion | flops 12845056 | bytes 3473408 | tf_op jit(solution)/shard_map/crab,crmb->crma/dot_general | solution.py:84
  1133.4 18.8 %fusion.20 = f32[512,2,8,128]{3,2,1,0:T(8,128)S(1)} fusion(f32[512,16,2,8]{3,2,1,0:T(2,128)} %multiply_add_fusion, f32[512,16]{1,0:T(8,128)S(1)} %copy-done.6, f32[128]{0:T(128)S(1)} %broadcast_add_fusion, f32[512,16]{1,0:T(8,128)S(1)} %copy-done.4), kind=kOutput, calls=%fused_computation.19 | convolution fusion | flops 203423744 | bytes 4784640 | tf_op jit(solution)/shard_map/cri,crmb->cmbi/dot_general | solution.py:102
  1152.3 0.0 copy-done
  1152.3 57.0 %fusion.37 = f32[512,2,8,128]{3,2,1,0:T(8,128)} fusion(f32[512,2,8,128]{3,2,1,0:T(8,128)S(1)} %fusion.20, f32[512,2,8,128]{3,2,1,0:T(8,128)S(1)} %copy-done, f32[128,128,512]{1,0,2:T(8,128)} %copy.28, pred[128,128]{1,0:T(8,128)(4,1)S(1)} %get-tuple-element.16, pred[128,128]{1,0:T(8,128)(4,1)S(1)} %get-tuple-element.15), kind=kOutput, calls=%fused_computation.45 | convolution fusion | flops 1628438528 | bytes 46170112 | tf_op jit(solution)/shard_map/cij,cmbj->cmbi/dot_general | solution.py:70
  1209.3 5.3 copy.37
  1214.6 5.2 fusion.25
  1219.8 2.4 copy.38
  (28 shorter events, 0.1 us)
Async XLA Ops:
  6.5 287.5 %all-gather.2.cloned.1.call-start = ((), (), s32[]{:S(2)}) async-start(), calls=%async_computation.1 | async-start | bytes 20971520 | tf_op jit(solution)/shard_map/all_gather | solution.py:37
  7.3 832.2 %reduce-scatter.2.cloned.1.call-start = ((), (), s32[]{:S(2)}) async-start(), calls=%async_computation.2 | async-start | bytes 37748736 | tf_op jit(solution)/shard_map/reduce_scatter | solution.py:47
  305.8 181.8 %collective-permute-start = (bf16[1024,4096]{1,0:T(8,128)(2,1)}, bf16[1024,4096]{1,0:T(8,128)(2,1)}, u32[]{:S(2)}, u32[]{:S(2)}) collective-permute-start(bf16[1024,4096]{1,0:T(8,128)(2,1)} %get-tuple-element.8), channel_id=1, source_target_pairs={{0,1},{1,0},{2,3},{3,2},{4,5},{5,4},{6,7},{7,6},{8,9},{9,8},{10,11... | collective-permute-start | bytes 25165832 | tf_op jit(solution)/shard_map/ppermute | solution.py:14
  558.1 0.8 copy-start.8
  558.1 0.8 copy-start.9
  558.1 1.1 copy-start.11
  558.1 508.0 %all-reduce.2.cloned.1.call-start = ((), (), s32[]{:S(2)}) async-start(), calls=%async_computation.3 | async-start | bytes 524288 | tf_op jit(solution)/shard_map/psum | solution.py:95
  559.0 295.2 %copy-start.3 = (f32[512,16]{1,0:T(8,128)}, f32[512,16]{1,0:T(8,128)S(1)}, u32[]{:S(2)}) copy-start(f32[512,16]{1,0:T(8,128)S(1)} %copy.27) | copy-start | bytes 98308
  559.1 13.2 %copy-start.5 = (f32[512,16]{1,0:T(8,128)}, f32[512,16]{1,0:T(8,128)S(1)}, u32[]{:S(2)}) copy-start(f32[512,16]{1,0:T(8,128)S(1)} %copy.48) | copy-start | bytes 98308
  844.8 4.0 copy-start.1
  934.0 6.2 copy-start.2
  940.3 25.7 %copy-start.7 = (f32[512,128]{1,0:T(8,128)S(1)}, f32[512,128]{1,0:T(8,128)}, u32[]{:S(2)}) copy-start(f32[512,128]{1,0:T(8,128)} %multiply_reduce_fusion) | copy-start | bytes 786436
  1070.8 62.6 %copy-start.4 = (f32[512,16]{1,0:T(8,128)S(1)}, f32[512,16]{1,0:T(8,128)}, u32[]{:S(2)}) copy-start(f32[512,16]{1,0:T(8,128)} %copy-done.3) | copy-start | bytes 98308
  1070.8 62.6 %copy-start.6 = (f32[512,16]{1,0:T(8,128)S(1)}, f32[512,16]{1,0:T(8,128)}, u32[]{:S(2)}) copy-start(f32[512,16]{1,0:T(8,128)} %copy-done.5) | copy-start | bytes 98308
  1133.4 18.8 %copy-start = (f32[512,2,8,128]{3,2,1,0:T(8,128)S(1)}, f32[512,2,8,128]{3,2,1,0:T(8,128)}, u32[]{:S(2)}) copy-start(f32[512,2,8,128]{3,2,1,0:T(8,128)} %copy.29) | copy-start | bytes 12582916
  1209.3 5.3 copy-start.10
Sparse Core Ops, SparseCore 0:
  8.9 285.1 all-gather.1
  558.2 281.1 reduce-scatter.1
  940.4 30.8 all-reduce.1
where the time goes:
time: 1240 us; the launch traced here: 1230 us
  waiting for transfers between devices  735 us (59%)
  matrix products  278 us (22%)
  local copies, waits for them, and re-layouts  172 us (14%)
  other arithmetic  28.8 us (2%)
  between operations  13.7 us (1%)
    all_gather x1, waiting for transfers between devices, per_device(): whole = lax.all_gather(tokens, 'tp', axis=1, tiled=True)  287 us
    reduce_scatter x1, waiting for transfers between devices, per_device(): lax.psum_scatter(jnp.einsum('dkc,td->ckt', weight, both_rows, preferred_e...  267 us
    ppermute x1, waiting for transfers between devices, swapped(): return lax.ppermute(block, axis, route)  181 us
    gather x2, local copies, waits for them, and re-layouts, per_device(): jnp.take(lag_filter, jnp.maximum(offsets, 0), axis=1)  100 us
    dot_general x1, matrix products, per_device(): jnp.einsum('dkc,td->ckt', weight, both_rows, preferred_element_type=jnp.f...  70.5 us
    dot_general x1, matrix products, per_device(): jnp.einsum('crab,crmb->crma', within, block_ends, precision=highest)  62.6 us
    dot_general x1, matrix products, per_device(): seg_end = jnp.einsum('crb,crmb->crm', to_end, block_ends, precision=highest)  58.8 us
    dot_general x1, matrix products, per_device(): jnp.einsum('cij,cmbj->cmbi', toeplitz, prod_blocks, precision=highest)  57 us
  transfers between devices with their start and end apart: 4, of which 3 were waited for; matrix products, arithmetic and copies ran while one was open for 11% of the time, Pallas kernels for 0%

commit v1 on v0

v1 whole, which is shorter than its diff:
```python
import functools

import jax
import jax.numpy as jnp
from jax import lax
from jax.experimental import pallas as pl
from jax.experimental.pallas import tpu as pltpu
from jax.sharding import PartitionSpec as P

MIB = 1 << 20
DEPTH = 512
CHUNKS = (256, 256, 256, 256)


def exchanged(block, axis, mask):
    count = lax.axis_size(axis)
    return lax.ppermute(block, axis, [(i, i ^ mask) for i in range(count)])


def pole_gain(rate, residue, length):
    return residue * jnp.sqrt(jnp.maximum(-jnp.expm1(-2.0 * rate), 1.0 / length))


def project_kernel(n_own, n_pieces, per_part, has_init, final, place, *refs):
    refs = list(refs)
    tokens = refs.pop(0)
    own = refs.pop(0) if n_own else None
    pieces = [refs.pop(0) for _ in range(n_pieces)]
    init = refs.pop(0) if has_init else None
    outs = [refs.pop(0) for _ in range(2 if final else 1)]
    x_buf, w_buf, x_sem, w_sem = refs[:4]
    acc = refs[4] if final else outs[0]
    rows = x_buf.shape[1]
    per_quarter = tokens.shape[2] // DEPTH
    pair, ctx = place[0], place[1]
    n_half = tokens.shape[0] * per_quarter // 2
    steps = n_own + n_pieces
    slots = x_buf.shape[0]

    def start(step):
        slot = lax.rem(step, slots)
        rest = step - n_own
        part = jnp.bitwise_xor(ctx, lax.div(rest, per_part))
        theirs = (1 - pair) * n_half + part * per_part + lax.rem(rest, per_part)
        block = jnp.where(step < n_own, pair * n_half + step, theirs)
        quarter = lax.div(block, per_quarter)
        column = pl.multiple_of(lax.rem(block, per_quarter) * DEPTH, DEPTH)
        pltpu.make_async_copy(
            tokens.at[quarter, :, pl.ds(column, DEPTH)], x_buf.at[slot], x_sem.at[slot]
        ).start()

        if n_own:
            @pl.when(step < n_own)
            def _():
                row = pl.multiple_of(step * DEPTH, DEPTH)
                pltpu.make_async_copy(
                    own.at[:, pl.ds(row, DEPTH), :], w_buf.at[slot], w_sem.at[slot]
                ).start()

        for n, piece in enumerate(pieces):
            @pl.when(rest == n)
            def _():
                pltpu.make_async_copy(piece, w_buf.at[slot], w_sem.at[slot]).start()

    for ahead in range(slots - 1):
        start(jnp.int32(ahead))
    if has_init:
        acc[...] = init[...]
    else:
        acc[...] = jnp.zeros_like(acc)

    def body(step, carry):
        slot = lax.rem(step, slots)

        @pl.when(step + slots - 1 < steps)
        def _():
            start(step + slots - 1)

        pltpu.make_async_copy(x_buf.at[slot], x_buf.at[slot], x_sem.at[slot]).wait()
        pltpu.make_async_copy(w_buf.at[slot], w_buf.at[slot], w_sem.at[slot]).wait()
        block = x_buf[slot]
        for p in range(3):
            acc[p] += jnp.dot(block, w_buf[slot, p], preferred_element_type=jnp.float32)
        return carry

    lax.fori_loop(0, steps, body, 0)
    if final:
        kept, given = outs
        half = kept.shape[2]
        mine = pl.multiple_of(pair * half, 128)
        other = pl.multiple_of((1 - pair) * half, 128)
        for p in range(3):
            kept[p] = acc[p, :, pl.ds(mine, half)].astype(jnp.bfloat16)
            given[p] = acc[p, :, pl.ds(other, half)].astype(jnp.bfloat16)


def project(place, tokens, own, pieces, per_part, init, final):
    rows = tokens.shape[1]
    some = own if own is not None else pieces[0]
    width = some.shape[2]
    n_own = 0 if own is None else own.shape[1] // DEPTH
    slots = 3
    anywhere = pl.BlockSpec(memory_space=pl.ANY)
    local = pl.BlockSpec(memory_space=pltpu.VMEM)
    operands = [tokens] + ([own] if own is not None else []) + list(pieces)
    in_specs = [anywhere] * len(operands)
    if init is not None:
        operands.append(init)
        in_specs.append(local)
    scratch = [
        pltpu.VMEM((slots, rows, DEPTH), jnp.bfloat16),
        pltpu.VMEM((slots, 3, DEPTH, width), jnp.bfloat16),
        pltpu.SemaphoreType.DMA((slots,)),
        pltpu.SemaphoreType.DMA((slots,)),
    ]
    if final:
        scratch.append(pltpu.VMEM((3, rows, width), jnp.float32))
        out_shape = [jax.ShapeDtypeStruct((3, rows, width // 2), jnp.bfloat16)] * 2
        out_specs = [local, local]
    else:
        out_shape = jax.ShapeDtypeStruct((3, rows, width), jnp.float32)
        out_specs = local
    steps = n_own + len(pieces)
    return pl.pallas_call(
        functools.partial(project_kernel, n_own, len(pieces), per_part, init is not None, final),
        grid_spec=pltpu.PrefetchScalarGridSpec(
            num_scalar_prefetch=1,
            grid=(),
            in_specs=in_specs,
            out_specs=out_specs,
            scratch_shapes=scratch,
        ),
        out_shape=out_shape,
        compiler_params=pltpu.CompilerParams(vmem_limit_bytes=40 * MIB),
        cost_estimate=pl.CostEstimate(
            flops=2 * rows * steps * DEPTH * 3 * width,
            bytes_accessed=steps * DEPTH * (3 * width + rows) * 2,
            transcendentals=0,
        ),
        name="project",
    )(place, *operands)


def scan_kernel(kept, given, decay, gain, skip, state_in, local_ref, state_out, prod):
    poles = decay.shape[0]
    rows = kept.shape[1]
    groups = kept.shape[2] // 128
    for side, ref in enumerate((kept, given)):
        for g in range(groups):
            lanes = slice(g * 128, (g + 1) * 128)
            key = ref[1, :, lanes].astype(jnp.float32)
            value = ref[2, :, lanes].astype(jnp.float32)
            prod[:, side * groups + g, :] = key * value
    direct = skip[...]
    factors = [decay[r] for r in range(poles)]
    gains = [gain[r] for r in range(poles)]

    def step(t, states):
        p = prod[t]
        new = [factors[r] * states[r] + gains[r] * p for r in range(poles)]
        total = list(new)
        while len(total) > 1:
            total = [a + b for a, b in zip(total[::2], total[1::2])]
        local_ref[t] = total[0] + direct * p
        return tuple(new)

    states = lax.fori_loop(0, rows, step, tuple(state_in[r] for r in range(poles)), unroll=8)
    for r in range(poles):
        state_out[r] = states[r]


def scan(kept, given, decay, gain, skip, state):
    rows = kept.shape[1]
    local = pl.BlockSpec(memory_space=pltpu.VMEM)
    lanes = decay.shape[1:]
    return pl.pallas_call(
        scan_kernel,
        in_specs=[local] * 6,
        out_specs=[local] * 2,
        out_shape=[
            jax.ShapeDtypeStruct((rows,) + lanes, jnp.float32),
            jax.ShapeDtypeStruct(decay.shape, jnp.float32),
        ],
        scratch_shapes=[pltpu.VMEM((rows,) + lanes, jnp.float32)],
        compiler_params=pltpu.CompilerParams(vmem_limit_bytes=24 * MIB),
        cost_estimate=pl.CostEstimate(
            flops=64 * rows * lanes[0] * lanes[1],
            bytes_accessed=rows * lanes[0] * lanes[1] * 8,
            transcendentals=0,
        ),
        name="scan",
    )(kept, given, decay, gain, skip, state)


def finish_kernel(n_ctx, n_chunks, seg_len, place, order, *refs):
    refs = list(refs)
    ends = [refs.pop(0) for _ in range(n_ctx)]
    rate = refs.pop(0)
    decay = refs.pop(0)
    locals_ = [refs.pop(0) for _ in range(n_chunks)]
    kept = [refs.pop(0) for _ in range(n_chunks)]
    given = [refs.pop(0) for _ in range(n_chunks)]
    out = refs.pop(0)
    conv = refs.pop(0)
    poles, sublanes, _ = decay.shape
    groups = sublanes // 2
    pair, ctx = place[0], place[1]
    upper = lax.broadcasted_iota(jnp.int32, decay.shape[1:], 0) < groups
    targets = (order[2 * ctx + pair], order[2 * ctx + 1 - pair])
    states = [jnp.zeros(decay.shape[1:], jnp.float32) for _ in range(poles)]
    for mask in range(n_ctx):
        origin = jnp.bitwise_xor(ctx, mask)
        sources = (order[2 * origin + pair], order[2 * origin + 1 - pair])
        for cross in (0, 1):
            gaps = [targets[s] - 1 - sources[s ^ cross] for s in (0, 1)]
            gap = jnp.where(upper, gaps[0], gaps[1])
            span = jnp.maximum(gap, 0).astype(jnp.float32) * seg_len
            for r in range(poles):
                end = ends[mask][r]
                if cross:
                    end = jnp.concatenate([end[groups:], end[:groups]], axis=0)
                factor = jnp.where(gap >= 0, jnp.exp(-rate[r] * span), 0.0)
                states[r] = states[r] + factor * end
    factors = [decay[r] for r in range(poles)]
    states = tuple(states)
    base = 0
    for k in range(n_chunks):
        rows = locals_[k].shape[0]

        def step(t, states):
            new = [factors[r] * states[r] for r in range(poles)]
            total = list(new)
            while len(total) > 1:
                total = [a + b for a, b in zip(total[::2], total[1::2])]
            conv[t] = total[0] + locals_[k][t]
            return tuple(new)

        states = lax.fori_loop(0, rows, step, states, unroll=8)
        for side, ref in enumerate((kept[k], given[k])):
            segment = pair if side == 0 else 1 - pair
            column = pl.multiple_of(segment * seg_len + base, 128)
            for g in range(groups):
                lanes = slice(g * 128, (g + 1) * 128)
                query = ref[0, :, lanes].astype(jnp.float32)
                gated = query * conv[:rows, side * groups + g, :]
                out[lanes, pl.ds(column, rows)] = gated.T.astype(jnp.bfloat16)
        base += rows


def finish(place, order, ends, rate, decay, locals_, kept, given, seg_len):
    n_chunks = len(locals_)
    local = pl.BlockSpec(memory_space=pltpu.VMEM)
    operands = list(ends) + [rate, decay] + list(locals_) + list(kept) + list(given)
    lanes = decay.shape[1:]
    channels = kept[0].shape[2]
    longest = max(k.shape[1] for k in kept)
    return pl.pallas_call(
        functools.partial(finish_kernel, len(ends), n_chunks, seg_len),
        grid_spec=pltpu.PrefetchScalarGridSpec(
            num_scalar_prefetch=2,
            grid=(),
            in_specs=[local] * len(operands),
            out_specs=local,
            scratch_shapes=[pltpu.VMEM((longest,) + lanes, jnp.float32)],
        ),
        out_shape=jax.ShapeDtypeStruct((channels, 2 * seg_len), jnp.bfloat16),
        compiler_params=pltpu.CompilerParams(vmem_limit_bytes=40 * MIB),
        cost_estimate=pl.CostEstimate(
            flops=32 * seg_len * lanes[0] * lanes[1],
            bytes_accessed=seg_len * lanes[0] * lanes[1] * 8,
            transcendentals=0,
        ),
        name="finish",
    )(place, order, *operands)


def per_device(tokens, weight, rate, residue, skip, order):
    seg_len = tokens.shape[0]
    n_ctx = lax.axis_size("ctx")
    seq_len = 2 * n_ctx * seg_len
    pair_index = lax.axis_index("fsdp")
    ctx_index = lax.axis_index("ctx")
    place = jnp.stack([pair_index, ctx_index]).astype(jnp.int32)

    own = weight.transpose(1, 0, 2)
    part = own.shape[1] // n_ctx
    per_part = part // DEPTH
    pieces = {}
    for sub in range(per_part):
        piece = lax.dynamic_slice_in_dim(own, ctx_index * part + sub * DEPTH, DEPTH, 1)
        held = {0: exchanged(piece, "fsdp", 1)}
        bit = n_ctx // 2
        while bit:
            for mask in list(held):
                held[mask | bit] = exchanged(held[mask], "ctx", bit)
            bit //= 2
        for mask in range(n_ctx):
            pieces[mask, sub] = held[mask]
    ordered = [pieces[mask, sub] for mask in range(n_ctx) for sub in range(per_part)]

    channels = rate.shape[0]
    groups = channels // 128

    def spread(values):
        lanes = values.T.reshape(-1, groups, 128)
        return jnp.concatenate([lanes, lanes], axis=1)

    rates = spread(rate)
    decay = jnp.exp(-rates)
    gain = spread(pole_gain(rate, residue, float(seq_len)))
    direct = spread(skip[:, None])[0]

    kept, given, locals_ = [], [], []
    state = jnp.zeros_like(decay)
    base = 0
    for k, rows in enumerate(CHUNKS):
        block = lax.slice_in_dim(tokens, base, base + rows, axis=0)
        base += rows
        whole = lax.all_gather(block, "tp", axis=0, tiled=False)
        if k < 2:
            partial = project(place, whole, own, [], 1, None, False)
            keep, give = project(place, whole, None, ordered, per_part, partial, True)
        else:
            keep, give = project(place, whole, own, ordered, per_part, None, True)
        got = exchanged(give, "fsdp", 1)
        local, state = scan(keep, got, decay, gain, direct, state)
        kept.append(keep)
        given.append(got)
        locals_.append(local)

    ends = [state] + [exchanged(state, "ctx", mask) for mask in range(1, n_ctx)]
    return finish(place, order, ends, rates, decay, locals_, kept, given, seg_len)


def solution(mesh):
    placed = (
        P(("ctx", "fsdp"), "tp"),
        P("fsdp", None, "tp"),
        P(("tp", "fsdp"), None),
        P(("tp", "fsdp"), None),
        P(("tp", "fsdp")),
        P(),
    )
    return jax.shard_map(
        per_device, mesh=mesh, in_specs=placed, out_specs=P(("tp", "fsdp"), "ctx"), check_vma=False
    )
```

time: 1240 us -> 405 us (0.33)
  waiting for transfers between devices: 735 us -> 233 us
  matrix products: 278 us -> 0 us
  local copies, waits for them, and re-layouts: 172 us -> 21.6 us
  Pallas kernels: 0 us -> 117 us
  other arithmetic: 28.8 us -> 0.16 us
  starting transfers between devices: 1.57 us -> 16.2 us
    dot_general x6 -> x0, matrix products: 278 us -> none  [the longest x1 70.5 us: per_device(): jnp.einsum('dkc,td->ckt', weight, both_rows, preferred_element_type=jnp.f...]
    reduce_scatter x1 -> x0, waiting for transfers between devices: 267 us -> none  [per_device(): lax.psum_scatter(jnp.einsum('dkc,td->ckt', weight, both_rows, preferred_e...]
    all_gather x1 -> x4, waiting for transfers between devices: 287 us -> 27.3 us  [per_device(): whole = lax.all_gather(block, 'tp', axis=0, tiled=False)]
    pallas_call x0 -> x11, Pallas kernels: none -> 117 us  [the longest x6 89.5 us: project(): pl.pallas_call(functools.partial(project_kernel, n_own, len(pieces), per_...]
    gather x2 -> x0, local copies, waits for them, and re-layouts: 100 us -> none  [per_device(): jnp.take(lag_filter, jnp.maximum(offsets, 0), axis=1)]
    select_n x1 -> x0, local copies, waits for them, and re-layouts: 25.6 us -> none  [per_device(): jnp.where(block_mask[None, None], jnp.exp(-rate[:, :, None, None] * (bloc...]
    ppermute x1 -> x15, waiting for transfers between devices: 181 us -> 204 us  [exchanged(): return lax.ppermute(block, axis, [(i, i ^ mask) for i in range(count)])]
    dot_general x3 -> x0, local copies, waits for them, and re-layouts: 16.4 us -> none  [the longest x1 10.9 us: per_device(): jnp.einsum('crj,cmbj->crmb', tail, prod_blocks, precision=highest)]
  transfers between devices with their start and end apart: 4 -> 19, of which waited for: 3 -> 7; matrix products, arithmetic and copies ran while one was open for 11% -> 1% of each run, Pallas kernels for 0% -> 26%
where the time goes in v1:
time: 405 us; the launch traced here: 401 us
  waiting for transfers between devices  233 us (58%)
  Pallas kernels  117 us (29%)
  local copies, waits for them, and re-layouts  21.6 us (5%)
  starting transfers between devices  16.2 us (4%)
  between operations  13.4 us (3%)
    ppermute x15, waiting for transfers between devices, exchanged(): return lax.ppermute(block, axis, [(i, i ^ mask) for i in range(count)])  204 us
    pallas_call x6, Pallas kernels, project(): pl.pallas_call(functools.partial(project_kernel, n_own, len(pieces), per_...  89.5 us
    all_gather x4, waiting for transfers between devices, per_device(): whole = lax.all_gather(block, 'tp', axis=0, tiled=False)  27.3 us
    ppermute x15, starting transfers between devices, exchanged(): return lax.ppermute(block, axis, [(i, i ^ mask) for i in range(count)])  16.1 us
    pallas_call x4, Pallas kernels, scan(): pl.pallas_call(scan_kernel, in_specs=[local] * 6, out_specs=[local] * 2,...  15.9 us
    unnamed x36, local copies, waits for them, and re-layouts  13.6 us
    pallas_call x1, Pallas kernels, finish(): pl.pallas_call(functools.partial(finish_kernel, len(ends), n_chunks, seg_...  11.5 us
  transfers between devices with their start and end apart: 19, of which 7 were waited for; matrix products, arithmetic and copies ran while one was open for 1% of the time, Pallas kernels for 26%

profile of v1, /device:TPU:9, one launch (start us, length us, event | category | flops | bytes accessed | tf_op | source)
XLA Modules:
  0.0 401.2 jit_solution(14138843586953535095)
XLA Ops:
  6.5 4.4 %fusion = (bf16[256,2048]{1,0:T(8,128)(2,1)}, bf16[256,2048]{1,0:T(8,128)(2,1)}, bf16[256,2048]{1,0:T(8,128)(2,1)}, bf16[256,2048]{1,0:T(8,128)(2,1)}) fusion(bf16[1024,2048]{1,0:T(8,128)(2,1)} %param.6), kind=kLoop, calls=%fused_computation.8 | loop fusion | bytes 8388608 | tf_op jit(solution)/shard_map/slice | solution.py:317
  11.0 0.7 all-gather.15.cloned.1.call-update
  11.8 0.7 all-gather.11.cloned.1.call-update
  12.5 3.6 dynamic-slice_bitcast_fusion
  16.1 1.3 collective-permute-start
  17.4 0.2 collective-permute-start.1
  17.6 67.5 %collective-permute-done.refs_2_.refs_1_ = bf16[3,512,1024]{2,1,0:T(8,128)(2,1)S(1)} collective-permute-done((bf16[3,512,1024]{2,1,0:T(8,128)(2,1)S(1)}, bf16[3,512,1024]{2,1,0:T(8,128)(2,1)S(1)}, u32[]{:S(2)}, u32[]{:S(2)}) %collective-permute-start) | collective-permute-done | bytes 3145760 | tf_op jit(solution)/shard_map/ppermute | solution.py:17
  85.1 1.3 collective-permute-start.4
  86.4 66.2 %collective-permute-done.1.refs_3_.refs_2_ = bf16[3,512,1024]{2,1,0:T(8,128)(2,1)} collective-permute-done((bf16[3,512,1024]{2,1,0:T(8,128)(2,1)S(1)}, bf16[3,512,1024]{2,1,0:T(8,128)(2,1)}, u32[]{:S(2)}, u32[]{:S(2)}) %collective-permute-start.1) | collective-permute-done | bytes 3145760 | tf_op jit(solution)/shard_map/ppermute | solution.py:17
  152.6 1.2 collective-permute-start.5
  153.9 1.9 collective-permute-start.2
  155.8 0.1 collective-permute-start.3
  155.8 0.4 collective-permute-start.6
  156.3 64.7 %collective-permute-done.5.refs_7_.refs_6_ = bf16[3,512,1024]{2,1,0:T(8,128)(2,1)} collective-permute-done((bf16[3,512,1024]{2,1,0:T(8,128)(2,1)}, bf16[3,512,1024]{2,1,0:T(8,128)(2,1)}, u32[]{:S(2)}, u32[]{:S(2)}) %collective-permute-start.5) | collective-permute-done | bytes 3145760 | tf_op jit(solution)/shard_map/ppermute | solution.py:17
  221.0 2.5 collective-permute-start.7
  223.5 0.1 pad_add_fusion.place
  223.5 2.2 copy-done
  225.8 10.8 %project.8.refs_9_ = f32[3,256,1024]{2,1,0:T(8,128)S(1)} custom-call(s32[2]{0:T(128)S(1)} %pad_add_fusion.place, bf16[4,256,2048]{2,1,0:T(8,128)(2,1)S(1)} %bitcast.18, bf16[3,4096,1024]{2,1,0:T(8,128)(2,1)} %bitcast.21), custom_call_target="tpu_custom_call" | custom-call | flops 6442450944 | bytes 27262976 | tf_op jit(solution)/shard_map/project/pallas_call | solution.py:124
  236.6 1.6 copy-done.3
  238.2 2.2 copy-done.1
  240.4 10.7 %project.10.refs_9_ = f32[3,256,1024]{2,1,0:T(8,128)S(1)} custom-call(s32[2]{0:T(128)S(1)} %pad_add_fusion.place, bf16[4,256,2048]{2,1,0:T(8,128)(2,1)S(1)} %bitcast.20, bf16[3,4096,1024]{2,1,0:T(8,128)(2,1)} %bitcast.22), custom_call_target="tpu_custom_call" | custom-call | flops 6442450944 | bytes 27262976 | tf_op jit(solution)/shard_map/project/pallas_call | solution.py:124
  251.2 1.7 copy-done.2
  252.9 21.1 %project.7 = (bf16[3,256,512]{2,1,0:T(8,128)(2,1)S(1)}, bf16[3,256,512]{2,1,0:T(8,128)(2,1)}) custom-call(s32[2]{0:T(128)S(1)} %pad_add_fusion.place, bf16[4,256,2048]{2,1,0:T(8,128)(2,1)} %bitcast.25, bf16[3,4096,1024]{2,1,0:T(8,128)(2,1)} %bitcast.23, bf16[3,512,1024]{2,1,0:T(8,128)(2,1)S(1)} %collective-permute-done.refs_2_.refs_1_, ...), custom_call_target="tpu_custom_call" | custom-call | flops 12884901888 | bytes 54525952 | tf_op jit(solution)/shard_map/project/pallas_call | solution.py:124
  274.0 0.9 copy-done.4
  274.9 1.2 collective-permute-start.9
  276.1 13.2 %project.9 = (bf16[3,256,512]{2,1,0:T(8,128)(2,1)S(1)}, bf16[3,256,512]{2,1,0:T(8,128)(2,1)}) custom-call(s32[2]{0:T(128)S(1)} %pad_add_fusion.place, bf16[4,256,2048]{2,1,0:T(8,128)(2,1)} %bitcast.17, bf16[3,512,1024]{2,1,0:T(8,128)(2,1)S(1)} %collective-permute-done.refs_2_.refs_1_, bf16[3,512,1024]{2,1,0:T(8,128)(2,1)} %collective-permute-done.1.refs_3_.refs_2_, ...), custom_call_target="tpu_custom_call" | custom-call | flops 6442450944 | bytes 27262976 | tf_op jit(solution)/shard_map/project/pallas_call | solution.py:124
  289.3 0.9 copy-done.6
  290.2 0.2 collective-permute-start.10
  290.4 13.2 %project.11 = (bf16[3,256,512]{2,1,0:T(8,128)(2,1)S(1)}, bf16[3,256,512]{2,1,0:T(8,128)(2,1)}) custom-call(s32[2]{0:T(128)S(1)} %pad_add_fusion.place, bf16[4,256,2048]{2,1,0:T(8,128)(2,1)} %bitcast.19, bf16[3,512,1024]{2,1,0:T(8,128)(2,1)S(1)} %collective-permute-done.refs_2_.refs_1_, bf16[3,512,1024]{2,1,0:T(8,128)(2,1)} %collective-permute-done.1.refs_3_.refs_2_, ...), custom_call_target="tpu_custom_call" | custom-call | flops 6442450944 | bytes 27262976 | tf_op jit(solution)/shard_map/project/pallas_call | solution.py:124
  303.7 0.9 copy-done.9
  304.5 1.2 collective-permute-start.11
  305.8 27.3 %all-gather.9.cloned.1.call-done = bf16[1024,2048]{1,0:T(8,128)(2,1)} async-done(((bf16[256,2048]{1,0:T(8,128)(2,1)}), bf16[1024,2048]{1,0:T(8,128)(2,1)}) %all-gather.9.cloned.1.call-update) | async-done | bytes 4194320 | tf_op jit(solution)/shard_map/all_gather | solution.py:319
  333.1 20.5 %project.6 = (bf16[3,256,512]{2,1,0:T(8,128)(2,1)S(1)}, bf16[3,256,512]{2,1,0:T(8,128)(2,1)}) custom-call(s32[2]{0:T(128)S(1)} %pad_add_fusion.place, bf16[4,256,2048]{2,1,0:T(8,128)(2,1)} %bitcast.26, bf16[3,4096,1024]{2,1,0:T(8,128)(2,1)} %bitcast.24, bf16[3,512,1024]{2,1,0:T(8,128)(2,1)S(1)} %collective-permute-done.refs_2_.refs_1_, ...), custom_call_target="tpu_custom_call" | custom-call | flops 12884901888 | bytes 54525952 | tf_op jit(solution)/shard_map/project/pallas_call | solution.py:124
  353.6 0.9 copy-done.12
  354.6 1.3 collective-permute-start.8
  356.0 1.1 copy-done.10
  357.2 4.3 %scan.4 = (f32[256,8,128]{2,1,0:T(8,128)S(1)}, f32[16,8,128]{2,1,0:T(8,128)S(1)}) custom-call(bf16[3,256,512]{2,1,0:T(8,128)(2,1)S(1)} %copy-done.10, bf16[3,256,512]{2,1,0:T(8,128)(2,1)} %collective-permute-done.11.given.refs_14_, f32[16,8,128]{2,1,0:T(8,128)S(1)} %get-tuple-element.44.decay.refs_5_, f32[16,8,128]{2,1,0:T(8,128)S(1)} %pad_maximum_fusion.1.gain, ...), custom_call_target="tpu_custom_call" | custom-call | flops 16777216 | bytes 2097152 | tf_op jit(solution)/shard_map/scan/pallas_call | solution.py:176
  361.5 1.1 copy-done.7
  362.6 4.3 %scan.5 = (f32[256,8,128]{2,1,0:T(8,128)S(1)}, f32[16,8,128]{2,1,0:T(8,128)S(1)}) custom-call(bf16[3,256,512]{2,1,0:T(8,128)(2,1)S(1)} %copy-done.7, bf16[3,256,512]{2,1,0:T(8,128)(2,1)} %collective-permute-done.10.given.refs_15_, f32[16,8,128]{2,1,0:T(8,128)S(1)} %get-tuple-element.44.decay.refs_5_, f32[16,8,128]{2,1,0:T(8,128)S(1)} %pad_maximum_fusion.1.gain, ...), custom_call_target="tpu_custom_call" | custom-call | flops 16777216 | bytes 2097152 | tf_op jit(solution)/shard_map/scan/pallas_call | solution.py:176
  367.0 4.2 %scan.6 = (f32[256,8,128]{2,1,0:T(8,128)S(1)}, f32[16,8,128]{2,1,0:T(8,128)S(1)}) custom-call(bf16[3,256,512]{2,1,0:T(8,128)(2,1)S(1)} %copy-done.5, bf16[3,256,512]{2,1,0:T(8,128)(2,1)} %collective-permute-done.9.given.refs_16_, f32[16,8,128]{2,1,0:T(8,128)S(1)} %get-tuple-element.44.decay.refs_5_, f32[16,8,128]{2,1,0:T(8,128)S(1)} %pad_maximum_fusion.1.gain, ...), custom_call_target="tpu_custom_call" | custom-call | flops 16777216 | bytes 2097152 | tf_op jit(solution)/shard_map/scan/pallas_call | solution.py:176
  371.2 2.1 collective-permute-done.8.given.refs_17_
  373.3 3.1 scan.7
  376.4 1.5 collective-permute-start.12
  377.9 1.3 collective-permute-start.13
  379.1 0.4 collective-permute-start.14
  379.6 2.0 collective-permute-done.13.refs_2_
  381.5 1.7 collective-permute-done.14.refs_3_
  383.2 11.5 %finish.1 = bf16[512,2048]{1,0:T(8,128)(2,1)} custom-call(s32[2]{0:T(128)S(1)} %pad_add_fusion.place, s32[8]{0:T(128)S(1)} %copy-done.14, f32[16,8,128]{2,1,0:T(8,128)S(1)} %get-tuple-element.32.refs_0_, f32[16,8,128]{2,1,0:T(8,128)S(1)} %collective-permute-done.12.refs_1_, f32[16,8,128]{2,1,0:T(8,128)S(1)} %collective-permute-done.13.refs_2_, ...), custom_call_target="tpu_custom_call" | custom-call | flops 33554432 | bytes 8388608 | tf_op jit(solution)/shard_map/finish/pallas_call | solution.py:257
  (51 shorter events, 0.4 us)
Async XLA Ops:
  6.5 217.0 %all-gather.13.cloned.1.call-start = ((), (), s32[]{:S(2)}) async-start(), calls=%async_computation.2 | async-start | bytes 5242880 | tf_op jit(solution)/shard_map/all_gather | solution.py:319
  11.0 227.2 %all-gather.15.cloned.1.call-start = ((), (), s32[]{:S(2)}) async-start(), calls=%async_computation.3 | async-start | bytes 5242880 | tf_op jit(solution)/shard_map/all_gather | solution.py:319
  11.7 241.1 %all-gather.11.cloned.1.call-start = ((), (), s32[]{:S(2)}) async-start(), calls=%async_computation.1 | async-start | bytes 5242880 | tf_op jit(solution)/shard_map/all_gather | solution.py:319
  12.5 320.6 %all-gather.9.cloned.1.call-start = ((), (), s32[]{:S(2)}) async-start(), calls=%async_computation | async-start | bytes 5242880 | tf_op jit(solution)/shard_map/all_gather | solution.py:319
  16.1 69.0 %collective-permute-start = (bf16[3,512,1024]{2,1,0:T(8,128)(2,1)S(1)}, bf16[3,512,1024]{2,1,0:T(8,128)(2,1)S(1)}, u32[]{:S(2)}, u32[]{:S(2)}) collective-permute-start(bf16[3,512,1024]{2,1,0:T(8,128)(2,1)S(1)} %get-tuple-element.38), channel_id=1, source_target_pairs={{0,1},{1,0},{2,3},{3,2},{4,5},{5,4},{6,7},{7,6},{8,9},{9,8},{10,11... | collective-permute-start | bytes 9437192 | tf_op jit(solution)/shard_map/ppermute | solution.py:17
  17.4 135.2 %collective-permute-start.1 = (bf16[3,512,1024]{2,1,0:T(8,128)(2,1)S(1)}, bf16[3,512,1024]{2,1,0:T(8,128)(2,1)}, u32[]{:S(2)}, u32[]{:S(2)}) collective-permute-start(bf16[3,512,1024]{2,1,0:T(8,128)(2,1)S(1)} %get-tuple-element.37), channel_id=1, source_target_pairs={{0,1},{1,0},{2,3},{3,2},{4,5},{5,4},{6,7},{7,6},{8,9},{9,8},{10,11... | collective-permute-start | bytes 9437192 | tf_op jit(solution)/shard_map/ppermute | solution.py:17
  85.1 70.7 %collective-permute-start.4 = (bf16[3,512,1024]{2,1,0:T(8,128)(2,1)S(1)}, bf16[3,512,1024]{2,1,0:T(8,128)(2,1)}, u32[]{:S(2)}, u32[]{:S(2)}) collective-permute-start(bf16[3,512,1024]{2,1,0:T(8,128)(2,1)S(1)} %collective-permute-done.refs_2_.refs_1_), channel_id=1, source_target_pairs={{0,16},{8,24},{16,0},{24,8},{1,17},{9,25},{17,1},{25,9},{2,18},{10... | collective-permute-start | bytes 9437192 | tf_op jit(solution)/shard_map/ppermute | solution.py:17
  152.6 68.4 %collective-permute-start.5 = (bf16[3,512,1024]{2,1,0:T(8,128)(2,1)}, bf16[3,512,1024]{2,1,0:T(8,128)(2,1)}, u32[]{:S(2)}, u32[]{:S(2)}) collective-permute-start(bf16[3,512,1024]{2,1,0:T(8,128)(2,1)} %collective-permute-done.1.refs_3_.refs_2_), channel_id=1, source_target_pairs={{0,16},{8,24},{16,0},{24,8},{1,17},{9,25},{17,1},{25,9},{2,18},{10... | collective-permute-start | bytes 9437192 | tf_op jit(solution)/shard_map/ppermute | solution.py:17
  153.9 99.0 %collective-permute-start.2 = (bf16[3,512,1024]{2,1,0:T(8,128)(2,1)S(1)}, bf16[3,512,1024]{2,1,0:T(8,128)(2,1)}, u32[]{:S(2)}, u32[]{:S(2)}) collective-permute-start(bf16[3,512,1024]{2,1,0:T(8,128)(2,1)S(1)} %collective-permute-done.refs_2_.refs_1_), channel_id=1, source_target_pairs={{0,8},{8,0},{16,24},{24,16},{1,9},{9,1},{17,25},{25,17},{2,10},{10... | collective-permute-start | bytes 9437192 | tf_op jit(solution)/shard_map/ppermute | solution.py:17
  155.8 97.1 %collective-permute-start.3 = (bf16[3,512,1024]{2,1,0:T(8,128)(2,1)}, bf16[3,512,1024]{2,1,0:T(8,128)(2,1)}, u32[]{:S(2)}, u32[]{:S(2)}) collective-permute-start(bf16[3,512,1024]{2,1,0:T(8,128)(2,1)} %collective-permute-done.1.refs_3_.refs_2_), channel_id=1, source_target_pairs={{0,8},{8,0},{16,24},{24,16},{1,9},{9,1},{17,25},{25,17},{2,10},{10... | collective-permute-start | bytes 9437192 | tf_op jit(solution)/shard_map/ppermute | solution.py:17
  155.8 97.0 %collective-permute-start.6 = (bf16[3,512,1024]{2,1,0:T(8,128)(2,1)}, bf16[3,512,1024]{2,1,0:T(8,128)(2,1)}, u32[]{:S(2)}, u32[]{:S(2)}) collective-permute-start(bf16[3,512,1024]{2,1,0:T(8,128)(2,1)} %collective-permute-done.4.refs_6_.refs_5_), channel_id=1, source_target_pairs={{0,8},{8,0},{16,24},{24,16},{1,9},{9,1},{17,25},{25,17},{2,10},{10... | collective-permute-start | bytes 9437192 | tf_op jit(solution)/shard_map/ppermute | solution.py:17
  221.0 31.9 %collective-permute-start.7 = (bf16[3,512,1024]{2,1,0:T(8,128)(2,1)}, bf16[3,512,1024]{2,1,0:T(8,128)(2,1)}, u32[]{:S(2)}, u32[]{:S(2)}) collective-permute-start(bf16[3,512,1024]{2,1,0:T(8,128)(2,1)} %collective-permute-done.5.refs_7_.refs_6_), channel_id=1, source_target_pairs={{0,8},{8,0},{16,24},{24,16},{1,9},{9,1},{17,25},{25,17},{2,10},{10... | collective-permute-start | bytes 9437192 | tf_op jit(solution)/shard_map/ppermute | solution.py:17
  223.5 2.2 copy-start
  236.6 1.6 copy-start.3
  238.2 2.2 copy-start.1
  251.2 1.7 copy-start.2
  273.9 0.9 copy-start.4
  274.9 92.1 %collective-permute-start.9 = (bf16[3,256,512]{2,1,0:T(8,128)(2,1)}, bf16[3,256,512]{2,1,0:T(8,128)(2,1)}, u32[]{:S(2)}, u32[]{:S(2)}) collective-permute-start(bf16[3,256,512]{2,1,0:T(8,128)(2,1)} %get-tuple-element.24), channel_id=1, source_target_pairs={{0,1},{1,0},{2,3},{3,2},{4,5},{5,4},{6,7},{7,6},{8,9},{9,8},{10,11... | collective-permute-start | bytes 2359304 | tf_op jit(solution)/shard_map/ppermute | solution.py:17
  289.3 0.9 copy-start.6
  290.2 71.3 %collective-permute-start.10 = (bf16[3,256,512]{2,1,0:T(8,128)(2,1)}, bf16[3,256,512]{2,1,0:T(8,128)(2,1)}, u32[]{:S(2)}, u32[]{:S(2)}) collective-permute-start(bf16[3,256,512]{2,1,0:T(8,128)(2,1)} %get-tuple-element.26), channel_id=1, source_target_pairs={{0,1},{1,0},{2,3},{3,2},{4,5},{5,4},{6,7},{7,6},{8,9},{9,8},{10,11... | collective-permute-start | bytes 2359304 | tf_op jit(solution)/shard_map/ppermute | solution.py:17
  303.6 0.9 copy-start.9
  304.5 51.5 %collective-permute-start.11 = (bf16[3,256,512]{2,1,0:T(8,128)(2,1)}, bf16[3,256,512]{2,1,0:T(8,128)(2,1)}, u32[]{:S(2)}, u32[]{:S(2)}) collective-permute-start(bf16[3,256,512]{2,1,0:T(8,128)(2,1)} %get-tuple-element.28), channel_id=1, source_target_pairs={{0,1},{1,0},{2,3},{3,2},{4,5},{5,4},{6,7},{7,6},{8,9},{9,8},{10,11... | collective-permute-start | bytes 2359304 | tf_op jit(solution)/shard_map/ppermute | solution.py:17
  333.1 22.8 %copy-start.15 = (f32[512,16]{0,1:T(8,128)S(1)}, f32[512,16]{0,1:T(8,128)}, u32[]{:S(2)}) copy-start(f32[512,16]{0,1:T(8,128)} %param.8) | copy-start | bytes 98308
  333.1 22.8 %copy-start.16 = (f32[512,16]{0,1:T(8,128)S(1)}, f32[512,16]{0,1:T(8,128)}, u32[]{:S(2)}) copy-start(f32[512,16]{0,1:T(8,128)} %param.9) | copy-start | bytes 98308
  333.1 22.8 %copy-start.17 = (f32[512]{0:T(512)S(1)}, f32[512]{0:T(512)}, u32[]{:S(2)}) copy-start(f32[512]{0:T(512)} %param.10) | copy-start | bytes 6148
  353.6 0.9 copy-start.12
  354.5 12.4 %copy-start.5 = (bf16[3,256,512]{2,1,0:T(8,128)(2,1)S(1)}, bf16[3,256,512]{2,1,0:T(8,128)(2,1)}, u32[]{:S(2)}) copy-start(bf16[3,256,512]{2,1,0:T(8,128)(2,1)} %copy-done.4) | copy-start | bytes 2359300
  354.6 18.8 %collective-permute-start.8 = (bf16[3,256,512]{2,1,0:T(8,128)(2,1)}, bf16[3,256,512]{2,1,0:T(8,128)(2,1)S(1)}, u32[]{:S(2)}, u32[]{:S(2)}) collective-permute-start(bf16[3,256,512]{2,1,0:T(8,128)(2,1)} %get-tuple-element.22), channel_id=1, source_target_pairs={{0,1},{1,0},{2,3},{3,2},{4,5},{5,4},{6,7},{7,6},{8,9},{9,8},{10,11... | collective-permute-start | bytes 2359304 | tf_op jit(solution)/shard_map/ppermute | solution.py:17
  356.0 1.1 copy-start.10
  357.2 26.0 %copy-start.8 = (bf16[3,256,512]{2,1,0:T(8,128)(2,1)S(1)}, bf16[3,256,512]{2,1,0:T(8,128)(2,1)}, u32[]{:S(2)}) copy-start(bf16[3,256,512]{2,1,0:T(8,128)(2,1)} %copy-done.6) | copy-start | bytes 2359300
  357.2 26.0 %copy-start.14 = (s32[8]{0:T(128)S(1)}, s32[8]{0:T(128)}, u32[]{:S(2)}) copy-start(s32[8]{0:T(128)} %order.1) | copy-start | bytes 100
  361.5 1.1 copy-start.7
  362.6 10.7 %copy-start.13 = (bf16[3,256,512]{2,1,0:T(8,128)(2,1)S(1)}, bf16[3,256,512]{2,1,0:T(8,128)(2,1)}, u32[]{:S(2)}) copy-start(bf16[3,256,512]{2,1,0:T(8,128)(2,1)} %copy-done.12) | copy-start | bytes 2359300
  362.6 20.6 %copy-start.11 = (bf16[3,256,512]{2,1,0:T(8,128)(2,1)S(1)}, bf16[3,256,512]{2,1,0:T(8,128)(2,1)}, u32[]{:S(2)}) copy-start(bf16[3,256,512]{2,1,0:T(8,128)(2,1)} %copy-done.9) | copy-start | bytes 2359300
  376.4 3.2 collective-permute-start.12
  377.9 3.7 collective-permute-start.13
  379.1 4.0 %collective-permute-start.14 = (f32[16,8,128]{2,1,0:T(8,128)S(1)}, f32[16,8,128]{2,1,0:T(8,128)S(1)}, u32[]{:S(2)}, u32[]{:S(2)}) collective-permute-start(f32[16,8,128]{2,1,0:T(8,128)S(1)} %get-tuple-element.32.refs_0_), channel_id=1, source_target_pairs={{0,24},{8,16},{16,8},{24,0},{1,25},{9,17},{17,9},{25,1},{2,26},{10... | collective-permute-start | bytes 196616 | tf_op jit(solution)/shard_map/ppermute | solution.py:17
Sparse Core Ops, SparseCore 0:
  11.1 79.3 all-gather.12
  92.1 79.2 all-gather.14
  173.0 79.2 all-gather.10
  253.7 79.2 all-gather.8

commit v2 on v1

--- a/solution.py
+++ b/solution.py
@@ -1,4 +1,5 @@
 import functools
+from typing import NamedTuple
 
 import jax
 import jax.numpy as jnp
@@ -9,7 +10,15 @@
 
 MIB = 1 << 20
 DEPTH = 512
-CHUNKS = (256, 256, 256, 256)
+CHUNKS = (256, 256, 256, 128, 128)
+HALVES = (1024,)
+FAR = (1024,)
+
+
+class Plan(NamedTuple):
+    half_blocks: int
+    part_blocks: int
+    n_pieces: int
 
 
 def exchanged(block, axis, mask):
@@ -17,52 +26,52 @@
     return lax.ppermute(block, axis, [(i, i ^ mask) for i in range(count)])
 
 
+def after(value, *others):
+    return lax.optimization_barrier((value, *others))[0]
+
+
 def pole_gain(rate, residue, length):
     return residue * jnp.sqrt(jnp.maximum(-jnp.expm1(-2.0 * rate), 1.0 / length))
 
 
-def project_kernel(n_own, n_pieces, per_part, has_init, final, place, *refs):
+def project_kernel(plan, n_inputs, has_init, final, blocks, x_plan, place, *refs):
     refs = list(refs)
-    tokens = refs.pop(0)
-    own = refs.pop(0) if n_own else None
-    pieces = [refs.pop(0) for _ in range(n_pieces)]
+    inputs = [refs.pop(0) for _ in range(n_inputs)]
+    own = refs.pop(0)
+    pieces = [refs.pop(0) for _ in range(plan.n_pieces)]
     init = refs.pop(0) if has_init else None
     outs = [refs.pop(0) for _ in range(2 if final else 1)]
     x_buf, w_buf, x_sem, w_sem = refs[:4]
     acc = refs[4] if final else outs[0]
-    rows = x_buf.shape[1]
-    per_quarter = tokens.shape[2] // DEPTH
-    pair, ctx = place[0], place[1]
-    n_half = tokens.shape[0] * per_quarter // 2
-    steps = n_own + n_pieces
+    pair, ctx, tp = place[0], place[1], place[2]
     slots = x_buf.shape[0]
 
     def start(step):
         slot = lax.rem(step, slots)
-        rest = step - n_own
-        part = jnp.bitwise_xor(ctx, lax.div(rest, per_part))
-        theirs = (1 - pair) * n_half + part * per_part + lax.rem(rest, per_part)
-        block = jnp.where(step < n_own, pair * n_half + step, theirs)
-        quarter = lax.div(block, per_quarter)
-        column = pl.multiple_of(lax.rem(block, per_quarter) * DEPTH, DEPTH)
-        pltpu.make_async_copy(
-            tokens.at[quarter, :, pl.ds(column, DEPTH)], x_buf.at[slot], x_sem.at[slot]
-        ).start()
-
-        if n_own:
-            @pl.when(step < n_own)
+        block = x_plan(tp, step, inputs, x_buf.at[slot], x_sem.at[slot])
+        local = lax.rem(block, plan.half_blocks)
+        here = lax.div(block, plan.half_blocks) == pair
+
+        @pl.when(here)
+        def _():
+            row = pl.multiple_of(local * DEPTH, DEPTH)
+            pltpu.make_async_copy(
+                own.at[:, pl.ds(row, DEPTH), :], w_buf.at[slot], w_sem.at[slot]
+            ).start()
+
+        part = lax.div(local, plan.part_blocks)
+        number = jnp.bitwise_xor(part, ctx) * plan.part_blocks + lax.rem(local, plan.part_blocks)
+        for n in range(len(pieces) // 2):
+            @pl.when(jnp.logical_not(here) & (number == n))
             def _():
-                row = pl.multiple_of(step * DEPTH, DEPTH)
-                pltpu.make_async_copy(
-                    own.at[:, pl.ds(row, DEPTH), :], w_buf.at[slot], w_sem.at[slot]
-                ).start()
-
-        for n, piece in enumerate(pieces):
-            @pl.when(rest == n)
-            def _():
-                pltpu.make_async_copy(piece, w_buf.at[slot], w_sem.at[slot]).start()
-
-    for ahead in range(slots - 1):
+                for side in (0, 1):
+                    pltpu.make_async_copy(
+                        pieces[2 * n + side],
+                        w_buf.at[slot, :, pl.ds(side * (DEPTH // 2), DEPTH // 2), :],
+                        w_sem.at[slot],
+                    ).start()
+
+    for ahead in range(min(slots - 1, blocks)):
         start(jnp.int32(ahead))
     if has_init:
         acc[...] = init[...]
@@ -72,7 +81,7 @@
     def body(step, carry):
         slot = lax.rem(step, slots)
 
-        @pl.when(step + slots - 1 < steps)
+        @pl.when(step + slots - 1 < blocks)
         def _():
             start(step + slots - 1)
 
@@ -83,7 +92,7 @@
             acc[p] += jnp.dot(block, w_buf[slot, p], preferred_element_type=jnp.float32)
         return carry
 
-    lax.fori_loop(0, steps, body, 0)
+    lax.fori_loop(0, blocks, body, 0)
     if final:
         kept, given = outs
         half = kept.shape[2]
@@ -94,19 +103,16 @@
             given[p] = acc[p, :, pl.ds(other, half)].astype(jnp.bfloat16)
 
 
-def project(place, tokens, own, pieces, per_part, init, final):
-    rows = tokens.shape[1]
-    some = own if own is not None else pieces[0]
-    width = some.shape[2]
-    n_own = 0 if own is None else own.shape[1] // DEPTH
+def project(plan, place, inputs, own, pieces, init, base, rows, blocks, x_plan, final):
+    width = own.shape[2]
     slots = 3
     anywhere = pl.BlockSpec(memory_space=pl.ANY)
     local = pl.BlockSpec(memory_space=pltpu.VMEM)
-    operands = [tokens] + ([own] if own is not None else []) + list(pieces)
+    operands = list(inputs) + [own] + list(pieces)
     in_specs = [anywhere] * len(operands)
     if init is not None:
         operands.append(init)
-        in_specs.append(local)
+        in_specs.append(pl.BlockSpec((3, rows, width), lambda i, place: (0, base // rows, 0)))
     scratch = [
         pltpu.VMEM((slots, rows, DEPTH), jnp.bfloat16),
         pltpu.VMEM((slots, 3, DEPTH, width), jnp.bfloat16),
@@ -120,25 +126,99 @@
     else:
         out_shape = jax.ShapeDtypeStruct((3, rows, width), jnp.float32)
         out_specs = local
-    steps = n_own + len(pieces)
     return pl.pallas_call(
-        functools.partial(project_kernel, n_own, len(pieces), per_part, init is not None, final),
+        functools.partial(
+            project_kernel, plan, len(inputs), init is not None, final, blocks, x_plan
+        ),
         grid_spec=pltpu.PrefetchScalarGridSpec(
             num_scalar_prefetch=1,
-            grid=(),
+            grid=(1,),
             in_specs=in_specs,
             out_specs=out_specs,
             scratch_shapes=scratch,
         ),
         out_shape=out_shape,
-        compiler_params=pltpu.CompilerParams(vmem_limit_bytes=40 * MIB),
+        compiler_params=pltpu.CompilerParams(vmem_limit_bytes=44 * MIB),
         cost_estimate=pl.CostEstimate(
-            flops=2 * rows * steps * DEPTH * 3 * width,
-            bytes_accessed=steps * DEPTH * (3 * width + rows) * 2,
+            flops=0,
+            bytes_accessed=0,
             transcendentals=0,
         ),
         name="project",
     )(place, *operands)
+
+
+def columns(quarter_block):
+    return pl.ds(pl.multiple_of(quarter_block * DEPTH, DEPTH), DEPTH)
+
+
+def gathered_plan(per_quarter):
+    def plan(tp, step, inputs, target, sem):
+        source = inputs[0].at[lax.div(step, per_quarter), :, columns(lax.rem(step, per_quarter))]
+        pltpu.make_async_copy(source, target, sem).start()
+        return step
+
+    return plan
+
+
+def line_ends(tp):
+    return (tp == 0) | (tp == 3)
+
+
+def first_plan(per_quarter, n_halves):
+    def plan(tp, step, inputs, target, sem):
+        own, near, *rest = inputs
+        middle, ends = rest[:n_halves], rest[n_halves:]
+        high = lax.div(tp, 2)
+        early = step < 2 * per_quarter
+        block = jnp.where(
+            early,
+            high * 2 * per_quarter + step,
+            (2 - high) * per_quarter + step - 2 * per_quarter,
+        )
+        quarter = lax.div(block, per_quarter)
+        where = columns(lax.rem(block, per_quarter))
+
+        @pl.when(early & (quarter == tp))
+        def _():
+            pltpu.make_async_copy(own.at[:, where], target, sem).start()
+
+        @pl.when(early & (quarter != tp))
+        def _():
+            pltpu.make_async_copy(near.at[:, where], target, sem).start()
+
+        for at_end, sources in ((False, middle), (True, ends)):
+            @pl.when(jnp.logical_not(early) & (line_ends(tp) == at_end))
+            def _():
+                row = 0
+                for source in sources:
+                    size = source.shape[0]
+                    pltpu.make_async_copy(
+                        source.at[:, where], target.at[pl.ds(row, size), :], sem
+                    ).start()
+                    row += size
+
+        return block
+
+    return plan
+
+
+def last_plan(per_quarter, row, rows):
+    def plan(tp, step, inputs, target, sem):
+        middle, ends = inputs
+        where = columns(step)
+
+        @pl.when(line_ends(tp))
+        def _():
+            pltpu.make_async_copy(ends.at[:, where], target, sem).start()
+
+        @pl.when(jnp.logical_not(line_ends(tp)))
+        def _():
+            pltpu.make_async_copy(middle.at[pl.ds(row, rows), where], target, sem).start()
+
+        return jnp.where(tp < 2, 3, 0) * per_quarter + step
+
+    return plan
 
 
 def scan_kernel(kept, given, decay, gain, skip, state_in, local_ref, state_out, prod):
@@ -184,8 +264,8 @@
         scratch_shapes=[pltpu.VMEM((rows,) + lanes, jnp.float32)],
         compiler_params=pltpu.CompilerParams(vmem_limit_bytes=24 * MIB),
         cost_estimate=pl.CostEstimate(
-            flops=64 * rows * lanes[0] * lanes[1],
-            bytes_accessed=rows * lanes[0] * lanes[1] * 8,
+            flops=0,
+            bytes_accessed=0,
             transcendentals=0,
         ),
         name="scan",
@@ -280,23 +360,62 @@
     seq_len = 2 * n_ctx * seg_len
     pair_index = lax.axis_index("fsdp")
     ctx_index = lax.axis_index("ctx")
-    place = jnp.stack([pair_index, ctx_index]).astype(jnp.int32)
+    place = jnp.stack([pair_index, ctx_index, lax.axis_index("tp")]).astype(jnp.int32)
+
+    starts = [sum(CHUNKS[:k]) for k in range(len(CHUNKS))]
+    on_line = lax.axis_size("tp") == 4
+    passed, arrived = [], []
+    if on_line:
+        near = lax.ppermute(tokens, "tp", [(0, 1), (1, 0), (2, 3), (3, 2)])
+        middle, ends, row = [], [], 0
+        for rows in HALVES:
+            block = lax.slice_in_dim(tokens, row, row + rows, axis=0)
+            middle.append(lax.ppermute(block, "tp", [(1, 2), (2, 1)]))
+            ends.append(lax.ppermute(middle[-1], "tp", [(1, 0), (2, 3)]))
+            row += rows
+        far_middle, row = [], 0
+        for rows in FAR:
+            block = lax.slice_in_dim(near, row, row + rows, axis=0)
+            far_middle.append(lax.ppermute(block, "tp", [(1, 2), (2, 1)]))
+            row += rows
+        passed = ends + far_middle
+        arrived = [near] + middle
 
     own = weight.transpose(1, 0, 2)
     part = own.shape[1] // n_ctx
-    per_part = part // DEPTH
+    piece_len = DEPTH // 2
+    per_part = part // piece_len
     pieces = {}
+    bits = []
+    while 1 << len(bits) < n_ctx:
+        bits.insert(0, 1 << len(bits))
+    first = []
     for sub in range(per_part):
-        piece = lax.dynamic_slice_in_dim(own, ctx_index * part + sub * DEPTH, DEPTH, 1)
-        held = {0: exchanged(piece, "fsdp", 1)}
-        bit = n_ctx // 2
-        while bit:
+        piece = lax.dynamic_slice_in_dim(own, ctx_index * part + sub * piece_len, piece_len, 1)
+        if sub >= 2:
+            piece = after(piece, first[sub - 2])
+        if sub >= 3:
+            piece = after(piece, *[pieces[m, sub - 3] for m in range(n_ctx)])
+        first.append(exchanged(piece, "fsdp", 1))
+        held = {0: first[sub]}
+        for bit in bits:
             for mask in list(held):
-                held[mask | bit] = exchanged(held[mask], "ctx", bit)
-            bit //= 2
+                block = held[mask]
+                if bit == bits[0] and sub:
+                    block = after(block, pieces[bit, sub - 1])
+                if bit == bits[0] and sub >= 2:
+                    block = after(block, *[pieces[m, sub - 2] for m in range(n_ctx)])
+                if bit == bits[-1] and sub == per_part - 1:
+                    block = after(block, *passed)
+                if bit == bits[-1] and mask and sub in (0, per_part - 1):
+                    block = after(block, latest)
+                latest = exchanged(block, "ctx", bit)
+                held[mask | bit] = latest
         for mask in range(n_ctx):
             pieces[mask, sub] = held[mask]
     ordered = [pieces[mask, sub] for mask in range(n_ctx) for sub in range(per_part)]
+    plan = Plan(own.shape[1] // DEPTH, part // DEPTH, len(ordered))
+    per_quarter = tokens.shape[1] // DEPTH
 
     channels = rate.shape[0]
     groups = channels // 128
@@ -310,20 +429,49 @@
     gain = spread(pole_gain(rate, residue, float(seq_len)))
     direct = spread(skip[:, None])[0]
 
+    if on_line:
+        far_ends, where = [], []
+        for k, (base, rows) in enumerate(zip(starts, CHUNKS)):
+            row, n = base, 0
+            while row >= FAR[n]:
+                row -= FAR[n]
+                n += 1
+            where.append((n, row))
+            block = lax.slice_in_dim(far_middle[n], row, row + rows, axis=0)
+            if k >= 3:
+                block = after(block, far_ends[k - 3])
+            far_ends.append(lax.ppermute(block, "tp", [(1, 0), (2, 3)]))
+        near = after(near, *far_middle)
+        partial = project(
+            plan, place, [tokens, near, *middle, *ends], own, ordered, None, 0, seg_len,
+            3 * per_quarter, first_plan(per_quarter, len(HALVES)), False,
+        )
+    else:
+        partial = None
+
     kept, given, locals_ = [], [], []
     state = jnp.zeros_like(decay)
-    base = 0
-    for k, rows in enumerate(CHUNKS):
-        block = lax.slice_in_dim(tokens, base, base + rows, axis=0)
-        base += rows
-        whole = lax.all_gather(block, "tp", axis=0, tiled=False)
-        if k < 2:
-            partial = project(place, whole, own, [], 1, None, False)
-            keep, give = project(place, whole, None, ordered, per_part, partial, True)
+    states = []
+    for k, (base, rows) in enumerate(zip(starts, CHUNKS)):
+        if partial is not None:
+            last = far_ends[k]
+            if k == len(CHUNKS) - 1:
+                last = after(last, states[k - 3])
+            n, row = where[k]
+            keep, give = project(
+                plan, place, [far_middle[n], last], own, ordered, partial, base, rows,
+                per_quarter, last_plan(per_quarter, row, rows), True,
+            )
         else:
-            keep, give = project(place, whole, own, ordered, per_part, None, True)
+            block = lax.slice_in_dim(tokens, base, base + rows, axis=0)
+            whole = lax.all_gather(block, "tp", axis=0, tiled=False)
+            keep, give = project(
+                plan, place, [whole], own, ordered, None, 0, rows,
+                2 * plan.half_blocks, gathered_plan(per_quarter), True,
+            )
         got = exchanged(give, "fsdp", 1)
         local, state = scan(keep, got, decay, gain, direct, state)
+        states.append(state)
         kept.append(keep)
         given.append(got)
         locals_.append(local)

time: 405 us -> 361 us (0.89)
  waiting for transfers between devices: 233 us -> 155 us
  starting transfers between devices: 16.2 us -> 56.4 us
  between operations: 13.4 us -> 0.33 us
  Pallas kernels: 117 us -> 122 us
  local copies, waits for them, and re-layouts: 21.6 us -> 26.1 us
    ppermute x15 -> x24, waiting for transfers between devices: 204 us -> 114 us  [exchanged(): return lax.ppermute(block, axis, [(i, i ^ mask) for i in range(count)])]
    ppermute x0 -> x9, waiting for transfers between devices: none -> 41.1 us  [the longest x1 31.8 us: per_device(): far_middle.append(lax.ppermute(block, 'tp', [(1, 2), (2, 1)]))]
    all_gather x4 -> x0, waiting for transfers between devices: 27.3 us -> none  [per_device(): whole = lax.all_gather(block, 'tp', axis=0, tiled=False)]
    ppermute x0 -> x9, starting transfers between devices: none -> 23.1 us  [the longest x5 13.8 us: per_device(): far_ends.append(lax.ppermute(block, 'tp', [(1, 0), (2, 3)]))]
    ppermute x15 -> x24, starting transfers between devices: 16.1 us -> 33.3 us  [exchanged(): return lax.ppermute(block, axis, [(i, i ^ mask) for i in range(count)])]
    pallas_call x6, Pallas kernels: 89.5 us -> 94.5 us  [project(): pl.pallas_call(functools.partial(project_kernel, plan, len(inputs), init...]
    unnamed x36 -> x58, local copies, waits for them, and re-layouts: 13.6 us -> 18.4 us
    pallas_call x4 -> x5, Pallas kernels: 15.9 us -> 15.8 us  [scan(): pl.pallas_call(scan_kernel, in_specs=[local] * 6, out_specs=[local] * 2,...]
  transfers between devices with their start and end apart: 19 -> 33, of which waited for: 7 -> 13; matrix products, arithmetic and copies ran while one was open for 1% -> 2% of each run, Pallas kernels for 26% -> 30%
where the time goes in v2:
time: 361 us; the launch traced here: 360 us
  waiting for transfers between devices  155 us (43%)
  Pallas kernels  122 us (34%)
  starting transfers between devices  56.4 us (16%)
  local copies, waits for them, and re-layouts  26.1 us (7%)
    ppermute x24, waiting for transfers between devices, exchanged(): return lax.ppermute(block, axis, [(i, i ^ mask) for i in range(count)])  114 us
    pallas_call x6, Pallas kernels, project(): pl.pallas_call(functools.partial(project_kernel, plan, len(inputs), init...  94.5 us
    ppermute x24, starting transfers between devices, exchanged(): return lax.ppermute(block, axis, [(i, i ^ mask) for i in range(count)])  33.3 us
    ppermute x1, waiting for transfers between devices, per_device(): far_middle.append(lax.ppermute(block, 'tp', [(1, 2), (2, 1)]))  31.8 us
    unnamed x58, local copies, waits for them, and re-layouts  18.4 us
    pallas_call x5, Pallas kernels, scan(): pl.pallas_call(scan_kernel, in_specs=[local] * 6, out_specs=[local] * 2,...  15.8 us
    ppermute x5, starting transfers between devices, per_device(): far_ends.append(lax.ppermute(block, 'tp', [(1, 0), (2, 3)]))  13.8 us
    pallas_call x1, Pallas kernels, finish(): pl.pallas_call(functools.partial(finish_kernel, len(ends), n_chunks, seg_...  11.5 us
  transfers between devices with their start and end apart: 33, of which 13 were waited for; matrix products, arithmetic and copies ran while one was open for 2% of the time, Pallas kernels for 30%

profile of v2, /device:TPU:9, one launch (start us, length us, event | category | flops | bytes accessed | tf_op | source)
XLA Modules:
  0.0 360.0 jit_solution(8714502763458811772)
XLA Ops:
  0.0 4.5 %collective-permute-start.13 = (bf16[1024,2048]{1,0:T(8,128)(2,1)}, bf16[1024,2048]{1,0:T(8,128)(2,1)}, u32[]{:S(2)}, u32[]{:S(2)}) collective-permute-start(bf16[1024,2048]{1,0:T(8,128)(2,1)} %refs_0_.1), channel_id=1, source_target_pairs={{2,4},{4,2},{3,5},{5,3},{10,12},{12,10},{11,13},{13,11},{18,20},{2... | collective-permute-start | bytes 12582920 | tf_op jit(solution)/shard_map/ppermute | solution.py:373
  4.5 3.6 dynamic-slice_bitcast_fusion
  9.6 33.3 %collective-permute-done.4.refs_5_.refs_3_ = bf16[3,256,1024]{2,1,0:T(8,128)(2,1)S(1)} collective-permute-done((bf16[3,256,1024]{2,1,0:T(8,128)(2,1)S(1)}, bf16[3,256,1024]{2,1,0:T(8,128)(2,1)S(1)}, u32[]{:S(2)}, u32[]{:S(2)}) %collective-permute-start.4) | collective-permute-done | bytes 1572896 | tf_op jit(solution)/shard_map/ppermute | solution.py:26
  44.1 4.1 %collective-permute-start.7 = (bf16[3,256,1024]{2,1,0:T(8,128)(2,1)S(1)}, bf16[3,256,1024]{2,1,0:T(8,128)(2,1)S(1)}, u32[]{:S(2)}, u32[]{:S(2)}) collective-permute-start(bf16[3,256,1024]{2,1,0:T(8,128)(2,1)S(1)} %collective-permute-done.4.refs_5_.refs_3_), channel_id=1, source_target_pairs={{0,8},{8,0},{16,24},{24,16},{1,9},{9,1},{17,25},{25,17},{2,10},{10... | collective-permute-start | bytes 4718600 | tf_op jit(solution)/shard_map/ppermute | solution.py:26
  48.2 28.4 %collective-permute-done.5.refs_6_.refs_4_ = bf16[3,256,1024]{2,1,0:T(8,128)(2,1)S(1)} collective-permute-done((bf16[3,256,1024]{2,1,0:T(8,128)(2,1)S(1)}, bf16[3,256,1024]{2,1,0:T(8,128)(2,1)S(1)}, u32[]{:S(2)}, u32[]{:S(2)}) %collective-permute-start.5) | collective-permute-done | bytes 1572896 | tf_op jit(solution)/shard_map/ppermute | solution.py:26
  80.2 2.6 collective-permute-start.9
  82.8 8.9 %collective-permute-done.refs_1_ = bf16[1024,2048]{1,0:T(8,128)(2,1)} collective-permute-done((bf16[1024,2048]{1,0:T(8,128)(2,1)}, bf16[1024,2048]{1,0:T(8,128)(2,1)}, u32[]{:S(2)}, u32[]{:S(2)}) %collective-permute-start) | collective-permute-done | bytes 4194336 | tf_op jit(solution)/shard_map/ppermute | solution.py:369
  91.8 3.2 collective-permute-start.1
  95.0 1.6 collective-permute-start.14
  96.5 13.9 %collective-permute-done.6.refs_7_.refs_5_ = bf16[3,256,1024]{2,1,0:T(8,128)(2,1)S(1)} collective-permute-done((bf16[3,256,1024]{2,1,0:T(8,128)(2,1)S(1)}, bf16[3,256,1024]{2,1,0:T(8,128)(2,1)S(1)}, u32[]{:S(2)}, u32[]{:S(2)}) %collective-permute-start.6) | collective-permute-done | bytes 1572896 | tf_op jit(solution)/shard_map/ppermute | solution.py:26
  113.0 3.8 %collective-permute-start.11 = (bf16[3,256,1024]{2,1,0:T(8,128)(2,1)S(1)}, bf16[3,256,1024]{2,1,0:T(8,128)(2,1)S(1)}, u32[]{:S(2)}, u32[]{:S(2)}) collective-permute-start(bf16[3,256,1024]{2,1,0:T(8,128)(2,1)S(1)} %collective-permute-done.5.refs_6_.refs_4_), channel_id=1, source_target_pairs={{0,8},{8,0},{16,24},{24,16},{1,9},{9,1},{17,25},{25,17},{2,10},{10... | collective-permute-start | bytes 4718600 | tf_op jit(solution)/shard_map/ppermute | solution.py:26
  116.7 27.6 %collective-permute-done.17.refs_15_.refs_13_ = bf16[3,256,1024]{2,1,0:T(8,128)(2,1)} collective-permute-done((bf16[3,256,1024]{2,1,0:T(8,128)(2,1)S(1)}, bf16[3,256,1024]{2,1,0:T(8,128)(2,1)}, u32[]{:S(2)}, u32[]{:S(2)}) %collective-permute-start.17) | collective-permute-done | bytes 1572896 | tf_op jit(solution)/shard_map/ppermute | solution.py:26
  144.4 4.1 %collective-permute-start.18 = (bf16[3,256,1024]{2,1,0:T(8,128)(2,1)S(1)}, bf16[3,256,1024]{2,1,0:T(8,128)(2,1)S(1)}, u32[]{:S(2)}, u32[]{:S(2)}) collective-permute-start(bf16[3,256,1024]{2,1,0:T(8,128)(2,1)S(1)} %collective-permute-done.16.refs_14_.refs_12_), channel_id=1, source_target_pairs={{0,8},{8,0},{16,24},{24,16},{1,9},{9,1},{17,25},{25,17},{2,10},{10... | collective-permute-start | bytes 4718600 | tf_op jit(solution)/shard_map/ppermute | solution.py:26
  149.6 1.9 collective-permute-done.18.refs_18_.refs_16_
  152.7 31.8 %collective-permute-done.1.refs_0_ = bf16[1024,2048]{1,0:T(8,128)(2,1)S(1)} collective-permute-done((bf16[1024,2048]{1,0:T(8,128)(2,1)}, bf16[1024,2048]{1,0:T(8,128)(2,1)S(1)}, u32[]{:S(2)}, u32[]{:S(2)}) %collective-permute-start.1) | collective-permute-done | bytes 4194336 | tf_op jit(solution)/shard_map/ppermute | solution.py:379
  184.9 2.5 collective-permute-start.15
  191.9 1.8 fusion
  193.7 5.0 %collective-permute-start.23 = (bf16[256,2048]{1,0:T(8,128)(2,1)}, bf16[256,2048]{1,0:T(8,128)(2,1)}, u32[]{:S(2)}, u32[]{:S(2)}) collective-permute-start(bf16[256,2048]{1,0:T(8,128)(2,1)} %get-tuple-element.82), channel_id=1, source_target_pairs={{2,0},{4,6},{3,1},{5,7},{10,8},{12,14},{11,9},{13,15},{18,16},{20,... | collective-permute-start | bytes 3145736 | tf_op jit(solution)/shard_map/ppermute | solution.py:443
  198.7 2.3 collective-permute-start.2
  202.2 2.3 collective-permute-start.28
  204.5 1.4 copy-done.1
  205.9 1.4 copy-done.4
  207.3 1.4 copy-done.7
  208.7 1.4 copy-done.10
  210.1 50.0 %project.6.refs_19_ = f32[3,1024,1024]{2,1,0:T(8,128)} custom-call(s32[3]{0:T(128)S(1)} %pad_add_fusion.place, bf16[1024,2048]{1,0:T(8,128)(2,1)} %refs_0_.1, bf16[1024,2048]{1,0:T(8,128)(2,1)} %collective-permute-done.refs_1_, bf16[1024,2048]{1,0:T(8,128)(2,1)} %collective-permute-done.13.refs_2_, bf16[1024,2048]{1,0:T(8,128)(2,1)} %copy-done.25, ...), custom_call_target="tpu_custom_call" | custom-call | tf_op jit(solution)/shard_map/project/pallas_call | solution.py:129
  260.2 9.7 %project.8 = (bf16[3,256,512]{2,1,0:T(8,128)(2,1)S(1)}, bf16[3,256,512]{2,1,0:T(8,128)(2,1)}) custom-call(s32[3]{0:T(128)S(1)} %pad_add_fusion.place, bf16[1024,2048]{1,0:T(8,128)(2,1)} %copy-done.18, bf16[256,2048]{1,0:T(8,128)(2,1)} %collective-permute-done.23.refs_1_, bf16[3,4096,1024]{2,1,0:T(8,128)(2,1)} %bitcast.19, ...), custom_call_target="tpu_custom_call" | custom-call | tf_op jit(solution)/shard_map/project/pallas_call | solution.py:129
  270.8 9.7 %project.7 = (bf16[3,256,512]{2,1,0:T(8,128)(2,1)S(1)}, bf16[3,256,512]{2,1,0:T(8,128)(2,1)}) custom-call(s32[3]{0:T(128)S(1)} %pad_add_fusion.place, bf16[1024,2048]{1,0:T(8,128)(2,1)} %copy-done.18, bf16[256,2048]{1,0:T(8,128)(2,1)} %collective-permute-done.2.refs_1_, bf16[3,4096,1024]{2,1,0:T(8,128)(2,1)} %bitcast.20, ...), custom_call_target="tpu_custom_call" | custom-call | tf_op jit(solution)/shard_map/project/pallas_call | solution.py:129
  281.4 1.5 collective-permute-start.22
  282.9 2.3 fusion.1
  285.1 2.1 collective-permute-start.26
  287.2 2.2 collective-permute-start.3
  289.5 9.7 %project.11 = (bf16[3,256,512]{2,1,0:T(8,128)(2,1)S(1)}, bf16[3,256,512]{2,1,0:T(8,128)(2,1)}) custom-call(s32[3]{0:T(128)S(1)} %pad_add_fusion.place, bf16[1024,2048]{1,0:T(8,128)(2,1)} %copy-done.18, bf16[256,2048]{1,0:T(8,128)(2,1)} %collective-permute-done.28.refs_1_, bf16[3,4096,1024]{2,1,0:T(8,128)(2,1)} %bitcast.21, ...), custom_call_target="tpu_custom_call" | custom-call | tf_op jit(solution)/shard_map/project/pallas_call | solution.py:129
  300.3 1.4 copy-done.2
  301.7 1.4 copy-done.5
  303.1 1.4 copy-done.8
  304.5 7.7 %project.10 = (bf16[3,128,512]{2,1,0:T(8,128)(2,1)S(1)}, bf16[3,128,512]{2,1,0:T(8,128)(2,1)S(1)}) custom-call(s32[3]{0:T(128)S(1)} %pad_add_fusion.place, bf16[1024,2048]{1,0:T(8,128)(2,1)} %copy-done.18, bf16[128,2048]{1,0:T(8,128)(2,1)} %collective-permute-done.26.refs_1_, bf16[3,4096,1024]{2,1,0:T(8,128)(2,1)} %bitcast.22, ...), custom_call_target="tpu_custom_call" | custom-call | tf_op jit(solution)/shard_map/project/pallas_call | solution.py:129
  312.2 1.5 collective-permute-start.27
  313.8 4.2 %scan.5 = (f32[256,8,128]{2,1,0:T(8,128)S(1)}, f32[16,8,128]{2,1,0:T(8,128)S(1)}) custom-call(bf16[3,256,512]{2,1,0:T(8,128)(2,1)S(1)} %copy-done.12, bf16[3,256,512]{2,1,0:T(8,128)(2,1)} %collective-permute-done.24.given.refs_16_, f32[16,8,128]{2,1,0:T(8,128)S(1)} %get-tuple-element.87.decay.refs_5_, f32[16,8,128]{2,1,0:T(8,128)S(1)} %pad_maximum_fusion.1.gain, ...), custom_call_target="tpu_custom_call" | custom-call | tf_op jit(solution)/shard_map/scan/pallas_call | solution.py:256
  318.0 4.2 %scan.6 = (f32[256,8,128]{2,1,0:T(8,128)S(1)}, f32[16,8,128]{2,1,0:T(8,128)S(1)}) custom-call(bf16[3,256,512]{2,1,0:T(8,128)(2,1)S(1)} %copy-done.14, bf16[3,256,512]{2,1,0:T(8,128)(2,1)} %collective-permute-done.22.given.refs_17_, f32[16,8,128]{2,1,0:T(8,128)S(1)} %get-tuple-element.87.decay.refs_5_, f32[16,8,128]{2,1,0:T(8,128)S(1)} %pad_maximum_fusion.1.gain, ...), custom_call_target="tpu_custom_call" | custom-call | tf_op jit(solution)/shard_map/scan/pallas_call | solution.py:256
  322.2 7.7 %project.9 = (bf16[3,128,512]{2,1,0:T(8,128)(2,1)S(1)}, bf16[3,128,512]{2,1,0:T(8,128)(2,1)S(1)}) custom-call(s32[3]{0:T(128)S(1)} %pad_add_fusion.place, bf16[1024,2048]{1,0:T(8,128)(2,1)} %copy-done.18, bf16[128,2048]{1,0:T(8,128)(2,1)} %collective-permute-done.3.refs_1_, bf16[3,4096,1024]{2,1,0:T(8,128)(2,1)} %bitcast.23, ...), custom_call_target="tpu_custom_call" | custom-call | tf_op jit(solution)/shard_map/project/pallas_call | solution.py:129
  330.1 4.2 %scan.7 = (f32[256,8,128]{2,1,0:T(8,128)S(1)}, f32[16,8,128]{2,1,0:T(8,128)S(1)}) custom-call(bf16[3,256,512]{2,1,0:T(8,128)(2,1)S(1)} %copy-done.16, bf16[3,256,512]{2,1,0:T(8,128)(2,1)} %collective-permute-done.29.given.refs_18_, f32[16,8,128]{2,1,0:T(8,128)S(1)} %get-tuple-element.87.decay.refs_5_, f32[16,8,128]{2,1,0:T(8,128)S(1)} %pad_maximum_fusion.1.gain, ...), custom_call_target="tpu_custom_call" | custom-call | tf_op jit(solution)/shard_map/scan/pallas_call | solution.py:256
  334.4 1.5 scan.8
  335.9 3.2 collective-permute-done.25.given.refs_20_
  339.1 1.5 scan.9
  340.7 2.5 collective-permute-start.30
  344.9 2.0 collective-permute-done.31.refs_2_
  346.9 1.6 collective-permute-done.32.refs_3_
  348.4 11.5 %finish.1 = bf16[512,2048]{1,0:T(8,128)(2,1)} custom-call(s32[3]{0:T(128)S(1)} %pad_add_fusion.place, s32[8]{0:T(128)S(1)} %copy-done.17, f32[16,8,128]{2,1,0:T(8,128)S(1)} %get-tuple-element.71.refs_0_, f32[16,8,128]{2,1,0:T(8,128)S(1)} %collective-permute-done.30.refs_1_, f32[16,8,128]{2,1,0:T(8,128)S(1)} %collective-permute-done.31.refs_2_, ...), custom_call_target="tpu_custom_call" | custom-call | flops 33554432 | bytes 8388608 | tf_op jit(solution)/shard_map/finish/pallas_call | solution.py:337
  (99 shorter events, 22.3 us)
Async XLA Ops:
  0.0 91.8 %collective-permute-start = (bf16[1024,2048]{1,0:T(8,128)(2,1)}, bf16[1024,2048]{1,0:T(8,128)(2,1)}, u32[]{:S(2)}, u32[]{:S(2)}) collective-permute-start(bf16[1024,2048]{1,0:T(8,128)(2,1)} %refs_0_.1), channel_id=1, source_target_pairs={{0,2},{2,0},{4,6},{6,4},{1,3},{3,1},{5,7},{7,5},{8,10},{10,8},{12,... | collective-permute-start | bytes 12582920 | tf_op jit(solution)/shard_map/ppermute | solution.py:369
  0.0 95.0 %collective-permute-start.13 = (bf16[1024,2048]{1,0:T(8,128)(2,1)}, bf16[1024,2048]{1,0:T(8,128)(2,1)}, u32[]{:S(2)}, u32[]{:S(2)}) collective-permute-start(bf16[1024,2048]{1,0:T(8,128)(2,1)} %refs_0_.1), channel_id=1, source_target_pairs={{2,4},{4,2},{3,5},{5,3},{10,12},{12,10},{11,13},{13,11},{18,20},{2... | collective-permute-start | bytes 12582920 | tf_op jit(solution)/shard_map/ppermute | solution.py:373
  8.1 34.8 %collective-permute-start.4 = (bf16[3,256,1024]{2,1,0:T(8,128)(2,1)S(1)}, bf16[3,256,1024]{2,1,0:T(8,128)(2,1)S(1)}, u32[]{:S(2)}, u32[]{:S(2)}) collective-permute-start(bf16[3,256,1024]{2,1,0:T(8,128)(2,1)S(1)} %get-tuple-element.79), channel_id=1, source_target_pairs={{0,1},{1,0},{2,3},{3,2},{4,5},{5,4},{6,7},{7,6},{8,9},{9,8},{10,11... | collective-permute-start | bytes 4718600 | tf_op jit(solution)/shard_map/ppermute | solution.py:26
  9.4 67.2 %collective-permute-start.5 = (bf16[3,256,1024]{2,1,0:T(8,128)(2,1)S(1)}, bf16[3,256,1024]{2,1,0:T(8,128)(2,1)S(1)}, u32[]{:S(2)}, u32[]{:S(2)}) collective-permute-start(bf16[3,256,1024]{2,1,0:T(8,128)(2,1)S(1)} %get-tuple-element.78), channel_id=1, source_target_pairs={{0,1},{1,0},{2,3},{3,2},{4,5},{5,4},{6,7},{7,6},{8,9},{9,8},{10,11... | collective-permute-start | bytes 4718600 | tf_op jit(solution)/shard_map/ppermute | solution.py:26
  42.9 34.9 %collective-permute-start.8 = (bf16[3,256,1024]{2,1,0:T(8,128)(2,1)S(1)}, bf16[3,256,1024]{2,1,0:T(8,128)(2,1)S(1)}, u32[]{:S(2)}, u32[]{:S(2)}) collective-permute-start(bf16[3,256,1024]{2,1,0:T(8,128)(2,1)S(1)} %collective-permute-done.4.refs_5_.refs_3_), channel_id=1, source_target_pairs={{0,16},{8,24},{16,0},{24,8},{1,17},{9,25},{17,1},{25,9},{2,18},{10... | collective-permute-start | bytes 4718600 | tf_op jit(solution)/shard_map/ppermute | solution.py:26
  44.1 35.0 %collective-permute-start.7 = (bf16[3,256,1024]{2,1,0:T(8,128)(2,1)S(1)}, bf16[3,256,1024]{2,1,0:T(8,128)(2,1)S(1)}, u32[]{:S(2)}, u32[]{:S(2)}) collective-permute-start(bf16[3,256,1024]{2,1,0:T(8,128)(2,1)S(1)} %collective-permute-done.4.refs_5_.refs_3_), channel_id=1, source_target_pairs={{0,8},{8,0},{16,24},{24,16},{1,9},{9,1},{17,25},{25,17},{2,10},{10... | collective-permute-start | bytes 4718600 | tf_op jit(solution)/shard_map/ppermute | solution.py:26
  76.6 33.8 %collective-permute-start.6 = (bf16[3,256,1024]{2,1,0:T(8,128)(2,1)S(1)}, bf16[3,256,1024]{2,1,0:T(8,128)(2,1)S(1)}, u32[]{:S(2)}, u32[]{:S(2)}) collective-permute-start(bf16[3,256,1024]{2,1,0:T(8,128)(2,1)S(1)} %get-tuple-element.42), channel_id=1, source_target_pairs={{0,1},{1,0},{2,3},{3,2},{4,5},{5,4},{6,7},{7,6},{8,9},{9,8},{10,11... | collective-permute-start | bytes 4718600 | tf_op jit(solution)/shard_map/ppermute | solution.py:26
  77.8 34.8 %copy-start.19 = (bf16[3,256,1024]{2,1,0:T(8,128)(2,1)}, bf16[3,256,1024]{2,1,0:T(8,128)(2,1)S(1)}, u32[]{:S(2)}) copy-start(bf16[3,256,1024]{2,1,0:T(8,128)(2,1)S(1)} %collective-permute-done.8.refs_13_.refs_11_) | copy-start | bytes 4718596
  77.8 33.6 %collective-permute-start.16 = (bf16[3,256,1024]{2,1,0:T(8,128)(2,1)S(1)}, bf16[3,256,1024]{2,1,0:T(8,128)(2,1)S(1)}, u32[]{:S(2)}, u32[]{:S(2)}) collective-permute-start(bf16[3,256,1024]{2,1,0:T(8,128)(2,1)S(1)} %collective-permute-done.5.refs_6_.refs_4_), channel_id=1, source_target_pairs={{0,16},{8,24},{16,0},{24,8},{1,17},{9,25},{17,1},{25,9},{2,18},{10... | collective-permute-start | bytes 4718600 | tf_op jit(solution)/shard_map/ppermute | solution.py:26
  80.2 31.2 %collective-permute-start.9 = (bf16[3,256,1024]{2,1,0:T(8,128)(2,1)S(1)}, bf16[3,256,1024]{2,1,0:T(8,128)(2,1)S(1)}, u32[]{:S(2)}, u32[]{:S(2)}) collective-permute-start(bf16[3,256,1024]{2,1,0:T(8,128)(2,1)S(1)} %collective-permute-done.8.refs_13_.refs_11_), channel_id=1, source_target_pairs={{0,8},{8,0},{16,24},{24,16},{1,9},{9,1},{17,25},{25,17},{2,10},{10... | collective-permute-start | bytes 4718600 | tf_op jit(solution)/shard_map/ppermute | solution.py:26
  91.8 92.7 %collective-permute-start.1 = (bf16[1024,2048]{1,0:T(8,128)(2,1)}, bf16[1024,2048]{1,0:T(8,128)(2,1)S(1)}, u32[]{:S(2)}, u32[]{:S(2)}) collective-permute-start(bf16[1024,2048]{1,0:T(8,128)(2,1)} %collective-permute-done.refs_1_), channel_id=1, source_target_pairs={{2,4},{4,2},{3,5},{5,3},{10,12},{12,10},{11,13},{13,11},{18,20},{2... | collective-permute-start | bytes 12582920 | tf_op jit(solution)/shard_map/ppermute | solution.py:379
  95.0 89.9 %collective-permute-start.14 = (bf16[1024,2048]{1,0:T(8,128)(2,1)}, bf16[1024,2048]{1,0:T(8,128)(2,1)S(1)}, u32[]{:S(2)}, u32[]{:S(2)}) collective-permute-start(bf16[1024,2048]{1,0:T(8,128)(2,1)} %collective-permute-done.13.refs_2_), channel_id=1, source_target_pairs={{2,0},{4,6},{3,1},{5,7},{10,8},{12,14},{11,9},{13,15},{18,16},{20,... | collective-permute-start | bytes 12582920 | tf_op jit(solution)/shard_map/ppermute | solution.py:374
  110.4 83.3 %copy-start.3 = (bf16[3,256,1024]{2,1,0:T(8,128)(2,1)}, bf16[3,256,1024]{2,1,0:T(8,128)(2,1)S(1)}, u32[]{:S(2)}) copy-start(bf16[3,256,1024]{2,1,0:T(8,128)(2,1)S(1)} %collective-permute-done.6.refs_7_.refs_5_) | copy-start | bytes 4718596
  111.4 79.0 %copy-start.20 = (bf16[3,256,1024]{2,1,0:T(8,128)(2,1)}, bf16[3,256,1024]{2,1,0:T(8,128)(2,1)S(1)}, u32[]{:S(2)}) copy-start(bf16[3,256,1024]{2,1,0:T(8,128)(2,1)S(1)} %collective-permute-done.16.refs_14_.refs_12_) | copy-start | bytes 4718596
  111.4 33.0 %collective-permute-start.17 = (bf16[3,256,1024]{2,1,0:T(8,128)(2,1)S(1)}, bf16[3,256,1024]{2,1,0:T(8,128)(2,1)}, u32[]{:S(2)}, u32[]{:S(2)}) collective-permute-start(bf16[3,256,1024]{2,1,0:T(8,128)(2,1)S(1)} %collective-permute-done.6.refs_7_.refs_5_), channel_id=1, source_target_pairs={{0,16},{8,24},{16,0},{24,8},{1,17},{9,25},{17,1},{25,9},{2,18},{10... | collective-permute-start | bytes 4718600 | tf_op jit(solution)/shard_map/ppermute | solution.py:26
  112.7 35.8 %collective-permute-start.10 = (bf16[3,256,1024]{2,1,0:T(8,128)(2,1)S(1)}, bf16[3,256,1024]{2,1,0:T(8,128)(2,1)S(1)}, u32[]{:S(2)}, u32[]{:S(2)}) collective-permute-start(bf16[3,256,1024]{2,1,0:T(8,128)(2,1)S(1)} %get-tuple-element.45), channel_id=1, source_target_pairs={{0,1},{1,0},{2,3},{3,2},{4,5},{5,4},{6,7},{7,6},{8,9},{9,8},{10,11... | collective-permute-start | bytes 4718600 | tf_op jit(solution)/shard_map/ppermute | solution.py:26
  113.0 35.5 %collective-permute-start.11 = (bf16[3,256,1024]{2,1,0:T(8,128)(2,1)S(1)}, bf16[3,256,1024]{2,1,0:T(8,128)(2,1)S(1)}, u32[]{:S(2)}, u32[]{:S(2)}) collective-permute-start(bf16[3,256,1024]{2,1,0:T(8,128)(2,1)S(1)} %collective-permute-done.5.refs_6_.refs_4_), channel_id=1, source_target_pairs={{0,8},{8,0},{16,24},{24,16},{1,9},{9,1},{17,25},{25,17},{2,10},{10... | collective-permute-start | bytes 4718600 | tf_op jit(solution)/shard_map/ppermute | solution.py:26
  144.4 7.1 %collective-permute-start.18 = (bf16[3,256,1024]{2,1,0:T(8,128)(2,1)S(1)}, bf16[3,256,1024]{2,1,0:T(8,128)(2,1)S(1)}, u32[]{:S(2)}, u32[]{:S(2)}) collective-permute-start(bf16[3,256,1024]{2,1,0:T(8,128)(2,1)S(1)} %collective-permute-done.16.refs_14_.refs_12_), channel_id=1, source_target_pairs={{0,8},{8,0},{16,24},{24,16},{1,9},{9,1},{17,25},{25,17},{2,10},{10... | collective-permute-start | bytes 4718600 | tf_op jit(solution)/shard_map/ppermute | solution.py:26
  151.5 38.9 %copy-start.22 = (bf16[3,256,1024]{2,1,0:T(8,128)(2,1)}, bf16[3,256,1024]{2,1,0:T(8,128)(2,1)S(1)}, u32[]{:S(2)}) copy-start(bf16[3,256,1024]{2,1,0:T(8,128)(2,1)S(1)} %collective-permute-done.18.refs_18_.refs_16_) | copy-start | bytes 4718596
  151.5 37.6 %collective-permute-start.19 = (bf16[3,256,1024]{2,1,0:T(8,128)(2,1)S(1)}, bf16[3,256,1024]{2,1,0:T(8,128)(2,1)}, u32[]{:S(2)}, u32[]{:S(2)}) collective-permute-start(bf16[3,256,1024]{2,1,0:T(8,128)(2,1)S(1)} %collective-permute-done.10.refs_8_.refs_6_), channel_id=1, source_target_pairs={{0,16},{8,24},{16,0},{24,8},{1,17},{9,25},{17,1},{25,9},{2,18},{10... | collective-permute-start | bytes 4718600 | tf_op jit(solution)/shard_map/ppermute | solution.py:26
  184.5 16.5 %copy-start.18 = (bf16[1024,2048]{1,0:T(8,128)(2,1)}, bf16[1024,2048]{1,0:T(8,128)(2,1)S(1)}, u32[]{:S(2)}) copy-start(bf16[1024,2048]{1,0:T(8,128)(2,1)S(1)} %collective-permute-done.1.refs_0_) | copy-start | bytes 12582916
  184.9 5.5 %copy-start.25 = (bf16[1024,2048]{1,0:T(8,128)(2,1)}, bf16[1024,2048]{1,0:T(8,128)(2,1)S(1)}, u32[]{:S(2)}) copy-start(bf16[1024,2048]{1,0:T(8,128)(2,1)S(1)} %collective-permute-done.14.refs_3_) | copy-start | bytes 12582916
  184.9 5.5 %collective-permute-start.15 = (bf16[3,256,1024]{2,1,0:T(8,128)(2,1)S(1)}, bf16[3,256,1024]{2,1,0:T(8,128)(2,1)S(1)}, u32[]{:S(2)}, u32[]{:S(2)}) collective-permute-start(bf16[3,256,1024]{2,1,0:T(8,128)(2,1)S(1)} %collective-permute-done.10.refs_8_.refs_6_), channel_id=1, source_target_pairs={{0,8},{8,0},{16,24},{24,16},{1,9},{9,1},{17,25},{25,17},{2,10},{10... | collective-permute-start | bytes 4718600 | tf_op jit(solution)/shard_map/ppermute | solution.py:26
  188.6 12.4 %collective-permute-start.12 = (bf16[3,256,1024]{2,1,0:T(8,128)(2,1)S(1)}, bf16[3,256,1024]{2,1,0:T(8,128)(2,1)S(1)}, u32[]{:S(2)}, u32[]{:S(2)}) collective-permute-start(bf16[3,256,1024]{2,1,0:T(8,128)(2,1)S(1)} %collective-permute-done.6.refs_7_.refs_5_), channel_id=1, source_target_pairs={{0,8},{8,0},{16,24},{24,16},{1,9},{9,1},{17,25},{25,17},{2,10},{10... | collective-permute-start | bytes 4718600 | tf_op jit(solution)/shard_map/ppermute | solution.py:26
  188.9 15.6 %collective-permute-start.20 = (bf16[3,256,1024]{2,1,0:T(8,128)(2,1)}, bf16[3,256,1024]{2,1,0:T(8,128)(2,1)}, u32[]{:S(2)}, u32[]{:S(2)}) collective-permute-start(bf16[3,256,1024]{2,1,0:T(8,128)(2,1)} %collective-permute-done.17.refs_15_.refs_13_), channel_id=1, source_target_pairs={{0,8},{8,0},{16,24},{24,16},{1,9},{9,1},{17,25},{25,17},{2,10},{10... | collective-permute-start | bytes 4718600 | tf_op jit(solution)/shard_map/ppermute | solution.py:26
  191.6 12.9 %collective-permute-start.21 = (bf16[3,256,1024]{2,1,0:T(8,128)(2,1)}, bf16[3,256,1024]{2,1,0:T(8,128)(2,1)}, u32[]{:S(2)}, u32[]{:S(2)}) collective-permute-start(bf16[3,256,1024]{2,1,0:T(8,128)(2,1)} %collective-permute-done.19.refs_16_.refs_14_), channel_id=1, source_target_pairs={{0,8},{8,0},{16,24},{24,16},{1,9},{9,1},{17,25},{25,17},{2,10},{10... | collective-permute-start | bytes 4718600 | tf_op jit(solution)/shard_map/ppermute | solution.py:26
  193.7 66.4 %collective-permute-start.23 = (bf16[256,2048]{1,0:T(8,128)(2,1)}, bf16[256,2048]{1,0:T(8,128)(2,1)}, u32[]{:S(2)}, u32[]{:S(2)}) collective-permute-start(bf16[256,2048]{1,0:T(8,128)(2,1)} %get-tuple-element.82), channel_id=1, source_target_pairs={{2,0},{4,6},{3,1},{5,7},{10,8},{12,14},{11,9},{13,15},{18,16},{20,... | collective-permute-start | bytes 3145736 | tf_op jit(solution)/shard_map/ppermute | solution.py:443
  198.7 72.1 %collective-permute-start.2 = (bf16[256,2048]{1,0:T(8,128)(2,1)}, bf16[256,2048]{1,0:T(8,128)(2,1)}, u32[]{:S(2)}, u32[]{:S(2)}) collective-permute-start(bf16[256,2048]{1,0:T(8,128)(2,1)} %get-tuple-element.83), channel_id=1, source_target_pairs={{2,0},{4,6},{3,1},{5,7},{10,8},{12,14},{11,9},{13,15},{18,16},{20,... | collective-permute-start | bytes 3145736 | tf_op jit(solution)/shard_map/ppermute | solution.py:443
  202.2 87.3 %collective-permute-start.28 = (bf16[256,2048]{1,0:T(8,128)(2,1)}, bf16[256,2048]{1,0:T(8,128)(2,1)}, u32[]{:S(2)}, u32[]{:S(2)}) collective-permute-start(bf16[256,2048]{1,0:T(8,128)(2,1)} %get-tuple-element.81), channel_id=1, source_target_pairs={{2,0},{4,6},{3,1},{5,7},{10,8},{12,14},{11,9},{13,15},{18,16},{20,... | collective-permute-start | bytes 3145736 | tf_op jit(solution)/shard_map/ppermute | solution.py:443
  204.5 1.4 copy-start.1
  270.8 43.0 %collective-permute-start.24 = (bf16[3,256,512]{2,1,0:T(8,128)(2,1)}, bf16[3,256,512]{2,1,0:T(8,128)(2,1)}, u32[]{:S(2)}, u32[]{:S(2)}) collective-permute-start(bf16[3,256,512]{2,1,0:T(8,128)(2,1)} %get-tuple-element.58), channel_id=1, source_target_pairs={{0,1},{1,0},{2,3},{3,2},{4,5},{5,4},{6,7},{7,6},{8,9},{9,8},{10,11... | collective-permute-start | bytes 2359304 | tf_op jit(solution)/shard_map/ppermute | solution.py:26
  281.4 36.6 %collective-permute-start.22 = (bf16[3,256,512]{2,1,0:T(8,128)(2,1)}, bf16[3,256,512]{2,1,0:T(8,128)(2,1)}, u32[]{:S(2)}, u32[]{:S(2)}) collective-permute-start(bf16[3,256,512]{2,1,0:T(8,128)(2,1)} %get-tuple-element.56), channel_id=1, source_target_pairs={{0,1},{1,0},{2,3},{3,2},{4,5},{5,4},{6,7},{7,6},{8,9},{9,8},{10,11... | collective-permute-start | bytes 2359304 | tf_op jit(solution)/shard_map/ppermute | solution.py:26
  285.1 15.1 %collective-permute-start.26 = (bf16[128,2048]{1,0:T(8,128)(2,1)}, bf16[128,2048]{1,0:T(8,128)(2,1)}, u32[]{:S(2)}, u32[]{:S(2)}) collective-permute-start(bf16[128,2048]{1,0:T(8,128)(2,1)} %get-tuple-element.64), channel_id=1, source_target_pairs={{2,0},{4,6},{3,1},{5,7},{10,8},{12,14},{11,9},{13,15},{18,16},{20,... | collective-permute-start | bytes 1572872 | tf_op jit(solution)/shard_map/ppermute | solution.py:443
  287.2 12.9 %copy-start.26 = (f32[512,16]{0,1:T(8,128)S(1)}, f32[512,16]{0,1:T(8,128)}, u32[]{:S(2)}) copy-start(f32[512,16]{0,1:T(8,128)} %param.8) | copy-start | bytes 98308
  287.2 12.9 %copy-start.27 = (f32[512,16]{0,1:T(8,128)S(1)}, f32[512,16]{0,1:T(8,128)}, u32[]{:S(2)}) copy-start(f32[512,16]{0,1:T(8,128)} %param.9) | copy-start | bytes 98308
  287.2 12.9 %copy-start.28 = (f32[512]{0:T(512)S(1)}, f32[512]{0:T(512)}, u32[]{:S(2)}) copy-start(f32[512]{0:T(512)} %param.10) | copy-start | bytes 6148
  287.2 35.0 %collective-permute-start.3 = (bf16[128,2048]{1,0:T(8,128)(2,1)}, bf16[128,2048]{1,0:T(8,128)(2,1)}, u32[]{:S(2)}, u32[]{:S(2)}) collective-permute-start(bf16[128,2048]{1,0:T(8,128)(2,1)} %get-tuple-element.41), channel_id=1, source_target_pairs={{2,0},{4,6},{3,1},{5,7},{10,8},{12,14},{11,9},{13,15},{18,16},{20,... | collective-permute-start | bytes 1572872 | tf_op jit(solution)/shard_map/ppermute | solution.py:443
  300.1 30.0 %collective-permute-start.29 = (bf16[3,256,512]{2,1,0:T(8,128)(2,1)}, bf16[3,256,512]{2,1,0:T(8,128)(2,1)}, u32[]{:S(2)}, u32[]{:S(2)}) collective-permute-start(bf16[3,256,512]{2,1,0:T(8,128)(2,1)} %get-tuple-element.68), channel_id=1, source_target_pairs={{0,1},{1,0},{2,3},{3,2},{4,5},{5,4},{6,7},{7,6},{8,9},{9,8},{10,11... | collective-permute-start | bytes 2359304 | tf_op jit(solution)/shard_map/ppermute | solution.py:26
  300.3 1.4 copy-start.2
  304.5 9.2 %copy-start.12 = (bf16[3,256,512]{2,1,0:T(8,128)(2,1)S(1)}, bf16[3,256,512]{2,1,0:T(8,128)(2,1)}, u32[]{:S(2)}) copy-start(bf16[3,256,512]{2,1,0:T(8,128)(2,1)} %copy-done.11) | copy-start | bytes 2359300
  312.2 5.8 %copy-start.14 = (bf16[3,256,512]{2,1,0:T(8,128)(2,1)S(1)}, bf16[3,256,512]{2,1,0:T(8,128)(2,1)}, u32[]{:S(2)}) copy-start(bf16[3,256,512]{2,1,0:T(8,128)(2,1)} %copy-done.13) | copy-start | bytes 2359300
  312.2 22.1 %collective-permute-start.27 = (bf16[3,128,512]{2,1,0:T(8,128)(2,1)S(1)}, bf16[3,128,512]{2,1,0:T(8,128)(2,1)S(1)}, u32[]{:S(2)}, u32[]{:S(2)}) collective-permute-start(bf16[3,128,512]{2,1,0:T(8,128)(2,1)S(1)} %get-tuple-element.66), channel_id=1, source_target_pairs={{0,1},{1,0},{2,3},{3,2},{4,5},{5,4},{6,7},{7,6},{8,9},{9,8},{10,11... | collective-permute-start | bytes 1179656 | tf_op jit(solution)/shard_map/ppermute | solution.py:26
  322.2 7.9 %copy-start.16 = (bf16[3,256,512]{2,1,0:T(8,128)(2,1)S(1)}, bf16[3,256,512]{2,1,0:T(8,128)(2,1)}, u32[]{:S(2)}) copy-start(bf16[3,256,512]{2,1,0:T(8,128)(2,1)} %copy-done.15) | copy-start | bytes 2359300
  330.0 9.1 %collective-permute-start.25 = (bf16[3,128,512]{2,1,0:T(8,128)(2,1)S(1)}, bf16[3,128,512]{2,1,0:T(8,128)(2,1)S(1)}, u32[]{:S(2)}, u32[]{:S(2)}) collective-permute-start(bf16[3,128,512]{2,1,0:T(8,128)(2,1)S(1)} %get-tuple-element.63), channel_id=1, source_target_pairs={{0,1},{1,0},{2,3},{3,2},{4,5},{5,4},{6,7},{7,6},{8,9},{9,8},{10,11... | collective-permute-start | bytes 1179656 | tf_op jit(solution)/shard_map/ppermute | solution.py:26
  330.1 18.3 %copy-start.17 = (s32[8]{0:T(128)S(1)}, s32[8]{0:T(128)}, u32[]{:S(2)}) copy-start(s32[8]{0:T(128)} %order.1) | copy-start | bytes 100
  340.7 4.2 %collective-permute-start.30 = (f32[16,8,128]{2,1,0:T(8,128)S(1)}, f32[16,8,128]{2,1,0:T(8,128)S(1)}, u32[]{:S(2)}, u32[]{:S(2)}) collective-permute-start(f32[16,8,128]{2,1,0:T(8,128)S(1)} %get-tuple-element.71.refs_0_), channel_id=1, source_target_pairs={{0,8},{8,0},{16,24},{24,16},{1,9},{9,1},{17,25},{25,17},{2,10},{10... | collective-permute-start | bytes 196616 | tf_op jit(solution)/shard_map/ppermute | solution.py:26
  343.2 3.7 %collective-permute-start.31 = (f32[16,8,128]{2,1,0:T(8,128)S(1)}, f32[16,8,128]{2,1,0:T(8,128)S(1)}, u32[]{:S(2)}, u32[]{:S(2)}) collective-permute-start(f32[16,8,128]{2,1,0:T(8,128)S(1)} %get-tuple-element.71.refs_0_), channel_id=1, source_target_pairs={{0,16},{8,24},{16,0},{24,8},{1,17},{9,25},{17,1},{25,9},{2,18},{10... | collective-permute-start | bytes 196616 | tf_op jit(solution)/shard_map/ppermute | solution.py:26
  344.1 4.3 %collective-permute-start.32 = (f32[16,8,128]{2,1,0:T(8,128)S(1)}, f32[16,8,128]{2,1,0:T(8,128)S(1)}, u32[]{:S(2)}, u32[]{:S(2)}) collective-permute-start(f32[16,8,128]{2,1,0:T(8,128)S(1)} %get-tuple-element.71.refs_0_), channel_id=1, source_target_pairs={{0,24},{8,16},{16,8},{24,0},{1,25},{9,17},{17,9},{25,1},{2,26},{10... | collective-permute-start | bytes 196616 | tf_op jit(solution)/shard_map/ppermute | solution.py:26
  (14 other events, 16.9 us)

commit v3 on v2

--- a/solution.py
+++ b/solution.py
@@ -11,8 +11,9 @@
 MIB = 1 << 20
 DEPTH = 512
 CHUNKS = (256, 256, 256, 128, 128)
-HALVES = (1024,)
-FAR = (1024,)
+PASSED = (1024,)
+T = {'y_y': True, 'y3_c0': True, 'y2_A': False, 'x_x': [0, 1, 1, 1], 'x_c': [0, 0, 1, 1], 'Ka': 'c3', 'x2_A': False, 'c_A': 9, 'c_P': [3], 'x_P': [], 'c_ser': [1, 0, 0, 1], 'copy': None, 'E': {2: 0, 3: 1, 4: 2}, 'S': {3: 0, 4: 1}}
+FREE = pl.CostEstimate(flops=0, bytes_accessed=0, transcendentals=0)
 
 
 class Plan(NamedTuple):
@@ -34,49 +35,54 @@
     return residue * jnp.sqrt(jnp.maximum(-jnp.expm1(-2.0 * rate), 1.0 / length))
 
 
-def project_kernel(plan, n_inputs, has_init, final, blocks, x_plan, place, *refs):
+def fetch_weights(plan, place, block, own, pieces, stride, target, sem):
+    pair, ctx = place[0], place[1]
+    local = lax.rem(block, plan.half_blocks)
+    here = lax.div(block, plan.half_blocks) == pair
+
+    @pl.when(here)
+    def _():
+        row = pl.multiple_of(local * DEPTH, DEPTH)
+        pltpu.make_async_copy(own.at[:, pl.ds(row, DEPTH), :], target, sem).start()
+
+    number = jnp.bitwise_xor(lax.div(local, plan.part_blocks), ctx)
+    if stride == 1:
+        number = number * plan.part_blocks + lax.rem(local, plan.part_blocks)
+    for n in range(len(pieces) // 2):
+        @pl.when(jnp.logical_not(here) & (number == n))
+        def _():
+            for side in (0, 1):
+                rows = pl.ds(side * (DEPTH // 2), DEPTH // 2)
+                pltpu.make_async_copy(pieces[2 * n + side], target.at[:, rows, :], sem).start()
+
+
+def project_kernel(plan, n_inputs, stride, base, final, blocks, x_plan, place, *refs):
     refs = list(refs)
     inputs = [refs.pop(0) for _ in range(n_inputs)]
     own = refs.pop(0)
-    pieces = [refs.pop(0) for _ in range(plan.n_pieces)]
-    init = refs.pop(0) if has_init else None
+    pieces = [refs.pop(0) for _ in range(plan.n_pieces // stride)]
+    init = refs.pop(0) if base is not None else None
     outs = [refs.pop(0) for _ in range(2 if final else 1)]
-    x_buf, w_buf, x_sem, w_sem = refs[:4]
-    acc = refs[4] if final else outs[0]
-    pair, ctx, tp = place[0], place[1], place[2]
+    x_buf, w_buf, x_sem, w_sem, acc_sem = refs[:5]
+    acc = refs[5] if final else outs[0]
+    pair, tp = place[0], place[2]
     slots = x_buf.shape[0]
 
     def start(step):
         slot = lax.rem(step, slots)
         block = x_plan(tp, step, inputs, x_buf.at[slot], x_sem.at[slot])
-        local = lax.rem(block, plan.half_blocks)
-        here = lax.div(block, plan.half_blocks) == pair
-
-        @pl.when(here)
-        def _():
-            row = pl.multiple_of(local * DEPTH, DEPTH)
-            pltpu.make_async_copy(
-                own.at[:, pl.ds(row, DEPTH), :], w_buf.at[slot], w_sem.at[slot]
-            ).start()
-
-        part = lax.div(local, plan.part_blocks)
-        number = jnp.bitwise_xor(part, ctx) * plan.part_blocks + lax.rem(local, plan.part_blocks)
-        for n in range(len(pieces) // 2):
-            @pl.when(jnp.logical_not(here) & (number == n))
-            def _():
-                for side in (0, 1):
-                    pltpu.make_async_copy(
-                        pieces[2 * n + side],
-                        w_buf.at[slot, :, pl.ds(side * (DEPTH // 2), DEPTH // 2), :],
-                        w_sem.at[slot],
-                    ).start()
-
+        fetch_weights(
+            plan, place, block, own, pieces, stride, w_buf.at[slot], w_sem.at[slot]
+        )
+
+    if init is not None:
+        pltpu.make_async_copy(init.at[:, pl.ds(base, acc.shape[1]), :], acc, acc_sem).start()
     for ahead in range(min(slots - 1, blocks)):
         start(jnp.int32(ahead))
-    if has_init:
-        acc[...] = init[...]
+    if init is None:
+        acc[...] = jnp.zeros_like(acc)
     else:
-        acc[...] = jnp.zeros_like(acc)
+        pltpu.make_async_copy(acc, acc, acc_sem).wait()
 
     def body(step, carry):
         slot = lax.rem(step, slots)
@@ -93,58 +99,51 @@
         return carry
 
     lax.fori_loop(0, blocks, body, 0)
-    if final:
-        kept, given = outs
-        half = kept.shape[2]
-        mine = pl.multiple_of(pair * half, 128)
-        other = pl.multiple_of((1 - pair) * half, 128)
-        for p in range(3):
-            kept[p] = acc[p, :, pl.ds(mine, half)].astype(jnp.bfloat16)
-            given[p] = acc[p, :, pl.ds(other, half)].astype(jnp.bfloat16)
-
-
-def project(plan, place, inputs, own, pieces, init, base, rows, blocks, x_plan, final):
+    if not final:
+        return
+    kept, given = outs
+    half = kept.shape[2]
+    mine = pl.multiple_of(pair * half, 128)
+    other = pl.multiple_of((1 - pair) * half, 128)
+    for p in range(3):
+        kept[p] = acc[p, :, pl.ds(mine, half)].astype(jnp.bfloat16)
+        given[p] = acc[p, :, pl.ds(other, half)].astype(jnp.bfloat16)
+
+
+def project(plan, place, inputs, own, pieces, stride, init, base, rows, blocks, x_plan, final):
     width = own.shape[2]
-    slots = 3
+    slots = 4 if final else 3
     anywhere = pl.BlockSpec(memory_space=pl.ANY)
     local = pl.BlockSpec(memory_space=pltpu.VMEM)
-    operands = list(inputs) + [own] + list(pieces)
-    in_specs = [anywhere] * len(operands)
-    if init is not None:
-        operands.append(init)
-        in_specs.append(pl.BlockSpec((3, rows, width), lambda i, place: (0, base // rows, 0)))
+    operands = list(inputs) + [own] + list(pieces) + ([] if init is None else [init])
+    total = (3, rows, width)
     scratch = [
         pltpu.VMEM((slots, rows, DEPTH), jnp.bfloat16),
         pltpu.VMEM((slots, 3, DEPTH, width), jnp.bfloat16),
         pltpu.SemaphoreType.DMA((slots,)),
         pltpu.SemaphoreType.DMA((slots,)),
+        pltpu.SemaphoreType.DMA,
     ]
+    out_shape = jax.ShapeDtypeStruct(total, jnp.float32)
     if final:
-        scratch.append(pltpu.VMEM((3, rows, width), jnp.float32))
+        scratch.append(pltpu.VMEM(total, jnp.float32))
         out_shape = [jax.ShapeDtypeStruct((3, rows, width // 2), jnp.bfloat16)] * 2
-        out_specs = [local, local]
-    else:
-        out_shape = jax.ShapeDtypeStruct((3, rows, width), jnp.float32)
-        out_specs = local
     return pl.pallas_call(
         functools.partial(
-            project_kernel, plan, len(inputs), init is not None, final, blocks, x_plan
+            project_kernel, plan, len(inputs), stride, None if init is None else base, final,
+            blocks, x_plan,
         ),
         grid_spec=pltpu.PrefetchScalarGridSpec(
             num_scalar_prefetch=1,
-            grid=(1,),
-            in_specs=in_specs,
-            out_specs=out_specs,
+            grid=(),
+            in_specs=[anywhere] * len(operands),
+            out_specs=[local, local] if final else local,
             scratch_shapes=scratch,
         ),
         out_shape=out_shape,
-        compiler_params=pltpu.CompilerParams(vmem_limit_bytes=44 * MIB),
-        cost_estimate=pl.CostEstimate(
-            flops=0,
-            bytes_accessed=0,
-            transcendentals=0,
-        ),
-        name="project",
+        compiler_params=pltpu.CompilerParams(vmem_limit_bytes=30 * MIB),
+        cost_estimate=FREE,
+        name="project" if final else "project_part",
     )(place, *operands)
 
 
@@ -165,42 +164,63 @@
     return (tp == 0) | (tp == 3)
 
 
-def first_plan(per_quarter, n_halves):
-    def plan(tp, step, inputs, target, sem):
-        own, near, *rest = inputs
-        middle, ends = rest[:n_halves], rest[n_halves:]
-        high = lax.div(tp, 2)
-        early = step < 2 * per_quarter
-        block = jnp.where(
-            early,
-            high * 2 * per_quarter + step,
-            (2 - high) * per_quarter + step - 2 * per_quarter,
-        )
-        quarter = lax.div(block, per_quarter)
-        where = columns(lax.rem(block, per_quarter))
-
-        @pl.when(early & (quarter == tp))
-        def _():
-            pltpu.make_async_copy(own.at[:, where], target, sem).start()
-
-        @pl.when(early & (quarter != tp))
-        def _():
-            pltpu.make_async_copy(near.at[:, where], target, sem).start()
-
-        for at_end, sources in ((False, middle), (True, ends)):
-            @pl.when(jnp.logical_not(early) & (line_ends(tp) == at_end))
-            def _():
-                row = 0
-                for source in sources:
-                    size = source.shape[0]
-                    pltpu.make_async_copy(
-                        source.at[:, where], target.at[pl.ds(row, size), :], sem
-                    ).start()
-                    row += size
-
-        return block
-
-    return plan
+def near_block(plan, tp, step, number, base, inputs, target, sem):
+    span = plan.half_blocks // 2 // plan.part_blocks
+    mine = step < span
+    side = jnp.where(mine, lax.rem(tp, 2), 1 - lax.rem(tp, 2))
+    within = lax.rem(step, span)
+    where = columns(within * plan.part_blocks + number)
+    for at, source in ((True, inputs[0]), (False, inputs[1])):
+        @pl.when(mine == at)
+        def _():
+            rows = pl.ds(base, target.shape[0])
+            pltpu.make_async_copy(source.at[rows, where], target, sem).start()
+
+    part = side * span + within
+    return lax.div(tp, 2) * plan.half_blocks + part * plan.part_blocks + number
+
+
+def near_plan(plan, number, base):
+    def x_plan(tp, step, inputs, target, sem):
+        return near_block(plan, tp, step, number, base, inputs, target, sem)
+
+    return x_plan
+
+
+def middle_plan(plan, number, base, segments):
+    span = plan.half_blocks // plan.part_blocks
+    per_quarter = plan.half_blocks // 2
+
+    def x_plan(tp, step, inputs, target, sem):
+        middle, ends = inputs[2], inputs[3:]
+        late = step - span
+        where = columns(jnp.maximum(late, 0))
+
+        @pl.when(step < span)
+        def _():
+            near_block(plan, tp, step, number, base, inputs, target, sem)
+
+        @pl.when((late >= 0) & jnp.logical_not(line_ends(tp)))
+        def _():
+            rows = pl.ds(base, target.shape[0])
+            pltpu.make_async_copy(middle.at[rows, where], target, sem).start()
+
+        @pl.when((late >= 0) & line_ends(tp))
+        def _():
+            row = 0
+            for source, (first, size) in zip(ends, segments):
+                pltpu.make_async_copy(
+                    source.at[pl.ds(first, size), where], target.at[pl.ds(row, size), :], sem
+                ).start()
+                row += size
+
+        half = span // 2
+        side = jnp.where(step < half, lax.rem(tp, 2), 1 - lax.rem(tp, 2))
+        part = side * half + lax.rem(step, half)
+        near = lax.div(tp, 2) * plan.half_blocks + part * plan.part_blocks + number
+        return jnp.where(late < 0, near, (2 - lax.div(tp, 2)) * per_quarter + late)
+
+    return x_plan
 
 
 def last_plan(per_quarter, row, rows):
@@ -263,11 +283,7 @@
         ],
         scratch_shapes=[pltpu.VMEM((rows,) + lanes, jnp.float32)],
         compiler_params=pltpu.CompilerParams(vmem_limit_bytes=24 * MIB),
-        cost_estimate=pl.CostEstimate(
-            flops=0,
-            bytes_accessed=0,
-            transcendentals=0,
-        ),
+        cost_estimate=FREE,
         name="scan",
     )(kept, given, decay, gain, skip, state)
 
@@ -363,28 +379,38 @@
     place = jnp.stack([pair_index, ctx_index, lax.axis_index("tp")]).astype(jnp.int32)
 
     starts = [sum(CHUNKS[:k]) for k in range(len(CHUNKS))]
-    on_line = lax.axis_size("tp") == 4
-    passed, arrived = [], []
+    on_line = lax.axis_size("tp") == 4 and n_ctx == 4
+    passed = []
     if on_line:
         near = lax.ppermute(tokens, "tp", [(0, 1), (1, 0), (2, 3), (3, 2)])
-        middle, ends, row = [], [], 0
-        for rows in HALVES:
-            block = lax.slice_in_dim(tokens, row, row + rows, axis=0)
-            middle.append(lax.ppermute(block, "tp", [(1, 2), (2, 1)]))
-            ends.append(lax.ppermute(middle[-1], "tp", [(1, 0), (2, 3)]))
+        middle = lax.ppermute(tokens, "tp", [(1, 2), (2, 1)])
+        ends, far_middle, row = [], [], 0
+        for rows in PASSED:
+            if T["copy"] is None:
+                block = lax.slice_in_dim(middle, row, row + rows, axis=0)
+                far = lax.slice_in_dim(near, row, row + rows, axis=0)
+            else:
+                block, far = take_rows(row, rows, middle, near)
+            ends.append(lax.ppermute(block, "tp", [(1, 0), (2, 3)]))
+            far_middle.append(lax.ppermute(far, "tp", [(1, 2), (2, 1)]))
             row += rows
-        far_middle, row = [], 0
-        for rows in FAR:
-            block = lax.slice_in_dim(near, row, row + rows, axis=0)
-            far_middle.append(lax.ppermute(block, "tp", [(1, 2), (2, 1)]))
-            row += rows
-        passed = ends + far_middle
-        arrived = [near] + middle
+        passed = [ends[0], far_middle[0]]
 
     own = weight.transpose(1, 0, 2)
     part = own.shape[1] // n_ctx
     piece_len = DEPTH // 2
     per_part = part // piece_len
+    plan = Plan(own.shape[1] // DEPTH, part // DEPTH, n_ctx * per_part)
+    per_quarter = tokens.shape[1] // DEPTH
+    partials = [None]
+
+    def add_part():
+        some = [pieces[m, n] for m in range(n_ctx) for n in (0, 1)]
+        return project(
+            plan, place, [tokens, near], own, some, plan.part_blocks, None, 0, seg_len,
+            plan.half_blocks // plan.part_blocks, near_plan(plan, 0, 0), False,
+        )
+
     pieces = {}
     bits = []
     while 1 << len(bits) < n_ctx:
@@ -392,30 +418,43 @@
     first = []
     for sub in range(per_part):
         piece = lax.dynamic_slice_in_dim(own, ctx_index * part + sub * piece_len, piece_len, 1)
-        if sub >= 2:
+        if sub >= 2 and T["y_y"]:
             piece = after(piece, first[sub - 2])
-        if sub >= 3:
-            piece = after(piece, *[pieces[m, sub - 3] for m in range(n_ctx)])
+        if sub == 3 and T["y3_c0"]:
+            piece = after(piece, *[pieces[m, 0] for m in range(n_ctx)])
+        if sub == 2 and T["y2_A"] and on_line:
+            piece = after(piece, near, middle)
         first.append(exchanged(piece, "fsdp", 1))
         held = {0: first[sub]}
         for bit in bits:
             for mask in list(held):
                 block = held[mask]
-                if bit == bits[0] and sub:
+                if bit == bits[0] and sub and T["x_x"][sub]:
                     block = after(block, pieces[bit, sub - 1])
-                if bit == bits[0] and sub >= 2:
+                if bit == bits[0] and sub >= 2 and T["x_c"][sub]:
                     block = after(block, *[pieces[m, sub - 2] for m in range(n_ctx)])
-                if bit == bits[-1] and sub == per_part - 1:
-                    block = after(block, *passed)
-                if bit == bits[-1] and mask and sub in (0, per_part - 1):
+                if on_line:
+                    if bit == bits[0] and sub == 3 and T["Ka"] == "x3":
+                        block = after(block, partials[1])
+                    if bit == bits[-1] and T["Ka"] == "c%d" % sub:
+                        block = after(block, partials[1])
+                    if bit == bits[0] and sub == 2 and T["x2_A"]:
+                        block = after(block, near, middle)
+                    if bit == bits[-1] and T["c_A"] == sub:
+                        block = after(block, near, middle)
+                    if bit == bits[-1] and sub in T["c_P"]:
+                        block = after(block, *passed)
+                    if bit == bits[0] and sub in T["x_P"]:
+                        block = after(block, *passed)
+                if bit == bits[-1] and mask and T["c_ser"][sub]:
                     block = after(block, latest)
                 latest = exchanged(block, "ctx", bit)
                 held[mask | bit] = latest
         for mask in range(n_ctx):
             pieces[mask, sub] = held[mask]
+        if sub == 1 and on_line:
+            partials.append(add_part())
     ordered = [pieces[mask, sub] for mask in range(n_ctx) for sub in range(per_part)]
-    plan = Plan(own.shape[1] // DEPTH, part // DEPTH, len(ordered))
-    per_quarter = tokens.shape[1] // DEPTH
 
     channels = rate.shape[0]
     groups = channels // 128
@@ -433,40 +472,46 @@
         far_ends, where = [], []
         for k, (base, rows) in enumerate(zip(starts, CHUNKS)):
             row, n = base, 0
-            while row >= FAR[n]:
-                row -= FAR[n]
+            while row >= PASSED[n]:
+                row -= PASSED[n]
                 n += 1
             where.append((n, row))
             block = lax.slice_in_dim(far_middle[n], row, row + rows, axis=0)
-            if k >= 3:
-                block = after(block, far_ends[k - 3])
+            if k in T["E"]:
+                block = after(block, far_ends[T["E"][k]])
             far_ends.append(lax.ppermute(block, "tp", [(1, 0), (2, 3)]))
-        near = after(near, *far_middle)
-        partial = project(
-            plan, place, [tokens, near, *middle, *ends], own, ordered, None, 0, seg_len,
-            3 * per_quarter, first_plan(per_quarter, len(HALVES)), False,
-        )
-    else:
-        partial = None
+        segments = {1024: (((0, 512),), ((512, 512),)), 768: (((0, 512),), ((512, 256), (0, 256)))}[PASSED[0]]
+        halves = []
+
+        def add_half(h):
+            sources = [tokens, near, middle] + ends[: len(segments[h])]
+            return project(
+                plan, place, sources, own, ordered, 1, partials[-1], h * 512, 512,
+                plan.half_blocks // plan.part_blocks + plan.half_blocks // 2,
+                middle_plan(plan, 1, h * 512, segments[h]), False,
+            )
+
 
     kept, given, locals_ = [], [], []
     state = jnp.zeros_like(decay)
     states = []
     for k, (base, rows) in enumerate(zip(starts, CHUNKS)):
-        if partial is not None:
+        if on_line:
             last = far_ends[k]
-            if k == len(CHUNKS) - 1:
-                last = after(last, states[k - 3])
+            if base % 512 == 0:
+                halves.append(add_half(base // 512))
+            if k in T["S"]:
+                last = after(last, states[T["S"][k]])
             n, row = where[k]
             keep, give = project(
-                plan, place, [far_middle[n], last], own, ordered, partial, base, rows,
+                plan, place, [far_middle[n], last], own, ordered, 1, halves[-1], base % 512, rows,
                 per_quarter, last_plan(per_quarter, row, rows), True,
             )
         else:
             block = lax.slice_in_dim(tokens, base, base + rows, axis=0)
             whole = lax.all_gather(block, "tp", axis=0, tiled=False)
             keep, give = project(
-                plan, place, [whole], own, ordered, None, 0, rows,
+                plan, place, [whole], own, ordered, 1, None, 0, rows,
                 2 * plan.half_blocks, gathered_plan(per_quarter), True,
             )
         got = exchanged(give, "fsdp", 1)

time: 361 us -> 374 us (1.036)
  waiting for transfers between devices: 155 us -> 144 us
  local copies, waits for them, and re-layouts: 26.1 us -> 36.4 us
  Pallas kernels: 122 us -> 132 us
    ppermute x3, waiting for transfers between devices: 32.2 us -> 9.97 us  [the longest x1 8.86 us: per_device(): far_middle.append(lax.ppermute(far, 'tp', [(1, 2), (2, 1)]))]
    pallas_call x6 -> x8, Pallas kernels: 94.5 us -> 104 us  [project(): pl.pallas_call(functools.partial(project_kernel, plan, len(inputs), strid...]
    unnamed x58 -> x78, local copies, waits for them, and re-layouts: 18.4 us -> 27.1 us
    ppermute x24, waiting for transfers between devices: 114 us -> 122 us  [exchanged(): return lax.ppermute(block, axis, [(i, i ^ mask) for i in range(count)])]
    ppermute x5, waiting for transfers between devices: 0.01 us -> 3.84 us  [per_device(): far_ends.append(lax.ppermute(block, 'tp', [(1, 0), (2, 3)]))]
  transfers between devices with their start and end apart: 33 -> 33, of which waited for: 13 -> 14; matrix products, arithmetic and copies ran while one was open for 2% -> 3% of each run, Pallas kernels for 30% -> 32%
where the time goes in v3:
time: 374 us; the launch traced here: 370 us
  waiting for transfers between devices  144 us (39%)
  Pallas kernels  132 us (35%)
  starting transfers between devices  57.3 us (15%)
  local copies, waits for them, and re-layouts  36.4 us (10%)
    ppermute x24, waiting for transfers between devices, exchanged(): return lax.ppermute(block, axis, [(i, i ^ mask) for i in range(count)])  122 us
    pallas_call x8, Pallas kernels, project(): pl.pallas_call(functools.partial(project_kernel, plan, len(inputs), strid...  104 us
    ppermute x24, starting transfers between devices, exchanged(): return lax.ppermute(block, axis, [(i, i ^ mask) for i in range(count)])  32.1 us
    unnamed x78, local copies, waits for them, and re-layouts  27.1 us
    pallas_call x5, Pallas kernels, scan(): pl.pallas_call(scan_kernel, in_specs=[local] * 6, out_specs=[local] * 2,...  16.1 us
    ppermute x5, starting transfers between devices, per_device(): far_ends.append(lax.ppermute(block, 'tp', [(1, 0), (2, 3)]))  13.9 us
    pallas_call x1, Pallas kernels, finish(): pl.pallas_call(functools.partial(finish_kernel, len(ends), n_chunks, seg_...  11.6 us
    ppermute x1, waiting for transfers between devices, per_device(): far_middle.append(lax.ppermute(far, 'tp', [(1, 2), (2, 1)]))  8.86 us
  transfers between devices with their start and end apart: 33, of which 14 were waited for; matrix products, arithmetic and copies ran while one was open for 3% of the time, Pallas kernels for 32%

profile of v3, /device:TPU:9, one launch (start us, length us, event | category | flops | bytes accessed | tf_op | source)
XLA Modules:
  0.0 370.4 jit_solution(8054006067801262714)
XLA Ops:
  0.0 4.5 %collective-permute-start.17 = (bf16[1024,2048]{1,0:T(8,128)(2,1)}, bf16[1024,2048]{1,0:T(8,128)(2,1)}, u32[]{:S(2)}, u32[]{:S(2)}) collective-permute-start(bf16[1024,2048]{1,0:T(8,128)(2,1)} %refs_0_.5), channel_id=1, source_target_pairs={{2,4},{4,2},{3,5},{5,3},{10,12},{12,10},{11,13},{13,11},{18,20},{2... | collective-permute-start | bytes 12582920 | tf_op jit(solution)/shard_map/ppermute | solution.py:386
  4.5 4.8 %dynamic-slice_bitcast_fusion = (bf16[3,256,1024]{2,1,0:T(8,128)(2,1)}, bf16[3,256,1024]{2,1,0:T(8,128)(2,1)S(1)}, bf16[3,256,1024]{2,1,0:T(8,128)(2,1)S(1)}, bf16[3,256,1024]{2,1,0:T(8,128)(2,1)S(1)}) fusion(bf16[4096,3,1024]{2,0,1:T(8,128)(2,1)} %param.7, s32[]{:T(128)S(6)} %select_n.15, s32[]{:T(128)S(6)} %select_n.13, s32[]{:T(128)S(6)} %select_n.12, ...), kind=kLoop, calls=%fused_computation | loop fusion | bytes 12582928 | tf_op jit(solution)/shard_map/dynamic_slice | solution.py:420
  10.5 33.5 %collective-permute-done.6.refs_3_.refs_5_ = bf16[3,256,1024]{2,1,0:T(8,128)(2,1)S(1)} collective-permute-done((bf16[3,256,1024]{2,1,0:T(8,128)(2,1)S(1)}, bf16[3,256,1024]{2,1,0:T(8,128)(2,1)S(1)}, u32[]{:S(2)}, u32[]{:S(2)}) %collective-permute-start.6) | collective-permute-done | bytes 1572896 | tf_op jit(solution)/shard_map/ppermute | solution.py:27
  44.0 2.1 collective-permute-start.9
  49.1 33.1 %collective-permute-done.10.refs_7_.refs_13_.refs_11_ = bf16[3,256,1024]{2,1,0:T(8,128)(2,1)S(1)} collective-permute-done((bf16[3,256,1024]{2,1,0:T(8,128)(2,1)S(1)}, bf16[3,256,1024]{2,1,0:T(8,128)(2,1)S(1)}, u32[]{:S(2)}, u32[]{:S(2)}) %collective-permute-start.10) | collective-permute-done | bytes 1572896 | tf_op jit(solution)/shard_map/ppermute | solution.py:27
  84.0 7.7 %collective-permute-done.refs_1_ = bf16[1024,2048]{1,0:T(8,128)(2,1)} collective-permute-done((bf16[1024,2048]{1,0:T(8,128)(2,1)}, bf16[1024,2048]{1,0:T(8,128)(2,1)}, u32[]{:S(2)}, u32[]{:S(2)}) %collective-permute-start) | collective-permute-done | bytes 4194336 | tf_op jit(solution)/shard_map/ppermute | solution.py:385
  91.8 3.2 collective-permute-start.1
  95.0 3.6 collective-permute-start.18
  102.1 2.4 collective-permute-start.13
  105.6 27.5 %collective-permute-done.8.refs_7_.refs_5_ = bf16[3,256,1024]{2,1,0:T(8,128)(2,1)} collective-permute-done((bf16[3,256,1024]{2,1,0:T(8,128)(2,1)S(1)}, bf16[3,256,1024]{2,1,0:T(8,128)(2,1)}, u32[]{:S(2)}, u32[]{:S(2)}) %collective-permute-start.8) | collective-permute-done | bytes 1572896 | tf_op jit(solution)/shard_map/ppermute | solution.py:27
  133.9 3.0 collective-permute-start.16
  140.3 1.4 copy-done.1
  141.7 1.4 copy-done.5
  145.9 2.2 copy-done.25
  148.1 21.8 %project_part.3.refs_21_ = f32[3,1024,1024]{2,1,0:T(8,128)} custom-call(s32[3]{0:T(128)S(1)} %pad_add_fusion.place, bf16[1024,2048]{1,0:T(8,128)(2,1)S(1)} %copy-done.25, bf16[1024,2048]{1,0:T(8,128)(2,1)} %collective-permute-done.refs_1_, bf16[3,4096,1024]{2,1,0:T(8,128)(2,1)} %bitcast.18, bf16[3,256,1024]{2,1,0:T(8,128)(2,1)S(1)} %collective-permute-done.6.refs_3_.refs_5_, ...), custom_call_target="tpu_custom_call" | custom-call | tf_op jit(solution)/shard_map/project_part/pallas_call | solution.py:131
  170.0 4.4 %collective-permute-done.20.refs_15_.refs_13_ = bf16[3,256,1024]{2,1,0:T(8,128)(2,1)} collective-permute-done((bf16[3,256,1024]{2,1,0:T(8,128)(2,1)}, bf16[3,256,1024]{2,1,0:T(8,128)(2,1)}, u32[]{:S(2)}, u32[]{:S(2)}) %collective-permute-start.20) | collective-permute-done | bytes 1572896 | tf_op jit(solution)/shard_map/ppermute | solution.py:27
  175.6 8.9 %collective-permute-done.1.refs_0_ = bf16[1024,2048]{1,0:T(8,128)(2,1)} collective-permute-done((bf16[1024,2048]{1,0:T(8,128)(2,1)}, bf16[1024,2048]{1,0:T(8,128)(2,1)}, u32[]{:S(2)}, u32[]{:S(2)}) %collective-permute-start.1) | collective-permute-done | bytes 4194336 | tf_op jit(solution)/shard_map/ppermute | solution.py:395
  185.6 2.1 collective-permute-start.19
  187.7 2.3 fusion.1
  190.0 4.2 %collective-permute-start.2 = (bf16[256,2048]{1,0:T(8,128)(2,1)S(1)}, bf16[256,2048]{1,0:T(8,128)(2,1)S(1)}, u32[]{:S(2)}, u32[]{:S(2)}) collective-permute-start(bf16[256,2048]{1,0:T(8,128)(2,1)S(1)} %get-tuple-element.90), channel_id=1, source_target_pairs={{2,0},{4,6},{3,1},{5,7},{10,8},{12,14},{11,9},{13,15},{18,16},{20,... | collective-permute-start | bytes 3145736 | tf_op jit(solution)/shard_map/ppermute | solution.py:482
  194.8 15.0 %collective-permute-done.21.refs_16_.refs_14_ = bf16[3,256,1024]{2,1,0:T(8,128)(2,1)S(1)} collective-permute-done((bf16[3,256,1024]{2,1,0:T(8,128)(2,1)}, bf16[3,256,1024]{2,1,0:T(8,128)(2,1)S(1)}, u32[]{:S(2)}, u32[]{:S(2)}) %collective-permute-start.21) | collective-permute-done | bytes 1572896 | tf_op jit(solution)/shard_map/ppermute | solution.py:27
  209.8 1.7 collective-permute-start.23
  212.8 3.8 %collective-permute-done.2.refs_1_ = bf16[256,2048]{1,0:T(8,128)(2,1)S(1)} collective-permute-done((bf16[256,2048]{1,0:T(8,128)(2,1)S(1)}, bf16[256,2048]{1,0:T(8,128)(2,1)S(1)}, u32[]{:S(2)}, u32[]{:S(2)}) %collective-permute-start.2) | collective-permute-done | bytes 1048608 | tf_op jit(solution)/shard_map/ppermute | solution.py:482
  216.7 4.2 %collective-permute-start.3 = (bf16[256,2048]{1,0:T(8,128)(2,1)S(1)}, bf16[256,2048]{1,0:T(8,128)(2,1)S(1)}, u32[]{:S(2)}, u32[]{:S(2)}) collective-permute-start(bf16[256,2048]{1,0:T(8,128)(2,1)S(1)} %get-tuple-element.44), channel_id=1, source_target_pairs={{2,0},{4,6},{3,1},{5,7},{10,8},{12,14},{11,9},{13,15},{18,16},{20,... | collective-permute-start | bytes 3145736 | tf_op jit(solution)/shard_map/ppermute | solution.py:482
  222.1 23.4 %project_part.4.refs_19_ = f32[3,512,1024]{2,1,0:T(8,128)} custom-call(s32[3]{0:T(128)S(1)} %pad_add_fusion.place, bf16[1024,2048]{1,0:T(8,128)(2,1)} %refs_0_.5, bf16[1024,2048]{1,0:T(8,128)(2,1)} %collective-permute-done.refs_1_, bf16[1024,2048]{1,0:T(8,128)(2,1)} %collective-permute-done.17.refs_2_, bf16[1024,2048]{1,0:T(8,128)(2,1)} %collective-permute-done.18.refs_3_, ...), custom_call_target="tpu_custom_call" | custom-call | tf_op jit(solution)/shard_map/project_part/pallas_call | solution.py:131
  245.6 8.4 %project.5 = (bf16[3,256,512]{2,1,0:T(8,128)(2,1)S(1)}, bf16[3,256,512]{2,1,0:T(8,128)(2,1)}) custom-call(s32[3]{0:T(128)S(1)} %pad_add_fusion.place, bf16[1024,2048]{1,0:T(8,128)(2,1)} %collective-permute-done.1.refs_0_, bf16[256,2048]{1,0:T(8,128)(2,1)S(1)} %collective-permute-done.5.refs_1_, bf16[3,4096,1024]{2,1,0:T(8,128)(2,1)} %bitcast.20, ...), custom_call_target="tpu_custom_call" | custom-call | tf_op jit(solution)/shard_map/project/pallas_call | solution.py:131
  255.1 8.4 %project.6 = (bf16[3,256,512]{2,1,0:T(8,128)(2,1)S(1)}, bf16[3,256,512]{2,1,0:T(8,128)(2,1)}) custom-call(s32[3]{0:T(128)S(1)} %pad_add_fusion.place, bf16[1024,2048]{1,0:T(8,128)(2,1)} %collective-permute-done.1.refs_0_, bf16[256,2048]{1,0:T(8,128)(2,1)S(1)} %collective-permute-done.2.refs_1_, bf16[3,4096,1024]{2,1,0:T(8,128)(2,1)} %bitcast.21, ...), custom_call_target="tpu_custom_call" | custom-call | tf_op jit(solution)/shard_map/project/pallas_call | solution.py:131
  264.5 1.7 collective-permute-start.25
  266.1 2.3 fusion
  268.4 2.1 collective-permute-start.27
  270.5 2.1 collective-permute-start.4
  272.6 23.4 %project_part.5.refs_19_ = f32[3,512,1024]{2,1,0:T(8,128)} custom-call(s32[3]{0:T(128)S(1)} %pad_add_fusion.place, bf16[1024,2048]{1,0:T(8,128)(2,1)} %refs_0_.5, bf16[1024,2048]{1,0:T(8,128)(2,1)} %collective-permute-done.refs_1_, bf16[1024,2048]{1,0:T(8,128)(2,1)} %collective-permute-done.17.refs_2_, bf16[1024,2048]{1,0:T(8,128)(2,1)} %collective-permute-done.18.refs_3_, ...), custom_call_target="tpu_custom_call" | custom-call | tf_op jit(solution)/shard_map/project_part/pallas_call | solution.py:131
  296.1 8.4 %project.9 = (bf16[3,256,512]{2,1,0:T(8,128)(2,1)S(1)}, bf16[3,256,512]{2,1,0:T(8,128)(2,1)}) custom-call(s32[3]{0:T(128)S(1)} %pad_add_fusion.place, bf16[1024,2048]{1,0:T(8,128)(2,1)} %collective-permute-done.1.refs_0_, bf16[256,2048]{1,0:T(8,128)(2,1)S(1)} %collective-permute-done.3.refs_1_, bf16[3,4096,1024]{2,1,0:T(8,128)(2,1)} %bitcast.23, ...), custom_call_target="tpu_custom_call" | custom-call | tf_op jit(solution)/shard_map/project/pallas_call | solution.py:131
  306.8 4.4 %scan.5 = (f32[256,8,128]{2,1,0:T(8,128)S(1)}, f32[16,8,128]{2,1,0:T(8,128)S(1)}) custom-call(bf16[3,256,512]{2,1,0:T(8,128)(2,1)S(1)} %copy-done.30, bf16[3,256,512]{2,1,0:T(8,128)(2,1)} %collective-permute-done.25.given.refs_16_, f32[16,8,128]{2,1,0:T(8,128)S(1)} %get-tuple-element.93.decay.refs_5_, f32[16,8,128]{2,1,0:T(8,128)S(1)} %pad_maximum_fusion.1.gain, ...), custom_call_target="tpu_custom_call" | custom-call | tf_op jit(solution)/shard_map/scan/pallas_call | solution.py:276
  312.3 4.2 %scan.6 = (f32[256,8,128]{2,1,0:T(8,128)S(1)}, f32[16,8,128]{2,1,0:T(8,128)S(1)}) custom-call(bf16[3,256,512]{2,1,0:T(8,128)(2,1)S(1)} %copy-done.27, bf16[3,256,512]{2,1,0:T(8,128)(2,1)} %collective-permute-done.24.given.refs_17_, f32[16,8,128]{2,1,0:T(8,128)S(1)} %get-tuple-element.93.decay.refs_5_, f32[16,8,128]{2,1,0:T(8,128)S(1)} %pad_maximum_fusion.1.gain, ...), custom_call_target="tpu_custom_call" | custom-call | tf_op jit(solution)/shard_map/scan/pallas_call | solution.py:276
  325.1 5.2 %project.8 = (bf16[3,128,512]{2,1,0:T(8,128)(2,1)S(1)}, bf16[3,128,512]{2,1,0:T(8,128)(2,1)S(1)}) custom-call(s32[3]{0:T(128)S(1)} %pad_add_fusion.place, bf16[1024,2048]{1,0:T(8,128)(2,1)} %collective-permute-done.1.refs_0_, bf16[128,2048]{1,0:T(8,128)(2,1)} %collective-permute-done.27.refs_1_, bf16[3,4096,1024]{2,1,0:T(8,128)(2,1)} %bitcast.24, ...), custom_call_target="tpu_custom_call" | custom-call | tf_op jit(solution)/shard_map/project/pallas_call | solution.py:131
  330.3 3.1 collective-permute-start.28
  333.4 5.2 %project.7 = (bf16[3,128,512]{2,1,0:T(8,128)(2,1)S(1)}, bf16[3,128,512]{2,1,0:T(8,128)(2,1)S(1)}) custom-call(s32[3]{0:T(128)S(1)} %pad_add_fusion.place, bf16[1024,2048]{1,0:T(8,128)(2,1)} %collective-permute-done.1.refs_0_, bf16[128,2048]{1,0:T(8,128)(2,1)} %collective-permute-done.4.refs_1_, bf16[3,4096,1024]{2,1,0:T(8,128)(2,1)} %bitcast.25, ...), custom_call_target="tpu_custom_call" | custom-call | tf_op jit(solution)/shard_map/project/pallas_call | solution.py:131
  338.7 1.7 collective-permute-start.26
  340.4 4.4 %scan.7 = (f32[256,8,128]{2,1,0:T(8,128)S(1)}, f32[16,8,128]{2,1,0:T(8,128)S(1)}) custom-call(bf16[3,256,512]{2,1,0:T(8,128)(2,1)S(1)} %copy-done.33, bf16[3,256,512]{2,1,0:T(8,128)(2,1)} %collective-permute-done.29.given.refs_18_, f32[16,8,128]{2,1,0:T(8,128)S(1)} %get-tuple-element.93.decay.refs_5_, f32[16,8,128]{2,1,0:T(8,128)S(1)} %pad_maximum_fusion.1.gain, ...), custom_call_target="tpu_custom_call" | custom-call | tf_op jit(solution)/shard_map/scan/pallas_call | solution.py:276
  344.8 1.6 scan.8
  346.3 3.8 %collective-permute-done.26.given.refs_20_ = bf16[3,128,512]{2,1,0:T(8,128)(2,1)S(1)} collective-permute-done((bf16[3,128,512]{2,1,0:T(8,128)(2,1)S(1)}, bf16[3,128,512]{2,1,0:T(8,128)(2,1)S(1)}, u32[]{:S(2)}, u32[]{:S(2)}) %collective-permute-start.26) | collective-permute-done | bytes 393248 | tf_op jit(solution)/shard_map/ppermute | solution.py:27
  350.1 1.6 scan.9
  351.7 1.9 collective-permute-start.30
  353.5 1.7 collective-permute-start.32
  355.3 2.0 collective-permute-done.31.refs_2_
  357.2 1.6 collective-permute-done.32.refs_3_
  358.8 11.6 %finish.1 = bf16[512,2048]{1,0:T(8,128)(2,1)} custom-call(s32[3]{0:T(128)S(1)} %pad_add_fusion.place, s32[8]{0:T(128)S(1)} %copy-done.34, f32[16,8,128]{2,1,0:T(8,128)S(1)} %get-tuple-element.77.refs_0_, f32[16,8,128]{2,1,0:T(8,128)S(1)} %collective-permute-done.30.refs_1_, f32[16,8,128]{2,1,0:T(8,128)S(1)} %collective-permute-done.31.refs_2_, ...), custom_call_target="tpu_custom_call" | custom-call | flops 33554432 | bytes 8388608 | tf_op jit(solution)/shard_map/finish/pallas_call | solution.py:353
  (121 shorter events, 37.0 us)
Async XLA Ops:
  0.0 91.8 %collective-permute-start = (bf16[1024,2048]{1,0:T(8,128)(2,1)}, bf16[1024,2048]{1,0:T(8,128)(2,1)}, u32[]{:S(2)}, u32[]{:S(2)}) collective-permute-start(bf16[1024,2048]{1,0:T(8,128)(2,1)} %refs_0_.5), channel_id=1, source_target_pairs={{0,2},{2,0},{4,6},{6,4},{1,3},{3,1},{5,7},{7,5},{8,10},{10,8},{12,... | collective-permute-start | bytes 12582920 | tf_op jit(solution)/shard_map/ppermute | solution.py:385
  0.0 95.0 %collective-permute-start.17 = (bf16[1024,2048]{1,0:T(8,128)(2,1)}, bf16[1024,2048]{1,0:T(8,128)(2,1)}, u32[]{:S(2)}, u32[]{:S(2)}) collective-permute-start(bf16[1024,2048]{1,0:T(8,128)(2,1)} %refs_0_.5), channel_id=1, source_target_pairs={{2,4},{4,2},{3,5},{5,3},{10,12},{12,10},{11,13},{13,11},{18,20},{2... | collective-permute-start | bytes 12582920 | tf_op jit(solution)/shard_map/ppermute | solution.py:386
  9.3 34.8 %collective-permute-start.6 = (bf16[3,256,1024]{2,1,0:T(8,128)(2,1)S(1)}, bf16[3,256,1024]{2,1,0:T(8,128)(2,1)S(1)}, u32[]{:S(2)}, u32[]{:S(2)}) collective-permute-start(bf16[3,256,1024]{2,1,0:T(8,128)(2,1)S(1)} %get-tuple-element.85), channel_id=1, source_target_pairs={{0,1},{1,0},{2,3},{3,2},{4,5},{5,4},{6,7},{7,6},{8,9},{9,8},{10,11... | collective-permute-start | bytes 4718600 | tf_op jit(solution)/shard_map/ppermute | solution.py:27
  44.0 5.1 %collective-permute-start.9 = (bf16[3,256,1024]{2,1,0:T(8,128)(2,1)S(1)}, bf16[3,256,1024]{2,1,0:T(8,128)(2,1)S(1)}, u32[]{:S(2)}, u32[]{:S(2)}) collective-permute-start(bf16[3,256,1024]{2,1,0:T(8,128)(2,1)S(1)} %collective-permute-done.6.refs_3_.refs_5_), channel_id=1, source_target_pairs={{0,8},{8,0},{16,24},{24,16},{1,9},{9,1},{17,25},{25,17},{2,10},{10... | collective-permute-start | bytes 4718600 | tf_op jit(solution)/shard_map/ppermute | solution.py:27
  46.1 36.1 %collective-permute-start.10 = (bf16[3,256,1024]{2,1,0:T(8,128)(2,1)S(1)}, bf16[3,256,1024]{2,1,0:T(8,128)(2,1)S(1)}, u32[]{:S(2)}, u32[]{:S(2)}) collective-permute-start(bf16[3,256,1024]{2,1,0:T(8,128)(2,1)S(1)} %collective-permute-done.6.refs_3_.refs_5_), channel_id=1, source_target_pairs={{0,16},{8,24},{16,0},{24,8},{1,17},{9,25},{17,1},{25,9},{2,18},{10... | collective-permute-start | bytes 4718600 | tf_op jit(solution)/shard_map/ppermute | solution.py:27
  47.3 52.4 %collective-permute-start.7 = (bf16[3,256,1024]{2,1,0:T(8,128)(2,1)S(1)}, bf16[3,256,1024]{2,1,0:T(8,128)(2,1)S(1)}, u32[]{:S(2)}, u32[]{:S(2)}) collective-permute-start(bf16[3,256,1024]{2,1,0:T(8,128)(2,1)S(1)} %get-tuple-element.84), channel_id=1, source_target_pairs={{0,1},{1,0},{2,3},{3,2},{4,5},{5,4},{6,7},{7,6},{8,9},{9,8},{10,11... | collective-permute-start | bytes 4718600 | tf_op jit(solution)/shard_map/ppermute | solution.py:27
  82.2 18.7 %collective-permute-start.11 = (bf16[3,256,1024]{2,1,0:T(8,128)(2,1)S(1)}, bf16[3,256,1024]{2,1,0:T(8,128)(2,1)S(1)}, u32[]{:S(2)}, u32[]{:S(2)}) collective-permute-start(bf16[3,256,1024]{2,1,0:T(8,128)(2,1)S(1)} %collective-permute-done.10.refs_7_.refs_13_.refs_11_), channel_id=1, source_target_pairs={{0,8},{8,0},{16,24},{24,16},{1,9},{9,1},{17,25},{25,17},{2,10},{10... | collective-permute-start | bytes 4718600 | tf_op jit(solution)/shard_map/ppermute | solution.py:27
  91.8 92.7 %collective-permute-start.1 = (bf16[1024,2048]{1,0:T(8,128)(2,1)}, bf16[1024,2048]{1,0:T(8,128)(2,1)}, u32[]{:S(2)}, u32[]{:S(2)}) collective-permute-start(bf16[1024,2048]{1,0:T(8,128)(2,1)} %collective-permute-done.refs_1_), channel_id=1, source_target_pairs={{2,4},{4,2},{3,5},{5,3},{10,12},{12,10},{11,13},{13,11},{18,20},{2... | collective-permute-start | bytes 12582920 | tf_op jit(solution)/shard_map/ppermute | solution.py:395
  95.0 90.6 %collective-permute-start.18 = (bf16[1024,2048]{1,0:T(8,128)(2,1)}, bf16[1024,2048]{1,0:T(8,128)(2,1)}, u32[]{:S(2)}, u32[]{:S(2)}) collective-permute-start(bf16[1024,2048]{1,0:T(8,128)(2,1)} %collective-permute-done.17.refs_2_), channel_id=1, source_target_pairs={{2,0},{4,6},{3,1},{5,7},{10,8},{12,14},{11,9},{13,15},{18,16},{20,... | collective-permute-start | bytes 12582920 | tf_op jit(solution)/shard_map/ppermute | solution.py:394
  98.6 34.5 %collective-permute-start.8 = (bf16[3,256,1024]{2,1,0:T(8,128)(2,1)S(1)}, bf16[3,256,1024]{2,1,0:T(8,128)(2,1)}, u32[]{:S(2)}, u32[]{:S(2)}) collective-permute-start(bf16[3,256,1024]{2,1,0:T(8,128)(2,1)S(1)} %get-tuple-element.46), channel_id=1, source_target_pairs={{0,1},{1,0},{2,3},{3,2},{4,5},{5,4},{6,7},{7,6},{8,9},{9,8},{10,11... | collective-permute-start | bytes 4718600 | tf_op jit(solution)/shard_map/ppermute | solution.py:27
  99.7 34.2 %collective-permute-start.15 = (bf16[3,256,1024]{2,1,0:T(8,128)(2,1)S(1)}, bf16[3,256,1024]{2,1,0:T(8,128)(2,1)}, u32[]{:S(2)}, u32[]{:S(2)}) collective-permute-start(bf16[3,256,1024]{2,1,0:T(8,128)(2,1)S(1)} %collective-permute-done.7.refs_4_.refs_6_), channel_id=1, source_target_pairs={{0,16},{8,24},{16,0},{24,8},{1,17},{9,25},{17,1},{25,9},{2,18},{10... | collective-permute-start | bytes 4718600 | tf_op jit(solution)/shard_map/ppermute | solution.py:27
  102.1 34.8 %collective-permute-start.13 = (bf16[3,256,1024]{2,1,0:T(8,128)(2,1)S(1)}, bf16[3,256,1024]{2,1,0:T(8,128)(2,1)S(1)}, u32[]{:S(2)}, u32[]{:S(2)}) collective-permute-start(bf16[3,256,1024]{2,1,0:T(8,128)(2,1)S(1)} %collective-permute-done.7.refs_4_.refs_6_), channel_id=1, source_target_pairs={{0,8},{8,0},{16,24},{24,16},{1,9},{9,1},{17,25},{25,17},{2,10},{10... | collective-permute-start | bytes 4718600 | tf_op jit(solution)/shard_map/ppermute | solution.py:27
  133.1 36.9 %collective-permute-start.12 = (bf16[3,256,1024]{2,1,0:T(8,128)(2,1)}, bf16[3,256,1024]{2,1,0:T(8,128)(2,1)}, u32[]{:S(2)}, u32[]{:S(2)}) collective-permute-start(bf16[3,256,1024]{2,1,0:T(8,128)(2,1)} %get-tuple-element.49), channel_id=1, source_target_pairs={{0,1},{1,0},{2,3},{3,2},{4,5},{5,4},{6,7},{7,6},{8,9},{9,8},{10,11... | collective-permute-start | bytes 4718600 | tf_op jit(solution)/shard_map/ppermute | solution.py:27
  133.9 6.4 %collective-permute-start.16 = (bf16[3,256,1024]{2,1,0:T(8,128)(2,1)}, bf16[3,256,1024]{2,1,0:T(8,128)(2,1)}, u32[]{:S(2)}, u32[]{:S(2)}) collective-permute-start(bf16[3,256,1024]{2,1,0:T(8,128)(2,1)} %collective-permute-done.15.refs_8_.refs_14_.refs_12_), channel_id=1, source_target_pairs={{0,8},{8,0},{16,24},{24,16},{1,9},{9,1},{17,25},{25,17},{2,10},{10... | collective-permute-start | bytes 4718600 | tf_op jit(solution)/shard_map/ppermute | solution.py:27
  138.1 36.3 %collective-permute-start.20 = (bf16[3,256,1024]{2,1,0:T(8,128)(2,1)}, bf16[3,256,1024]{2,1,0:T(8,128)(2,1)}, u32[]{:S(2)}, u32[]{:S(2)}) collective-permute-start(bf16[3,256,1024]{2,1,0:T(8,128)(2,1)} %collective-permute-done.8.refs_7_.refs_5_), channel_id=1, source_target_pairs={{0,16},{8,24},{16,0},{24,8},{1,17},{9,25},{17,1},{25,9},{2,18},{10... | collective-permute-start | bytes 4718600 | tf_op jit(solution)/shard_map/ppermute | solution.py:27
  169.9 52.2 %copy-start.2 = (bf16[3,256,1024]{2,1,0:T(8,128)(2,1)S(1)}, bf16[3,256,1024]{2,1,0:T(8,128)(2,1)}, u32[]{:S(2)}) copy-start(bf16[3,256,1024]{2,1,0:T(8,128)(2,1)} %copy-done) | copy-start | bytes 4718596
  169.9 52.2 %copy-start.6 = (bf16[3,256,1024]{2,1,0:T(8,128)(2,1)S(1)}, bf16[3,256,1024]{2,1,0:T(8,128)(2,1)}, u32[]{:S(2)}) copy-start(bf16[3,256,1024]{2,1,0:T(8,128)(2,1)} %copy-done.4) | copy-start | bytes 4718596
  169.9 52.1 %copy-start.10 = (bf16[3,256,1024]{2,1,0:T(8,128)(2,1)S(1)}, bf16[3,256,1024]{2,1,0:T(8,128)(2,1)}, u32[]{:S(2)}) copy-start(bf16[3,256,1024]{2,1,0:T(8,128)(2,1)} %copy-done.8) | copy-start | bytes 4718596
  170.0 52.1 %copy-start.14 = (bf16[3,256,1024]{2,1,0:T(8,128)(2,1)S(1)}, bf16[3,256,1024]{2,1,0:T(8,128)(2,1)}, u32[]{:S(2)}) copy-start(bf16[3,256,1024]{2,1,0:T(8,128)(2,1)} %copy-done.12) | copy-start | bytes 4718596
  174.4 35.3 %collective-permute-start.21 = (bf16[3,256,1024]{2,1,0:T(8,128)(2,1)}, bf16[3,256,1024]{2,1,0:T(8,128)(2,1)S(1)}, u32[]{:S(2)}, u32[]{:S(2)}) collective-permute-start(bf16[3,256,1024]{2,1,0:T(8,128)(2,1)} %collective-permute-done.12.refs_8_.refs_6_), channel_id=1, source_target_pairs={{0,16},{8,24},{16,0},{24,8},{1,17},{9,25},{17,1},{25,9},{2,18},{10... | collective-permute-start | bytes 4718600 | tf_op jit(solution)/shard_map/ppermute | solution.py:27
  185.6 24.2 %collective-permute-start.19 = (bf16[3,256,1024]{2,1,0:T(8,128)(2,1)}, bf16[3,256,1024]{2,1,0:T(8,128)(2,1)S(1)}, u32[]{:S(2)}, u32[]{:S(2)}) collective-permute-start(bf16[3,256,1024]{2,1,0:T(8,128)(2,1)} %collective-permute-done.12.refs_8_.refs_6_), channel_id=1, source_target_pairs={{0,8},{8,0},{16,24},{24,16},{1,9},{9,1},{17,25},{25,17},{2,10},{10... | collective-permute-start | bytes 4718600 | tf_op jit(solution)/shard_map/ppermute | solution.py:27
  190.0 26.7 %collective-permute-start.2 = (bf16[256,2048]{1,0:T(8,128)(2,1)S(1)}, bf16[256,2048]{1,0:T(8,128)(2,1)S(1)}, u32[]{:S(2)}, u32[]{:S(2)}) collective-permute-start(bf16[256,2048]{1,0:T(8,128)(2,1)S(1)} %get-tuple-element.90), channel_id=1, source_target_pairs={{2,0},{4,6},{3,1},{5,7},{10,8},{12,14},{11,9},{13,15},{18,16},{20,... | collective-permute-start | bytes 3145736 | tf_op jit(solution)/shard_map/ppermute | solution.py:482
  194.2 26.7 %collective-permute-start.14 = (bf16[3,256,1024]{2,1,0:T(8,128)(2,1)}, bf16[3,256,1024]{2,1,0:T(8,128)(2,1)S(1)}, u32[]{:S(2)}, u32[]{:S(2)}) collective-permute-start(bf16[3,256,1024]{2,1,0:T(8,128)(2,1)} %collective-permute-done.8.refs_7_.refs_5_), channel_id=1, source_target_pairs={{0,8},{8,0},{16,24},{24,16},{1,9},{9,1},{17,25},{25,17},{2,10},{10... | collective-permute-start | bytes 4718600 | tf_op jit(solution)/shard_map/ppermute | solution.py:27
  194.5 26.3 %collective-permute-start.22 = (bf16[3,256,1024]{2,1,0:T(8,128)(2,1)}, bf16[3,256,1024]{2,1,0:T(8,128)(2,1)S(1)}, u32[]{:S(2)}, u32[]{:S(2)}) collective-permute-start(bf16[3,256,1024]{2,1,0:T(8,128)(2,1)} %collective-permute-done.20.refs_15_.refs_13_), channel_id=1, source_target_pairs={{0,8},{8,0},{16,24},{24,16},{1,9},{9,1},{17,25},{25,17},{2,10},{10... | collective-permute-start | bytes 4718600 | tf_op jit(solution)/shard_map/ppermute | solution.py:27
  209.8 86.3 %copy-start.16 = (bf16[3,256,1024]{2,1,0:T(8,128)(2,1)}, bf16[3,256,1024]{2,1,0:T(8,128)(2,1)S(1)}, u32[]{:S(2)}) copy-start(bf16[3,256,1024]{2,1,0:T(8,128)(2,1)S(1)} %collective-permute-done.21.refs_16_.refs_14_) | copy-start | bytes 4718596
  209.8 86.3 %copy-start.18 = (bf16[3,256,1024]{2,1,0:T(8,128)(2,1)}, bf16[3,256,1024]{2,1,0:T(8,128)(2,1)S(1)}, u32[]{:S(2)}) copy-start(bf16[3,256,1024]{2,1,0:T(8,128)(2,1)S(1)} %collective-permute-done.19.refs_12_.refs_10_) | copy-start | bytes 4718596
  209.8 11.1 %collective-permute-start.23 = (bf16[3,256,1024]{2,1,0:T(8,128)(2,1)S(1)}, bf16[3,256,1024]{2,1,0:T(8,128)(2,1)S(1)}, u32[]{:S(2)}, u32[]{:S(2)}) collective-permute-start(bf16[3,256,1024]{2,1,0:T(8,128)(2,1)S(1)} %collective-permute-done.21.refs_16_.refs_14_), channel_id=1, source_target_pairs={{0,8},{8,0},{16,24},{24,16},{1,9},{9,1},{17,25},{25,17},{2,10},{10... | collective-permute-start | bytes 4718600 | tf_op jit(solution)/shard_map/ppermute | solution.py:27
  211.5 34.1 %collective-permute-start.5 = (bf16[256,2048]{1,0:T(8,128)(2,1)S(1)}, bf16[256,2048]{1,0:T(8,128)(2,1)S(1)}, u32[]{:S(2)}, u32[]{:S(2)}) collective-permute-start(bf16[256,2048]{1,0:T(8,128)(2,1)S(1)} %get-tuple-element.89), channel_id=1, source_target_pairs={{2,0},{4,6},{3,1},{5,7},{10,8},{12,14},{11,9},{13,15},{18,16},{20,... | collective-permute-start | bytes 3145736 | tf_op jit(solution)/shard_map/ppermute | solution.py:482
  216.7 53.9 %collective-permute-start.3 = (bf16[256,2048]{1,0:T(8,128)(2,1)S(1)}, bf16[256,2048]{1,0:T(8,128)(2,1)S(1)}, u32[]{:S(2)}, u32[]{:S(2)}) collective-permute-start(bf16[256,2048]{1,0:T(8,128)(2,1)S(1)} %get-tuple-element.44), channel_id=1, source_target_pairs={{2,0},{4,6},{3,1},{5,7},{10,8},{12,14},{11,9},{13,15},{18,16},{20,... | collective-permute-start | bytes 3145736 | tf_op jit(solution)/shard_map/ppermute | solution.py:482
  220.9 75.2 %copy-start.20 = (bf16[3,256,1024]{2,1,0:T(8,128)(2,1)}, bf16[3,256,1024]{2,1,0:T(8,128)(2,1)S(1)}, u32[]{:S(2)}) copy-start(bf16[3,256,1024]{2,1,0:T(8,128)(2,1)S(1)} %collective-permute-done.14.refs_11_.refs_9_) | copy-start | bytes 4718596
  220.9 24.7 %copy-start.22 = (bf16[3,256,1024]{2,1,0:T(8,128)(2,1)}, bf16[3,256,1024]{2,1,0:T(8,128)(2,1)S(1)}, u32[]{:S(2)}) copy-start(bf16[3,256,1024]{2,1,0:T(8,128)(2,1)S(1)} %collective-permute-done.22.refs_19_.refs_17_) | copy-start | bytes 4718596
  254.9 56.3 %collective-permute-start.24 = (bf16[3,256,512]{2,1,0:T(8,128)(2,1)}, bf16[3,256,512]{2,1,0:T(8,128)(2,1)}, u32[]{:S(2)}, u32[]{:S(2)}) collective-permute-start(bf16[3,256,512]{2,1,0:T(8,128)(2,1)} %get-tuple-element.61), channel_id=1, source_target_pairs={{0,1},{1,0},{2,3},{3,2},{4,5},{5,4},{6,7},{7,6},{8,9},{9,8},{10,11... | collective-permute-start | bytes 2359304 | tf_op jit(solution)/shard_map/ppermute | solution.py:27
  264.5 41.2 %collective-permute-start.25 = (bf16[3,256,512]{2,1,0:T(8,128)(2,1)}, bf16[3,256,512]{2,1,0:T(8,128)(2,1)}, u32[]{:S(2)}, u32[]{:S(2)}) collective-permute-start(bf16[3,256,512]{2,1,0:T(8,128)(2,1)} %get-tuple-element.63), channel_id=1, source_target_pairs={{0,1},{1,0},{2,3},{3,2},{4,5},{5,4},{6,7},{7,6},{8,9},{9,8},{10,11... | collective-permute-start | bytes 2359304 | tf_op jit(solution)/shard_map/ppermute | solution.py:27
  268.4 48.1 %collective-permute-start.27 = (bf16[128,2048]{1,0:T(8,128)(2,1)}, bf16[128,2048]{1,0:T(8,128)(2,1)}, u32[]{:S(2)}, u32[]{:S(2)}) collective-permute-start(bf16[128,2048]{1,0:T(8,128)(2,1)} %get-tuple-element.69), channel_id=1, source_target_pairs={{2,0},{4,6},{3,1},{5,7},{10,8},{12,14},{11,9},{13,15},{18,16},{20,... | collective-permute-start | bytes 1572872 | tf_op jit(solution)/shard_map/ppermute | solution.py:482
  270.5 46.0 %collective-permute-start.4 = (bf16[128,2048]{1,0:T(8,128)(2,1)}, bf16[128,2048]{1,0:T(8,128)(2,1)}, u32[]{:S(2)}, u32[]{:S(2)}) collective-permute-start(bf16[128,2048]{1,0:T(8,128)(2,1)} %get-tuple-element.45), channel_id=1, source_target_pairs={{2,0},{4,6},{3,1},{5,7},{10,8},{12,14},{11,9},{13,15},{18,16},{20,... | collective-permute-start | bytes 1572872 | tf_op jit(solution)/shard_map/ppermute | solution.py:482
  296.1 9.4 %copy-start.38 = (f32[512]{0:T(512)S(1)}, f32[512]{0:T(512)}, u32[]{:S(2)}) copy-start(f32[512]{0:T(512)} %param.10) | copy-start | bytes 6148
  305.5 34.9 %collective-permute-start.29 = (bf16[3,256,512]{2,1,0:T(8,128)(2,1)}, bf16[3,256,512]{2,1,0:T(8,128)(2,1)}, u32[]{:S(2)}, u32[]{:S(2)}) collective-permute-start(bf16[3,256,512]{2,1,0:T(8,128)(2,1)} %get-tuple-element.74), channel_id=1, source_target_pairs={{0,1},{1,0},{2,3},{3,2},{4,5},{5,4},{6,7},{7,6},{8,9},{9,8},{10,11... | collective-permute-start | bytes 2359304 | tf_op jit(solution)/shard_map/ppermute | solution.py:27
  306.8 9.8 %copy-start.3 = (bf16[3,256,1024]{2,1,0:T(8,128)(2,1)S(1)}, bf16[3,256,1024]{2,1,0:T(8,128)(2,1)}, u32[]{:S(2)}) copy-start(bf16[3,256,1024]{2,1,0:T(8,128)(2,1)} %copy-done) | copy-start | bytes 4718596
  306.8 9.8 %copy-start.7 = (bf16[3,256,1024]{2,1,0:T(8,128)(2,1)S(1)}, bf16[3,256,1024]{2,1,0:T(8,128)(2,1)}, u32[]{:S(2)}) copy-start(bf16[3,256,1024]{2,1,0:T(8,128)(2,1)} %copy-done.4) | copy-start | bytes 4718596
  330.3 10.1 %copy-start.33 = (bf16[3,256,512]{2,1,0:T(8,128)(2,1)S(1)}, bf16[3,256,512]{2,1,0:T(8,128)(2,1)}, u32[]{:S(2)}) copy-start(bf16[3,256,512]{2,1,0:T(8,128)(2,1)} %copy-done.32) | copy-start | bytes 2359300
  330.3 14.4 %collective-permute-start.28 = (bf16[3,128,512]{2,1,0:T(8,128)(2,1)S(1)}, bf16[3,128,512]{2,1,0:T(8,128)(2,1)S(1)}, u32[]{:S(2)}, u32[]{:S(2)}) collective-permute-start(bf16[3,128,512]{2,1,0:T(8,128)(2,1)S(1)} %get-tuple-element.72), channel_id=1, source_target_pairs={{0,1},{1,0},{2,3},{3,2},{4,5},{5,4},{6,7},{7,6},{8,9},{9,8},{10,11... | collective-permute-start | bytes 1179656 | tf_op jit(solution)/shard_map/ppermute | solution.py:27
  338.7 11.4 %collective-permute-start.26 = (bf16[3,128,512]{2,1,0:T(8,128)(2,1)S(1)}, bf16[3,128,512]{2,1,0:T(8,128)(2,1)S(1)}, u32[]{:S(2)}, u32[]{:S(2)}) collective-permute-start(bf16[3,128,512]{2,1,0:T(8,128)(2,1)S(1)} %get-tuple-element.68), channel_id=1, source_target_pairs={{0,1},{1,0},{2,3},{3,2},{4,5},{5,4},{6,7},{7,6},{8,9},{9,8},{10,11... | collective-permute-start | bytes 1179656 | tf_op jit(solution)/shard_map/ppermute | solution.py:27
  340.4 18.4 %copy-start.28 = (bf16[3,256,512]{2,1,0:T(8,128)(2,1)S(1)}, bf16[3,256,512]{2,1,0:T(8,128)(2,1)}, u32[]{:S(2)}) copy-start(bf16[3,256,512]{2,1,0:T(8,128)(2,1)} %copy-done.26) | copy-start | bytes 2359300
  340.4 18.4 %copy-start.31 = (bf16[3,256,512]{2,1,0:T(8,128)(2,1)S(1)}, bf16[3,256,512]{2,1,0:T(8,128)(2,1)}, u32[]{:S(2)}) copy-start(bf16[3,256,512]{2,1,0:T(8,128)(2,1)} %copy-done.29) | copy-start | bytes 2359300
  340.4 18.4 %copy-start.34 = (s32[8]{0:T(128)S(1)}, s32[8]{0:T(128)}, u32[]{:S(2)}) copy-start(s32[8]{0:T(128)} %order.1) | copy-start | bytes 100
  351.7 3.6 collective-permute-start.30
  353.5 3.7 collective-permute-start.31
  353.5 5.2 %collective-permute-start.32 = (f32[16,8,128]{2,1,0:T(8,128)S(1)}, f32[16,8,128]{2,1,0:T(8,128)S(1)}, u32[]{:S(2)}, u32[]{:S(2)}) collective-permute-start(f32[16,8,128]{2,1,0:T(8,128)S(1)} %get-tuple-element.77.refs_0_), channel_id=1, source_target_pairs={{0,24},{8,16},{16,8},{24,0},{1,25},{9,17},{17,9},{25,1},{2,26},{10... | collective-permute-start | bytes 196616 | tf_op jit(solution)/shard_map/ppermute | solution.py:27
  (24 other events, 54.0 us)

commit v4 on v3

--- a/solution.py
+++ b/solution.py
@@ -12,7 +12,7 @@
 DEPTH = 512
 CHUNKS = (256, 256, 256, 128, 128)
 PASSED = (1024,)
-T = {'y_y': True, 'y3_c0': True, 'y2_A': False, 'x_x': [0, 1, 1, 1], 'x_c': [0, 0, 1, 1], 'Ka': 'c3', 'x2_A': False, 'c_A': 9, 'c_P': [3], 'x_P': [], 'c_ser': [1, 0, 0, 1], 'copy': None, 'E': {2: 0, 3: 1, 4: 2}, 'S': {3: 0, 4: 1}}
+T = {'y_y': True, 'y3_c0': True, 'y2_A': False, 'x_x': [0, 1, 1, 1], 'x_c': [0, 0, 1, 1], 'Ka': 'c3', 'x2_A': False, 'c_A': 9, 'c_P': [3], 'x_P': [], 'c_ser': [1, 0, 0, 1], 'E': [0, 1], 'S': {3: 0, 4: 1}, 'cK': 0, 'cP': 0}
 FREE = pl.CostEstimate(flops=0, bytes_accessed=0, transcendentals=0)
 
 
@@ -35,7 +35,7 @@
     return residue * jnp.sqrt(jnp.maximum(-jnp.expm1(-2.0 * rate), 1.0 / length))
 
 
-def fetch_weights(plan, place, block, own, pieces, stride, target, sem):
+def fetch_weights(plan, place, p, block, own, pieces, stride, target, sem):
     pair, ctx = place[0], place[1]
     local = lax.rem(block, plan.half_blocks)
     here = lax.div(block, plan.half_blocks) == pair
@@ -43,7 +43,7 @@
     @pl.when(here)
     def _():
         row = pl.multiple_of(local * DEPTH, DEPTH)
-        pltpu.make_async_copy(own.at[:, pl.ds(row, DEPTH), :], target, sem).start()
+        pltpu.make_async_copy(own.at[p, pl.ds(row, DEPTH), :], target, sem).start()
 
     number = jnp.bitwise_xor(lax.div(local, plan.part_blocks), ctx)
     if stride == 1:
@@ -53,7 +53,7 @@
         def _():
             for side in (0, 1):
                 rows = pl.ds(side * (DEPTH // 2), DEPTH // 2)
-                pltpu.make_async_copy(pieces[2 * n + side], target.at[:, rows, :], sem).start()
+                pltpu.make_async_copy(pieces[2 * n + side].at[p], target.at[rows, :], sem).start()
 
 
 def project_kernel(plan, n_inputs, stride, base, final, blocks, x_plan, place, *refs):
@@ -63,71 +63,85 @@
     pieces = [refs.pop(0) for _ in range(plan.n_pieces // stride)]
     init = refs.pop(0) if base is not None else None
     outs = [refs.pop(0) for _ in range(2 if final else 1)]
-    x_buf, w_buf, x_sem, w_sem, acc_sem = refs[:5]
-    acc = refs[5] if final else outs[0]
+    x_buf, w_buf, x_sem, w_sem = refs[:4]
+    if init is not None:
+        i_buf, i_sem = refs[4:6]
     pair, tp = place[0], place[2]
-    slots = x_buf.shape[0]
-
-    def start(step):
-        slot = lax.rem(step, slots)
-        block = x_plan(tp, step, inputs, x_buf.at[slot], x_sem.at[slot])
-        fetch_weights(
-            plan, place, block, own, pieces, stride, w_buf.at[slot], w_sem.at[slot]
-        )
-
-    if init is not None:
-        pltpu.make_async_copy(init.at[:, pl.ds(base, acc.shape[1]), :], acc, acc_sem).start()
-    for ahead in range(min(slots - 1, blocks)):
-        start(jnp.int32(ahead))
-    if init is None:
-        acc[...] = jnp.zeros_like(acc)
-    else:
-        pltpu.make_async_copy(acc, acc, acc_sem).wait()
-
-    def body(step, carry):
-        slot = lax.rem(step, slots)
-
-        @pl.when(step + slots - 1 < blocks)
-        def _():
-            start(step + slots - 1)
-
-        pltpu.make_async_copy(x_buf.at[slot], x_buf.at[slot], x_sem.at[slot]).wait()
-        pltpu.make_async_copy(w_buf.at[slot], w_buf.at[slot], w_sem.at[slot]).wait()
-        block = x_buf[slot]
-        for p in range(3):
-            acc[p] += jnp.dot(block, w_buf[slot, p], preferred_element_type=jnp.float32)
-        return carry
-
-    lax.fori_loop(0, blocks, body, 0)
-    if not final:
-        return
-    kept, given = outs
-    half = kept.shape[2]
-    mine = pl.multiple_of(pair * half, 128)
-    other = pl.multiple_of((1 - pair) * half, 128)
+    rows = x_buf.shape[0]
+
+    def fetch(p):
+        if init is not None:
+            pltpu.make_async_copy(
+                init.at[p, pl.ds(base, rows), :], i_buf.at[p], i_sem.at[p]
+            ).start()
+
+        def one(step, carry):
+            depth = pl.ds(pl.multiple_of(step * DEPTH, DEPTH), DEPTH)
+            block = x_plan(tp, step, inputs, x_buf.at[:, depth], x_sem, p == 0)
+            fetch_weights(
+                plan, place, p, block, own, pieces, stride, w_buf.at[p, depth, :], w_sem.at[p]
+            )
+            return carry
+
+        lax.fori_loop(0, blocks, one, 0)
+
+    fetch(0)
+    fetch(1)
+    pltpu.make_async_copy(x_buf, x_buf, x_sem).wait()
     for p in range(3):
-        kept[p] = acc[p, :, pl.ds(mine, half)].astype(jnp.bfloat16)
-        given[p] = acc[p, :, pl.ds(other, half)].astype(jnp.bfloat16)
+        pltpu.make_async_copy(w_buf.at[p], w_buf.at[p], w_sem.at[p]).wait()
+        if init is not None:
+            pltpu.make_async_copy(i_buf.at[p], i_buf.at[p], i_sem.at[p]).wait()
+        if p == 0:
+            fetch(2)
+        if not final:
+            chunk = min(rows, 256)
+
+            def multiply(m, carry):
+                some = pl.ds(pl.multiple_of(m * chunk, chunk), chunk)
+                new = jnp.dot(x_buf[some, :], w_buf[p], preferred_element_type=jnp.float32)
+                outs[0][p, some, :] = new if init is None else i_buf[p, some, :] + new
+                return carry
+
+            lax.fori_loop(0, rows // chunk, multiply, 0)
+            continue
+        kept, given = outs
+        half = kept.shape[2]
+        for mine, out in ((True, kept), (False, given)):
+            lanes = pl.ds(pl.multiple_of((pair if mine else 1 - pair) * half, 128), half)
+            new = jnp.dot(x_buf[...], w_buf[p, :, lanes], preferred_element_type=jnp.float32)
+            if init is not None:
+                new = i_buf[p, :, lanes] + new
+            new = new.astype(jnp.bfloat16)
+            if mine or p == 0:
+                out[p] = new
+            elif p == 1:
+                out[1] = new
+            else:
+                product = out[1].astype(jnp.float32) * new.astype(jnp.float32)
+                out[1] = product.astype(jnp.bfloat16)
 
 
 def project(plan, place, inputs, own, pieces, stride, init, base, rows, blocks, x_plan, final):
     width = own.shape[2]
-    slots = 4 if final else 3
     anywhere = pl.BlockSpec(memory_space=pl.ANY)
     local = pl.BlockSpec(memory_space=pltpu.VMEM)
     operands = list(inputs) + [own] + list(pieces) + ([] if init is None else [init])
-    total = (3, rows, width)
+    depth = blocks * DEPTH
     scratch = [
-        pltpu.VMEM((slots, rows, DEPTH), jnp.bfloat16),
-        pltpu.VMEM((slots, 3, DEPTH, width), jnp.bfloat16),
-        pltpu.SemaphoreType.DMA((slots,)),
-        pltpu.SemaphoreType.DMA((slots,)),
+        pltpu.VMEM((rows, depth), jnp.bfloat16),
+        pltpu.VMEM((3, depth, width), jnp.bfloat16),
         pltpu.SemaphoreType.DMA,
+        pltpu.SemaphoreType.DMA((3,)),
     ]
-    out_shape = jax.ShapeDtypeStruct(total, jnp.float32)
+    if init is not None:
+        scratch.append(pltpu.VMEM((3, rows, width), jnp.float32))
+        scratch.append(pltpu.SemaphoreType.DMA((3,)))
+    out_shape = jax.ShapeDtypeStruct((3, rows, width), jnp.float32)
     if final:
-        scratch.append(pltpu.VMEM(total, jnp.float32))
-        out_shape = [jax.ShapeDtypeStruct((3, rows, width // 2), jnp.bfloat16)] * 2
+        out_shape = [
+            jax.ShapeDtypeStruct((n, rows, width // 2), jnp.bfloat16) for n in (3, 2)
+        ]
     return pl.pallas_call(
         functools.partial(
             project_kernel, plan, len(inputs), stride, None if init is None else base, final,
@@ -141,8 +155,10 @@
             scratch_shapes=scratch,
         ),
         out_shape=out_shape,
-        compiler_params=pltpu.CompilerParams(vmem_limit_bytes=30 * MIB),
-        cost_estimate=FREE,
+        compiler_params=pltpu.CompilerParams(vmem_limit_bytes=56 * MIB),
+        cost_estimate=pl.CostEstimate(
+            flops=T["cP"] if final else T["cK"], bytes_accessed=0, transcendentals=0
+        ),
         name="project" if final else "project_part",
     )(place, *operands)
 
@@ -152,9 +168,10 @@
 
 
 def gathered_plan(per_quarter):
-    def plan(tp, step, inputs, target, sem):
+    def plan(tp, step, inputs, target, sem, copy):
         source = inputs[0].at[lax.div(step, per_quarter), :, columns(lax.rem(step, per_quarter))]
-        pltpu.make_async_copy(source, target, sem).start()
+        if copy:
+            pltpu.make_async_copy(source, target, sem).start()
         return step
 
     return plan
@@ -164,25 +181,28 @@
     return (tp == 0) | (tp == 3)
 
 
-def near_block(plan, tp, step, number, base, inputs, target, sem):
+def near_block(plan, tp, step, number, base, inputs, target, sem, copy):
     span = plan.half_blocks // 2 // plan.part_blocks
     mine = step < span
     side = jnp.where(mine, lax.rem(tp, 2), 1 - lax.rem(tp, 2))
     within = lax.rem(step, span)
     where = columns(within * plan.part_blocks + number)
+    part = side * span + within
+    block = lax.div(tp, 2) * plan.half_blocks + part * plan.part_blocks + number
+    if not copy:
+        return block
     for at, source in ((True, inputs[0]), (False, inputs[1])):
         @pl.when(mine == at)
         def _():
             rows = pl.ds(base, target.shape[0])
             pltpu.make_async_copy(source.at[rows, where], target, sem).start()
 
-    part = side * span + within
-    return lax.div(tp, 2) * plan.half_blocks + part * plan.part_blocks + number
+    return block
 
 
 def near_plan(plan, number, base):
-    def x_plan(tp, step, inputs, target, sem):
-        return near_block(plan, tp, step, number, base, inputs, target, sem)
+    def x_plan(tp, step, inputs, target, sem, copy):
+        return near_block(plan, tp, step, number, base, inputs, target, sem, copy)
 
     return x_plan
 
@@ -191,14 +211,21 @@
     span = plan.half_blocks // plan.part_blocks
     per_quarter = plan.half_blocks // 2
 
-    def x_plan(tp, step, inputs, target, sem):
+    def x_plan(tp, step, inputs, target, sem, copy):
         middle, ends = inputs[2], inputs[3:]
         late = step - span
+        half = span // 2
+        side = jnp.where(step < half, lax.rem(tp, 2), 1 - lax.rem(tp, 2))
+        part = side * half + lax.rem(step, half)
+        near = lax.div(tp, 2) * plan.half_blocks + part * plan.part_blocks + number
+        block = jnp.where(late < 0, near, (2 - lax.div(tp, 2)) * per_quarter + late)
+        if not copy:
+            return block
         where = columns(jnp.maximum(late, 0))
 
         @pl.when(step < span)
         def _():
-            near_block(plan, tp, step, number, base, inputs, target, sem)
+            near_block(plan, tp, step, number, base, inputs, target, sem, copy)
 
         @pl.when((late >= 0) & jnp.logical_not(line_ends(tp)))
         def _():
@@ -214,17 +241,16 @@
                 ).start()
                 row += size
 
-        half = span // 2
-        side = jnp.where(step < half, lax.rem(tp, 2), 1 - lax.rem(tp, 2))
-        part = side * half + lax.rem(step, half)
-        near = lax.div(tp, 2) * plan.half_blocks + part * plan.part_blocks + number
-        return jnp.where(late < 0, near, (2 - lax.div(tp, 2)) * per_quarter + late)
+        return block
 
     return x_plan
 
 
 def last_plan(per_quarter, row, rows):
-    def plan(tp, step, inputs, target, sem):
+    def plan(tp, step, inputs, target, sem, copy):
+        block = jnp.where(tp < 2, 3, 0) * per_quarter + step
+        if not copy:
+            return block
         middle, ends = inputs
         where = columns(step)
 
@@ -236,7 +262,7 @@
         def _():
             pltpu.make_async_copy(middle.at[pl.ds(row, rows), where], target, sem).start()
 
-        return jnp.where(tp < 2, 3, 0) * per_quarter + step
+        return block
 
     return plan
 
@@ -248,9 +274,10 @@
     for side, ref in enumerate((kept, given)):
         for g in range(groups):
             lanes = slice(g * 128, (g + 1) * 128)
-            key = ref[1, :, lanes].astype(jnp.float32)
-            value = ref[2, :, lanes].astype(jnp.float32)
-            prod[:, side * groups + g, :] = key * value
+            product = ref[1, :, lanes].astype(jnp.float32)
+            if side == 0:
+                product = product * ref[2, :, lanes].astype(jnp.float32)
+            prod[:, side * groups + g, :] = product
     direct = skip[...]
     factors = [decay[r] for r in range(poles)]
     gains = [gain[r] for r in range(poles)]
@@ -386,11 +413,8 @@
         middle = lax.ppermute(tokens, "tp", [(1, 2), (2, 1)])
         ends, far_middle, row = [], [], 0
         for rows in PASSED:
-            if T["copy"] is None:
-                block = lax.slice_in_dim(middle, row, row + rows, axis=0)
-                far = lax.slice_in_dim(near, row, row + rows, axis=0)
-            else:
-                block, far = take_rows(row, rows, middle, near)
+            block = lax.slice_in_dim(middle, row, row + rows, axis=0)
+            far = lax.slice_in_dim(near, row, row + rows, axis=0)
             ends.append(lax.ppermute(block, "tp", [(1, 0), (2, 3)]))
             far_middle.append(lax.ppermute(far, "tp", [(1, 2), (2, 1)]))
             row += rows
@@ -469,42 +493,39 @@
     direct = spread(skip[:, None])[0]
 
     if on_line:
-        far_ends, where = [], []
-        for k, (base, rows) in enumerate(zip(starts, CHUNKS)):
-            row, n = base, 0
-            while row >= PASSED[n]:
-                row -= PASSED[n]
-                n += 1
-            where.append((n, row))
-            block = lax.slice_in_dim(far_middle[n], row, row + rows, axis=0)
-            if k in T["E"]:
-                block = after(block, far_ends[T["E"][k]])
-            far_ends.append(lax.ppermute(block, "tp", [(1, 0), (2, 3)]))
         segments = {1024: (((0, 512),), ((512, 512),)), 768: (((0, 512),), ((512, 256), (0, 256)))}[PASSED[0]]
-        halves = []
-
-        def add_half(h):
-            sources = [tokens, near, middle] + ends[: len(segments[h])]
+
+        def add_half(h, first):
+            sources = [first, near, middle] + ends[: len(segments[h])]
             return project(
                 plan, place, sources, own, ordered, 1, partials[-1], h * 512, 512,
                 plan.half_blocks // plan.part_blocks + plan.half_blocks // 2,
                 middle_plan(plan, 1, h * 512, segments[h]), False,
             )
 
+        halves = [add_half(0, tokens)]
 
     kept, given, locals_ = [], [], []
     state = jnp.zeros_like(decay)
     states = []
     for k, (base, rows) in enumerate(zip(starts, CHUNKS)):
         if on_line:
-            last = far_ends[k]
-            if base % 512 == 0:
-                halves.append(add_half(base // 512))
+            n, row = 0, base
+            while row >= PASSED[n]:
+                row -= PASSED[n]
+                n += 1
+            if k == 1:
+                halves.append(add_half(1, after(tokens, kept[0])))
+            block = lax.slice_in_dim(far_middle[n], row, row + rows, axis=0)
+            if k >= 3:
+                block = after(block, halves[T["E"][k - 3]])
+            last = lax.ppermute(block, "tp", [(1, 0), (2, 3)])
+            if k == 1:
+                last = after(last, halves[1])
             if k in T["S"]:
                 last = after(last, states[T["S"][k]])
-            n, row = where[k]
             keep, give = project(
-                plan, place, [far_middle[n], last], own, ordered, 1, halves[-1], base % 512, rows,
+                plan, place, [far_middle[n], last], own, ordered, 1, halves[base // 512], base % 512, rows,
                 per_quarter, last_plan(per_quarter, row, rows), True,
             )
         else:

time: 374 us -> 339 us (0.906)
  local copies, waits for them, and re-layouts: 36.4 us -> 16.8 us
  waiting for transfers between devices: 144 us -> 130 us
    unnamed x78 -> x54, local copies, waits for them, and re-layouts: 27.1 us -> 5.98 us
    ppermute x24, waiting for transfers between devices: 122 us -> 115 us  [exchanged(): return lax.ppermute(block, axis, [(i, i ^ mask) for i in range(count)])]
    pallas_call x8, Pallas kernels: 104 us -> 111 us  [project(): pl.pallas_call(functools.partial(project_kernel, plan, len(inputs), strid...]
    pallas_call x5, Pallas kernels: 16.1 us -> 12.2 us  [scan(): pl.pallas_call(scan_kernel, in_specs=[local] * 6, out_specs=[local] * 2,...]
    ppermute x5, waiting for transfers between devices: 3.84 us -> 0.01 us  [per_device(): last = lax.ppermute(block, 'tp', [(1, 0), (2, 3)])]
  transfers between devices with their start and end apart: 33 -> 33, of which waited for: 14 -> 14; matrix products, arithmetic and copies ran while one was open for 3% -> 3% of each run, Pallas kernels for 32% -> 36%
where the time goes in v4:
time: 339 us; the launch traced here: 338 us
  Pallas kernels  133 us (39%)
  waiting for transfers between devices  130 us (38%)
  starting transfers between devices  56.3 us (17%)
  local copies, waits for them, and re-layouts  16.8 us (5%)
    ppermute x24, waiting for transfers between devices, exchanged(): return lax.ppermute(block, axis, [(i, i ^ mask) for i in range(count)])  115 us
    pallas_call x8, Pallas kernels, project(): pl.pallas_call(functools.partial(project_kernel, plan, len(inputs), strid...  111 us
    ppermute x24, starting transfers between devices, exchanged(): return lax.ppermute(block, axis, [(i, i ^ mask) for i in range(count)])  34.3 us
    pallas_call x5, Pallas kernels, scan(): pl.pallas_call(scan_kernel, in_specs=[local] * 6, out_specs=[local] * 2,...  12.2 us
    ppermute x5, starting transfers between devices, per_device(): last = lax.ppermute(block, 'tp', [(1, 0), (2, 3)])  10.6 us
    pallas_call x1, Pallas kernels, finish(): pl.pallas_call(functools.partial(finish_kernel, len(ends), n_chunks, seg_...  9.89 us
    ppermute x1, waiting for transfers between devices, per_device(): near = lax.ppermute(tokens, 'tp', [(0, 1), (1, 0), (2, 3), (3, 2)])  8.95 us
  transfers between devices with their start and end apart: 33, of which 14 were waited for; matrix products, arithmetic and copies ran while one was open for 3% of the time, Pallas kernels for 36%

profile of v4, /device:TPU:9, one launch (start us, length us, event | category | flops | bytes accessed | tf_op | source)
XLA Modules:
  0.0 337.9 jit_solution(17660853300067297736)
XLA Ops:
  0.0 4.5 %collective-permute-start.14 = (bf16[1024,2048]{1,0:T(8,128)(2,1)}, bf16[1024,2048]{1,0:T(8,128)(2,1)}, u32[]{:S(2)}, u32[]{:S(2)}) collective-permute-start(bf16[1024,2048]{1,0:T(8,128)(2,1)} %refs_0_.4), channel_id=1, source_target_pairs={{2,4},{4,2},{3,5},{5,3},{10,12},{12,10},{11,13},{13,11},{18,20},{2... | collective-permute-start | bytes 12582920 | tf_op jit(solution)/shard_map/ppermute | solution.py:413
  4.5 4.8 %dynamic-slice_bitcast_fusion = (bf16[3,256,1024]{2,1,0:T(8,128)(2,1)}, bf16[3,256,1024]{2,1,0:T(8,128)(2,1)S(1)}, bf16[3,256,1024]{2,1,0:T(8,128)(2,1)S(1)}, bf16[3,256,1024]{2,1,0:T(8,128)(2,1)S(1)}) fusion(bf16[4096,3,1024]{2,0,1:T(8,128)(2,1)} %param.7, s32[]{:T(128)S(6)} %select_n.15, s32[]{:T(128)S(6)} %select_n.13, s32[]{:T(128)S(6)} %select_n.12, ...), kind=kLoop, calls=%fused_computation | loop fusion | bytes 12582928 | tf_op jit(solution)/shard_map/dynamic_slice | solution.py:444
  9.3 1.2 collective-permute-start.3
  10.7 33.3 %collective-permute-done.3.refs_3_.refs_5_ = bf16[3,256,1024]{2,1,0:T(8,128)(2,1)S(1)} collective-permute-done((bf16[3,256,1024]{2,1,0:T(8,128)(2,1)S(1)}, bf16[3,256,1024]{2,1,0:T(8,128)(2,1)S(1)}, u32[]{:S(2)}, u32[]{:S(2)}) %collective-permute-start.3) | collective-permute-done | bytes 1572896 | tf_op jit(solution)/shard_map/ppermute | solution.py:27
  44.0 1.2 collective-permute-start.7
  45.2 4.1 %collective-permute-start.6 = (bf16[3,256,1024]{2,1,0:T(8,128)(2,1)S(1)}, bf16[3,256,1024]{2,1,0:T(8,128)(2,1)S(1)}, u32[]{:S(2)}, u32[]{:S(2)}) collective-permute-start(bf16[3,256,1024]{2,1,0:T(8,128)(2,1)S(1)} %collective-permute-done.3.refs_3_.refs_5_), channel_id=1, source_target_pairs={{0,8},{8,0},{16,24},{24,16},{1,9},{9,1},{17,25},{25,17},{2,10},{10... | collective-permute-start | bytes 4718600 | tf_op jit(solution)/shard_map/ppermute | solution.py:27
  49.3 28.4 %collective-permute-done.4.refs_4_.refs_6_ = bf16[3,256,1024]{2,1,0:T(8,128)(2,1)S(1)} collective-permute-done((bf16[3,256,1024]{2,1,0:T(8,128)(2,1)S(1)}, bf16[3,256,1024]{2,1,0:T(8,128)(2,1)S(1)}, u32[]{:S(2)}, u32[]{:S(2)}) %collective-permute-start.4) | collective-permute-done | bytes 1572896 | tf_op jit(solution)/shard_map/ppermute | solution.py:27
  77.7 1.2 collective-permute-start.5
  79.0 1.2 collective-permute-start.12
  80.2 2.6 collective-permute-start.8
  82.8 8.9 %collective-permute-done.refs_1_ = bf16[1024,2048]{1,0:T(8,128)(2,1)} collective-permute-done((bf16[1024,2048]{1,0:T(8,128)(2,1)}, bf16[1024,2048]{1,0:T(8,128)(2,1)}, u32[]{:S(2)}, u32[]{:S(2)}) %collective-permute-start) | collective-permute-done | bytes 4194336 | tf_op jit(solution)/shard_map/ppermute | solution.py:412
  91.8 3.2 collective-permute-start.1
  95.0 3.7 %collective-permute-start.15 = (bf16[1024,2048]{1,0:T(8,128)(2,1)}, bf16[1024,2048]{1,0:T(8,128)(2,1)}, u32[]{:S(2)}, u32[]{:S(2)}) collective-permute-start(bf16[1024,2048]{1,0:T(8,128)(2,1)} %collective-permute-done.14.refs_2_), channel_id=1, source_target_pairs={{2,0},{4,6},{3,1},{5,7},{10,8},{12,14},{11,9},{13,15},{18,16},{20,... | collective-permute-start | bytes 12582920 | tf_op jit(solution)/shard_map/ppermute | solution.py:418
  98.7 13.0 %collective-permute-done.5.refs_7_.refs_5_ = bf16[3,256,1024]{2,1,0:T(8,128)(2,1)S(1)} collective-permute-done((bf16[3,256,1024]{2,1,0:T(8,128)(2,1)S(1)}, bf16[3,256,1024]{2,1,0:T(8,128)(2,1)S(1)}, u32[]{:S(2)}, u32[]{:S(2)}) %collective-permute-start.5) | collective-permute-done | bytes 1572896 | tf_op jit(solution)/shard_map/ppermute | solution.py:27
  112.6 1.2 collective-permute-start.17
  114.2 3.7 %collective-permute-start.10 = (bf16[3,256,1024]{2,1,0:T(8,128)(2,1)S(1)}, bf16[3,256,1024]{2,1,0:T(8,128)(2,1)}, u32[]{:S(2)}, u32[]{:S(2)}) collective-permute-start(bf16[3,256,1024]{2,1,0:T(8,128)(2,1)S(1)} %collective-permute-done.4.refs_4_.refs_6_), channel_id=1, source_target_pairs={{0,8},{8,0},{16,24},{24,16},{1,9},{9,1},{17,25},{25,17},{2,10},{10... | collective-permute-start | bytes 4718600 | tf_op jit(solution)/shard_map/ppermute | solution.py:27
  117.9 27.6 %collective-permute-done.17.refs_15_.refs_13_ = bf16[3,256,1024]{2,1,0:T(8,128)(2,1)S(1)} collective-permute-done((bf16[3,256,1024]{2,1,0:T(8,128)(2,1)S(1)}, bf16[3,256,1024]{2,1,0:T(8,128)(2,1)S(1)}, u32[]{:S(2)}, u32[]{:S(2)}) %collective-permute-start.17) | collective-permute-done | bytes 1572896 | tf_op jit(solution)/shard_map/ppermute | solution.py:27
  146.6 4.0 %collective-permute-start.13 = (bf16[3,256,1024]{2,1,0:T(8,128)(2,1)}, bf16[3,256,1024]{2,1,0:T(8,128)(2,1)}, u32[]{:S(2)}, u32[]{:S(2)}) collective-permute-start(bf16[3,256,1024]{2,1,0:T(8,128)(2,1)} %collective-permute-done.12.refs_8_.refs_14_.refs_12_), channel_id=1, source_target_pairs={{0,8},{8,0},{16,24},{24,16},{1,9},{9,1},{17,25},{25,17},{2,10},{10... | collective-permute-start | bytes 4718600 | tf_op jit(solution)/shard_map/ppermute | solution.py:27
  151.3 2.7 collective-permute-done.13.refs_10_.refs_18_.refs_16_
  154.0 1.2 collective-permute-start.18
  155.3 24.0 %project_part.3.refs_21_ = f32[3,1024,1024]{2,1,0:T(8,128)} custom-call(s32[3]{0:T(128)} %pad_add_fusion.place, bf16[1024,2048]{1,0:T(8,128)(2,1)} %refs_0_.4, bf16[1024,2048]{1,0:T(8,128)(2,1)} %collective-permute-done.refs_1_, bf16[3,4096,1024]{2,1,0:T(8,128)(2,1)} %bitcast.18, bf16[3,256,1024]{2,1,0:T(8,128)(2,1)} %copy-done.7, ...), custom_call_target="tpu_custom_call" | custom-call | tf_op jit(solution)/shard_map/project_part/pallas_call | solution.py:145
  179.2 5.2 %collective-permute-done.1.refs_0_ = bf16[1024,2048]{1,0:T(8,128)(2,1)} collective-permute-done((bf16[1024,2048]{1,0:T(8,128)(2,1)}, bf16[1024,2048]{1,0:T(8,128)(2,1)}, u32[]{:S(2)}, u32[]{:S(2)}) %collective-permute-start.1) | collective-permute-done | bytes 4194336 | tf_op jit(solution)/shard_map/ppermute | solution.py:419
  185.7 2.1 collective-permute-start.16
  188.3 1.5 collective-permute-done.18.refs_16_.refs_14_
  189.9 3.4 %collective-permute-done.16.refs_12_.refs_10_ = bf16[3,256,1024]{2,1,0:T(8,128)(2,1)S(1)} collective-permute-done((bf16[3,256,1024]{2,1,0:T(8,128)(2,1)}, bf16[3,256,1024]{2,1,0:T(8,128)(2,1)S(1)}, u32[]{:S(2)}, u32[]{:S(2)}) %collective-permute-start.16) | collective-permute-done | bytes 1572896 | tf_op jit(solution)/shard_map/ppermute | solution.py:27
  193.6 3.8 %fusion = (bf16[256,2048]{1,0:T(8,128)(2,1)}, bf16[256,2048]{1,0:T(8,128)(2,1)}, bf16[256,2048]{1,0:T(8,128)(2,1)}) fusion(bf16[1024,2048]{1,0:T(8,128)(2,1)} %collective-permute-done.1.refs_0_), kind=kLoop, calls=%fused_computation.10 | loop fusion | bytes 6291456 | tf_op jit(solution)/shard_map/slice | solution.py:519
  197.4 5.1 %collective-permute-start.2 = (bf16[256,2048]{1,0:T(8,128)(2,1)}, bf16[256,2048]{1,0:T(8,128)(2,1)}, u32[]{:S(2)}, u32[]{:S(2)}) collective-permute-start(bf16[256,2048]{1,0:T(8,128)(2,1)} %get-tuple-element.91), channel_id=1, source_target_pairs={{2,0},{4,6},{3,1},{5,7},{10,8},{12,14},{11,9},{13,15},{18,16},{20,... | collective-permute-start | bytes 3145736 | tf_op jit(solution)/shard_map/ppermute | solution.py:522
  202.5 1.3 collective-permute-start.22
  203.9 1.5 collective-permute-start.28
  205.4 2.3 fusion.1
  208.8 22.7 %project_part.4.refs_19_ = f32[3,512,1024]{2,1,0:T(8,128)} custom-call(s32[3]{0:T(128)} %pad_add_fusion.place, bf16[1024,2048]{1,0:T(8,128)(2,1)} %refs_0_.4, bf16[1024,2048]{1,0:T(8,128)(2,1)} %collective-permute-done.refs_1_, bf16[1024,2048]{1,0:T(8,128)(2,1)} %collective-permute-done.14.refs_2_, bf16[1024,2048]{1,0:T(8,128)(2,1)} %collective-permute-done.15.refs_3_, ...), custom_call_target="tpu_custom_call" | custom-call | tf_op jit(solution)/shard_map/project_part/pallas_call | solution.py:145
  231.5 8.8 %project.5 = (bf16[3,256,512]{2,1,0:T(8,128)(2,1)}, bf16[2,256,512]{2,1,0:T(8,128)(2,1)}) custom-call(s32[3]{0:T(128)} %pad_add_fusion.place, bf16[1024,2048]{1,0:T(8,128)(2,1)} %collective-permute-done.1.refs_0_, bf16[256,2048]{1,0:T(8,128)(2,1)} %collective-permute-done.2.refs_1_, bf16[3,4096,1024]{2,1,0:T(8,128)(2,1)} %bitcast.20, ...), custom_call_target="tpu_custom_call" | custom-call | tf_op jit(solution)/shard_map/project/pallas_call | solution.py:145
  241.5 22.8 %project_part.5.refs_19_ = f32[3,512,1024]{2,1,0:T(8,128)} custom-call(s32[3]{0:T(128)} %pad_add_fusion.place, bf16[1024,2048]{1,0:T(8,128)(2,1)} %refs_0_.4, bf16[1024,2048]{1,0:T(8,128)(2,1)} %collective-permute-done.refs_1_, bf16[1024,2048]{1,0:T(8,128)(2,1)} %collective-permute-done.14.refs_2_, bf16[1024,2048]{1,0:T(8,128)(2,1)} %collective-permute-done.15.refs_3_, ...), custom_call_target="tpu_custom_call" | custom-call | tf_op jit(solution)/shard_map/project_part/pallas_call | solution.py:145
  265.3 8.8 %project.6 = (bf16[3,256,512]{2,1,0:T(8,128)(2,1)}, bf16[2,256,512]{2,1,0:T(8,128)(2,1)}) custom-call(s32[3]{0:T(128)} %pad_add_fusion.place, bf16[1024,2048]{1,0:T(8,128)(2,1)} %collective-permute-done.1.refs_0_, bf16[256,2048]{1,0:T(8,128)(2,1)} %copy-done.21, bf16[3,4096,1024]{2,1,0:T(8,128)(2,1)} %bitcast.22, bf16[3,256,1024]{2,1,0:T(8,128)(2,1)} %copy-done.7, ...), custom_call_target="tpu_custom_call" | custom-call | tf_op jit(solution)/shard_map/project/pallas_call | solution.py:145
  274.5 1.3 collective-permute-start.26
  275.9 1.3 collective-permute-start.21
  278.3 8.8 %project.9 = (bf16[3,256,512]{2,1,0:T(8,128)(2,1)}, bf16[2,256,512]{2,1,0:T(8,128)(2,1)}) custom-call(s32[3]{0:T(128)} %pad_add_fusion.place, bf16[1024,2048]{1,0:T(8,128)(2,1)} %collective-permute-done.1.refs_0_, bf16[256,2048]{1,0:T(8,128)(2,1)} %copy-done.20, bf16[3,4096,1024]{2,1,0:T(8,128)(2,1)} %bitcast.23, bf16[3,256,1024]{2,1,0:T(8,128)(2,1)} %copy-done.7, ...), custom_call_target="tpu_custom_call" | custom-call | tf_op jit(solution)/shard_map/project/pallas_call | solution.py:145
  288.4 3.1 scan.5
  292.3 7.7 %project.8 = (bf16[3,128,512]{2,1,0:T(8,128)(2,1)}, bf16[2,128,512]{2,1,0:T(8,128)(2,1)}) custom-call(s32[3]{0:T(128)} %pad_add_fusion.place, bf16[1024,2048]{1,0:T(8,128)(2,1)} %collective-permute-done.1.refs_0_, bf16[128,2048]{1,0:T(8,128)(2,1)} %copy-done.23, bf16[3,4096,1024]{2,1,0:T(8,128)(2,1)} %bitcast.24, bf16[3,256,1024]{2,1,0:T(8,128)(2,1)} %copy-done.7, ...), custom_call_target="tpu_custom_call" | custom-call | tf_op jit(solution)/shard_map/project/pallas_call | solution.py:145
  300.5 3.1 scan.6
  304.3 7.7 %project.7 = (bf16[3,128,512]{2,1,0:T(8,128)(2,1)}, bf16[2,128,512]{2,1,0:T(8,128)(2,1)}) custom-call(s32[3]{0:T(128)} %pad_add_fusion.place, bf16[1024,2048]{1,0:T(8,128)(2,1)} %collective-permute-done.1.refs_0_, bf16[128,2048]{1,0:T(8,128)(2,1)} %copy-done.22, bf16[3,4096,1024]{2,1,0:T(8,128)(2,1)} %bitcast.25, bf16[3,256,1024]{2,1,0:T(8,128)(2,1)} %copy-done.7, ...), custom_call_target="tpu_custom_call" | custom-call | tf_op jit(solution)/shard_map/project/pallas_call | solution.py:145
  313.3 3.1 scan.7
  316.3 1.5 scan.8
  318.3 1.5 scan.9
  319.9 2.8 collective-permute-start.30
  324.4 2.0 collective-permute-done.31.refs_2_
  326.3 1.6 collective-permute-done.32.refs_3_
  328.0 9.9 %finish.1 = bf16[512,2048]{1,0:T(8,128)(2,1)} custom-call(s32[3]{0:T(128)S(1)} %copy-done.5, s32[8]{0:T(128)S(1)} %copy-done.6, f32[16,8,128]{2,1,0:T(8,128)S(1)} %get-tuple-element.79.refs_0_, f32[16,8,128]{2,1,0:T(8,128)S(1)} %collective-permute-done.30.refs_1_, f32[16,8,128]{2,1,0:T(8,128)S(1)} %collective-permute-done.31.refs_2_, ...), custom_call_target="tpu_custom_call" | custom-call | flops 33554432 | bytes 8388608 | tf_op jit(solution)/shard_map/finish/pallas_call | solution.py:380
  (97 shorter events, 17.0 us)
Async XLA Ops:
  0.0 91.8 %collective-permute-start = (bf16[1024,2048]{1,0:T(8,128)(2,1)}, bf16[1024,2048]{1,0:T(8,128)(2,1)}, u32[]{:S(2)}, u32[]{:S(2)}) collective-permute-start(bf16[1024,2048]{1,0:T(8,128)(2,1)} %refs_0_.4), channel_id=1, source_target_pairs={{0,2},{2,0},{4,6},{6,4},{1,3},{3,1},{5,7},{7,5},{8,10},{10,8},{12,... | collective-permute-start | bytes 12582920 | tf_op jit(solution)/shard_map/ppermute | solution.py:412
  0.0 95.0 %collective-permute-start.14 = (bf16[1024,2048]{1,0:T(8,128)(2,1)}, bf16[1024,2048]{1,0:T(8,128)(2,1)}, u32[]{:S(2)}, u32[]{:S(2)}) collective-permute-start(bf16[1024,2048]{1,0:T(8,128)(2,1)} %refs_0_.4), channel_id=1, source_target_pairs={{2,4},{4,2},{3,5},{5,3},{10,12},{12,10},{11,13},{13,11},{18,20},{2... | collective-permute-start | bytes 12582920 | tf_op jit(solution)/shard_map/ppermute | solution.py:413
  9.3 34.8 %collective-permute-start.3 = (bf16[3,256,1024]{2,1,0:T(8,128)(2,1)S(1)}, bf16[3,256,1024]{2,1,0:T(8,128)(2,1)S(1)}, u32[]{:S(2)}, u32[]{:S(2)}) collective-permute-start(bf16[3,256,1024]{2,1,0:T(8,128)(2,1)S(1)} %get-tuple-element.87), channel_id=1, source_target_pairs={{0,1},{1,0},{2,3},{3,2},{4,5},{5,4},{6,7},{7,6},{8,9},{9,8},{10,11... | collective-permute-start | bytes 4718600 | tf_op jit(solution)/shard_map/ppermute | solution.py:27
  10.5 67.2 %collective-permute-start.4 = (bf16[3,256,1024]{2,1,0:T(8,128)(2,1)S(1)}, bf16[3,256,1024]{2,1,0:T(8,128)(2,1)S(1)}, u32[]{:S(2)}, u32[]{:S(2)}) collective-permute-start(bf16[3,256,1024]{2,1,0:T(8,128)(2,1)S(1)} %get-tuple-element.86), channel_id=1, source_target_pairs={{0,1},{1,0},{2,3},{3,2},{4,5},{5,4},{6,7},{7,6},{8,9},{9,8},{10,11... | collective-permute-start | bytes 4718600 | tf_op jit(solution)/shard_map/ppermute | solution.py:27
  44.0 111.2 %copy-start.7 = (bf16[3,256,1024]{2,1,0:T(8,128)(2,1)}, bf16[3,256,1024]{2,1,0:T(8,128)(2,1)S(1)}, u32[]{:S(2)}) copy-start(bf16[3,256,1024]{2,1,0:T(8,128)(2,1)S(1)} %collective-permute-done.3.refs_3_.refs_5_) | copy-start | bytes 4718596
  44.0 34.9 %collective-permute-start.7 = (bf16[3,256,1024]{2,1,0:T(8,128)(2,1)S(1)}, bf16[3,256,1024]{2,1,0:T(8,128)(2,1)S(1)}, u32[]{:S(2)}, u32[]{:S(2)}) collective-permute-start(bf16[3,256,1024]{2,1,0:T(8,128)(2,1)S(1)} %collective-permute-done.3.refs_3_.refs_5_), channel_id=1, source_target_pairs={{0,16},{8,24},{16,0},{24,8},{1,17},{9,25},{17,1},{25,9},{2,18},{10... | collective-permute-start | bytes 4718600 | tf_op jit(solution)/shard_map/ppermute | solution.py:27
  45.2 35.0 %collective-permute-start.6 = (bf16[3,256,1024]{2,1,0:T(8,128)(2,1)S(1)}, bf16[3,256,1024]{2,1,0:T(8,128)(2,1)S(1)}, u32[]{:S(2)}, u32[]{:S(2)}) collective-permute-start(bf16[3,256,1024]{2,1,0:T(8,128)(2,1)S(1)} %collective-permute-done.3.refs_3_.refs_5_), channel_id=1, source_target_pairs={{0,8},{8,0},{16,24},{24,16},{1,9},{9,1},{17,25},{25,17},{2,10},{10... | collective-permute-start | bytes 4718600 | tf_op jit(solution)/shard_map/ppermute | solution.py:27
  77.7 77.5 %copy-start.8 = (bf16[3,256,1024]{2,1,0:T(8,128)(2,1)}, bf16[3,256,1024]{2,1,0:T(8,128)(2,1)S(1)}, u32[]{:S(2)}) copy-start(bf16[3,256,1024]{2,1,0:T(8,128)(2,1)S(1)} %collective-permute-done.4.refs_4_.refs_6_) | copy-start | bytes 4718596
  77.7 33.9 %collective-permute-start.5 = (bf16[3,256,1024]{2,1,0:T(8,128)(2,1)S(1)}, bf16[3,256,1024]{2,1,0:T(8,128)(2,1)S(1)}, u32[]{:S(2)}, u32[]{:S(2)}) collective-permute-start(bf16[3,256,1024]{2,1,0:T(8,128)(2,1)S(1)} %get-tuple-element.45), channel_id=1, source_target_pairs={{0,1},{1,0},{2,3},{3,2},{4,5},{5,4},{6,7},{7,6},{8,9},{9,8},{10,11... | collective-permute-start | bytes 4718600 | tf_op jit(solution)/shard_map/ppermute | solution.py:27
  79.0 34.9 %copy-start.9 = (bf16[3,256,1024]{2,1,0:T(8,128)(2,1)}, bf16[3,256,1024]{2,1,0:T(8,128)(2,1)S(1)}, u32[]{:S(2)}) copy-start(bf16[3,256,1024]{2,1,0:T(8,128)(2,1)S(1)} %collective-permute-done.7.refs_7_.refs_13_.refs_11_) | copy-start | bytes 4718596
  79.0 33.7 %collective-permute-start.12 = (bf16[3,256,1024]{2,1,0:T(8,128)(2,1)S(1)}, bf16[3,256,1024]{2,1,0:T(8,128)(2,1)}, u32[]{:S(2)}, u32[]{:S(2)}) collective-permute-start(bf16[3,256,1024]{2,1,0:T(8,128)(2,1)S(1)} %collective-permute-done.4.refs_4_.refs_6_), channel_id=1, source_target_pairs={{0,16},{8,24},{16,0},{24,8},{1,17},{9,25},{17,1},{25,9},{2,18},{10... | collective-permute-start | bytes 4718600 | tf_op jit(solution)/shard_map/ppermute | solution.py:27
  80.2 34.0 %copy-start.10 = (bf16[3,256,1024]{2,1,0:T(8,128)(2,1)}, bf16[3,256,1024]{2,1,0:T(8,128)(2,1)S(1)}, u32[]{:S(2)}) copy-start(bf16[3,256,1024]{2,1,0:T(8,128)(2,1)S(1)} %collective-permute-done.6.refs_5_.refs_9_.refs_7_) | copy-start | bytes 4718596
  80.2 32.4 %collective-permute-start.8 = (bf16[3,256,1024]{2,1,0:T(8,128)(2,1)S(1)}, bf16[3,256,1024]{2,1,0:T(8,128)(2,1)S(1)}, u32[]{:S(2)}, u32[]{:S(2)}) collective-permute-start(bf16[3,256,1024]{2,1,0:T(8,128)(2,1)S(1)} %collective-permute-done.7.refs_7_.refs_13_.refs_11_), channel_id=1, source_target_pairs={{0,8},{8,0},{16,24},{24,16},{1,9},{9,1},{17,25},{25,17},{2,10},{10... | collective-permute-start | bytes 4718600 | tf_op jit(solution)/shard_map/ppermute | solution.py:27
  91.8 92.7 %collective-permute-start.1 = (bf16[1024,2048]{1,0:T(8,128)(2,1)}, bf16[1024,2048]{1,0:T(8,128)(2,1)}, u32[]{:S(2)}, u32[]{:S(2)}) collective-permute-start(bf16[1024,2048]{1,0:T(8,128)(2,1)} %collective-permute-done.refs_1_), channel_id=1, source_target_pairs={{2,4},{4,2},{3,5},{5,3},{10,12},{12,10},{11,13},{13,11},{18,20},{2... | collective-permute-start | bytes 12582920 | tf_op jit(solution)/shard_map/ppermute | solution.py:419
  95.0 90.7 %collective-permute-start.15 = (bf16[1024,2048]{1,0:T(8,128)(2,1)}, bf16[1024,2048]{1,0:T(8,128)(2,1)}, u32[]{:S(2)}, u32[]{:S(2)}) collective-permute-start(bf16[1024,2048]{1,0:T(8,128)(2,1)} %collective-permute-done.14.refs_2_), channel_id=1, source_target_pairs={{2,0},{4,6},{3,1},{5,7},{10,8},{12,14},{11,9},{13,15},{18,16},{20,... | collective-permute-start | bytes 12582920 | tf_op jit(solution)/shard_map/ppermute | solution.py:418
  111.7 33.8 %copy-start.12 = (bf16[3,256,1024]{2,1,0:T(8,128)(2,1)}, bf16[3,256,1024]{2,1,0:T(8,128)(2,1)S(1)}, u32[]{:S(2)}) copy-start(bf16[3,256,1024]{2,1,0:T(8,128)(2,1)S(1)} %collective-permute-done.5.refs_7_.refs_5_) | copy-start | bytes 4718596
  112.6 32.8 %collective-permute-start.17 = (bf16[3,256,1024]{2,1,0:T(8,128)(2,1)S(1)}, bf16[3,256,1024]{2,1,0:T(8,128)(2,1)S(1)}, u32[]{:S(2)}, u32[]{:S(2)}) collective-permute-start(bf16[3,256,1024]{2,1,0:T(8,128)(2,1)S(1)} %collective-permute-done.5.refs_7_.refs_5_), channel_id=1, source_target_pairs={{0,16},{8,24},{16,0},{24,8},{1,17},{9,25},{17,1},{25,9},{2,18},{10... | collective-permute-start | bytes 4718600 | tf_op jit(solution)/shard_map/ppermute | solution.py:27
  113.9 37.5 %collective-permute-start.9 = (bf16[3,256,1024]{2,1,0:T(8,128)(2,1)}, bf16[3,256,1024]{2,1,0:T(8,128)(2,1)}, u32[]{:S(2)}, u32[]{:S(2)}) collective-permute-start(bf16[3,256,1024]{2,1,0:T(8,128)(2,1)} %get-tuple-element.48), channel_id=1, source_target_pairs={{0,1},{1,0},{2,3},{3,2},{4,5},{5,4},{6,7},{7,6},{8,9},{9,8},{10,11... | collective-permute-start | bytes 4718600 | tf_op jit(solution)/shard_map/ppermute | solution.py:27
  114.2 37.1 %collective-permute-start.10 = (bf16[3,256,1024]{2,1,0:T(8,128)(2,1)S(1)}, bf16[3,256,1024]{2,1,0:T(8,128)(2,1)}, u32[]{:S(2)}, u32[]{:S(2)}) collective-permute-start(bf16[3,256,1024]{2,1,0:T(8,128)(2,1)S(1)} %collective-permute-done.4.refs_4_.refs_6_), channel_id=1, source_target_pairs={{0,8},{8,0},{16,24},{24,16},{1,9},{9,1},{17,25},{25,17},{2,10},{10... | collective-permute-start | bytes 4718600 | tf_op jit(solution)/shard_map/ppermute | solution.py:27
  146.6 7.4 %collective-permute-start.13 = (bf16[3,256,1024]{2,1,0:T(8,128)(2,1)}, bf16[3,256,1024]{2,1,0:T(8,128)(2,1)}, u32[]{:S(2)}, u32[]{:S(2)}) collective-permute-start(bf16[3,256,1024]{2,1,0:T(8,128)(2,1)} %collective-permute-done.12.refs_8_.refs_14_.refs_12_), channel_id=1, source_target_pairs={{0,8},{8,0},{16,24},{24,16},{1,9},{9,1},{17,25},{25,17},{2,10},{10... | collective-permute-start | bytes 4718600 | tf_op jit(solution)/shard_map/ppermute | solution.py:27
  154.0 35.8 %collective-permute-start.18 = (bf16[3,256,1024]{2,1,0:T(8,128)(2,1)}, bf16[3,256,1024]{2,1,0:T(8,128)(2,1)S(1)}, u32[]{:S(2)}, u32[]{:S(2)}) collective-permute-start(bf16[3,256,1024]{2,1,0:T(8,128)(2,1)} %collective-permute-done.9.refs_8_.refs_6_), channel_id=1, source_target_pairs={{0,16},{8,24},{16,0},{24,8},{1,17},{9,25},{17,1},{25,9},{2,18},{10... | collective-permute-start | bytes 4718600 | tf_op jit(solution)/shard_map/ppermute | solution.py:27
  155.3 32.6 %copy-start.13 = (bf16[3,256,1024]{2,1,0:T(8,128)(2,1)S(1)}, bf16[3,256,1024]{2,1,0:T(8,128)(2,1)}, u32[]{:S(2)}) copy-start(bf16[3,256,1024]{2,1,0:T(8,128)(2,1)} %copy-done.12) | copy-start | bytes 4718596
  155.3 32.6 %copy-start.15 = (bf16[3,256,1024]{2,1,0:T(8,128)(2,1)S(1)}, bf16[3,256,1024]{2,1,0:T(8,128)(2,1)}, u32[]{:S(2)}) copy-start(bf16[3,256,1024]{2,1,0:T(8,128)(2,1)} %copy-done.14) | copy-start | bytes 4718596
  185.7 7.6 %collective-permute-start.16 = (bf16[3,256,1024]{2,1,0:T(8,128)(2,1)}, bf16[3,256,1024]{2,1,0:T(8,128)(2,1)S(1)}, u32[]{:S(2)}, u32[]{:S(2)}) collective-permute-start(bf16[3,256,1024]{2,1,0:T(8,128)(2,1)} %collective-permute-done.9.refs_8_.refs_6_), channel_id=1, source_target_pairs={{0,8},{8,0},{16,24},{24,16},{1,9},{9,1},{17,25},{25,17},{2,10},{10... | collective-permute-start | bytes 4718600 | tf_op jit(solution)/shard_map/ppermute | solution.py:27
  187.8 16.0 %collective-permute-start.11 = (bf16[3,256,1024]{2,1,0:T(8,128)(2,1)S(1)}, bf16[3,256,1024]{2,1,0:T(8,128)(2,1)S(1)}, u32[]{:S(2)}, u32[]{:S(2)}) collective-permute-start(bf16[3,256,1024]{2,1,0:T(8,128)(2,1)S(1)} %copy-done.13), channel_id=1, source_target_pairs={{0,8},{8,0},{16,24},{24,16},{1,9},{9,1},{17,25},{25,17},{2,10},{10... | collective-permute-start | bytes 4718600 | tf_op jit(solution)/shard_map/ppermute | solution.py:27
  187.8 19.9 %collective-permute-start.19 = (bf16[3,256,1024]{2,1,0:T(8,128)(2,1)S(1)}, bf16[3,256,1024]{2,1,0:T(8,128)(2,1)S(1)}, u32[]{:S(2)}, u32[]{:S(2)}) collective-permute-start(bf16[3,256,1024]{2,1,0:T(8,128)(2,1)S(1)} %copy-done.15), channel_id=1, source_target_pairs={{0,8},{8,0},{16,24},{24,16},{1,9},{9,1},{17,25},{25,17},{2,10},{10... | collective-permute-start | bytes 4718600 | tf_op jit(solution)/shard_map/ppermute | solution.py:27
  193.2 15.6 %collective-permute-start.20 = (bf16[3,256,1024]{2,1,0:T(8,128)(2,1)S(1)}, bf16[3,256,1024]{2,1,0:T(8,128)(2,1)}, u32[]{:S(2)}, u32[]{:S(2)}) collective-permute-start(bf16[3,256,1024]{2,1,0:T(8,128)(2,1)S(1)} %collective-permute-done.18.refs_16_.refs_14_), channel_id=1, source_target_pairs={{0,8},{8,0},{16,24},{24,16},{1,9},{9,1},{17,25},{25,17},{2,10},{10... | collective-permute-start | bytes 4718600 | tf_op jit(solution)/shard_map/ppermute | solution.py:27
  197.4 34.1 %collective-permute-start.2 = (bf16[256,2048]{1,0:T(8,128)(2,1)}, bf16[256,2048]{1,0:T(8,128)(2,1)}, u32[]{:S(2)}, u32[]{:S(2)}) collective-permute-start(bf16[256,2048]{1,0:T(8,128)(2,1)} %get-tuple-element.91), channel_id=1, source_target_pairs={{2,0},{4,6},{3,1},{5,7},{10,8},{12,14},{11,9},{13,15},{18,16},{20,... | collective-permute-start | bytes 3145736 | tf_op jit(solution)/shard_map/ppermute | solution.py:522
  202.5 61.8 %collective-permute-start.22 = (bf16[256,2048]{1,0:T(8,128)(2,1)}, bf16[256,2048]{1,0:T(8,128)(2,1)S(1)}, u32[]{:S(2)}, u32[]{:S(2)}) collective-permute-start(bf16[256,2048]{1,0:T(8,128)(2,1)} %get-tuple-element.90), channel_id=1, source_target_pairs={{2,0},{4,6},{3,1},{5,7},{10,8},{12,14},{11,9},{13,15},{18,16},{20,... | collective-permute-start | bytes 3145736 | tf_op jit(solution)/shard_map/ppermute | solution.py:522
  203.9 73.4 %collective-permute-start.28 = (bf16[256,2048]{1,0:T(8,128)(2,1)}, bf16[256,2048]{1,0:T(8,128)(2,1)S(1)}, u32[]{:S(2)}, u32[]{:S(2)}) collective-permute-start(bf16[256,2048]{1,0:T(8,128)(2,1)} %get-tuple-element.89), channel_id=1, source_target_pairs={{2,0},{4,6},{3,1},{5,7},{10,8},{12,14},{11,9},{13,15},{18,16},{20,... | collective-permute-start | bytes 3145736 | tf_op jit(solution)/shard_map/ppermute | solution.py:522
  240.3 48.1 %collective-permute-start.24 = (bf16[2,256,512]{2,1,0:T(8,128)(2,1)}, bf16[2,256,512]{2,1,0:T(8,128)(2,1)S(1)}, u32[]{:S(2)}, u32[]{:S(2)}) collective-permute-start(bf16[2,256,512]{2,1,0:T(8,128)(2,1)} %get-tuple-element.65), channel_id=1, source_target_pairs={{0,1},{1,0},{2,3},{3,2},{4,5},{5,4},{6,7},{7,6},{8,9},{9,8},{10,11... | collective-permute-start | bytes 1572872 | tf_op jit(solution)/shard_map/ppermute | solution.py:27
  264.2 13.0 %copy-start.24 = (f32[512,16]{0,1:T(8,128)S(1)}, f32[512,16]{0,1:T(8,128)}, u32[]{:S(2)}) copy-start(f32[512,16]{0,1:T(8,128)} %param.8) | copy-start | bytes 98308
  264.2 13.0 %copy-start.25 = (f32[512,16]{0,1:T(8,128)S(1)}, f32[512,16]{0,1:T(8,128)}, u32[]{:S(2)}) copy-start(f32[512,16]{0,1:T(8,128)} %param.9) | copy-start | bytes 98308
  274.1 26.4 %collective-permute-start.23 = (bf16[2,256,512]{2,1,0:T(8,128)(2,1)}, bf16[2,256,512]{2,1,0:T(8,128)(2,1)S(1)}, u32[]{:S(2)}, u32[]{:S(2)}) collective-permute-start(bf16[2,256,512]{2,1,0:T(8,128)(2,1)} %get-tuple-element.64), channel_id=1, source_target_pairs={{0,1},{1,0},{2,3},{3,2},{4,5},{5,4},{6,7},{7,6},{8,9},{9,8},{10,11... | collective-permute-start | bytes 1572872 | tf_op jit(solution)/shard_map/ppermute | solution.py:27
  274.5 16.9 %collective-permute-start.26 = (bf16[128,2048]{1,0:T(8,128)(2,1)}, bf16[128,2048]{1,0:T(8,128)(2,1)S(1)}, u32[]{:S(2)}, u32[]{:S(2)}) collective-permute-start(bf16[128,2048]{1,0:T(8,128)(2,1)} %get-tuple-element.71), channel_id=1, source_target_pairs={{2,0},{4,6},{3,1},{5,7},{10,8},{12,14},{11,9},{13,15},{18,16},{20,... | collective-permute-start | bytes 1572872 | tf_op jit(solution)/shard_map/ppermute | solution.py:522
  275.9 27.7 %collective-permute-start.21 = (bf16[128,2048]{1,0:T(8,128)(2,1)}, bf16[128,2048]{1,0:T(8,128)(2,1)S(1)}, u32[]{:S(2)}, u32[]{:S(2)}) collective-permute-start(bf16[128,2048]{1,0:T(8,128)(2,1)} %get-tuple-element.61), channel_id=1, source_target_pairs={{2,0},{4,6},{3,1},{5,7},{10,8},{12,14},{11,9},{13,15},{18,16},{20,... | collective-permute-start | bytes 1572872 | tf_op jit(solution)/shard_map/ppermute | solution.py:522
  277.2 11.0 %copy-start.26 = (f32[512]{0:T(512)S(1)}, f32[512]{0:T(512)}, u32[]{:S(2)}) copy-start(f32[512]{0:T(512)} %param.10) | copy-start | bytes 6148
  277.3 11.1 %copy-start = (bf16[3,256,512]{2,1,0:T(8,128)(2,1)S(1)}, bf16[3,256,512]{2,1,0:T(8,128)(2,1)}, u32[]{:S(2)}) copy-start(bf16[3,256,512]{2,1,0:T(8,128)(2,1)} %get-tuple-element.59.kept.refs_11_) | copy-start | bytes 2359300
  287.1 26.2 %collective-permute-start.29 = (bf16[2,256,512]{2,1,0:T(8,128)(2,1)}, bf16[2,256,512]{2,1,0:T(8,128)(2,1)S(1)}, u32[]{:S(2)}, u32[]{:S(2)}) collective-permute-start(bf16[2,256,512]{2,1,0:T(8,128)(2,1)} %get-tuple-element.76), channel_id=1, source_target_pairs={{0,1},{1,0},{2,3},{3,2},{4,5},{5,4},{6,7},{7,6},{8,9},{9,8},{10,11... | collective-permute-start | bytes 1572872 | tf_op jit(solution)/shard_map/ppermute | solution.py:27
  292.3 8.2 %copy-start.1 = (bf16[3,256,512]{2,1,0:T(8,128)(2,1)S(1)}, bf16[3,256,512]{2,1,0:T(8,128)(2,1)}, u32[]{:S(2)}) copy-start(bf16[3,256,512]{2,1,0:T(8,128)(2,1)} %get-tuple-element.63.kept.refs_12_) | copy-start | bytes 2359300
  300.0 16.3 %collective-permute-start.27 = (bf16[2,128,512]{2,1,0:T(8,128)(2,1)}, bf16[2,128,512]{2,1,0:T(8,128)(2,1)S(1)}, u32[]{:S(2)}, u32[]{:S(2)}) collective-permute-start(bf16[2,128,512]{2,1,0:T(8,128)(2,1)} %get-tuple-element.74), channel_id=1, source_target_pairs={{0,1},{1,0},{2,3},{3,2},{4,5},{5,4},{6,7},{7,6},{8,9},{9,8},{10,11... | collective-permute-start | bytes 786440 | tf_op jit(solution)/shard_map/ppermute | solution.py:27
  304.3 8.9 %copy-start.2 = (bf16[3,256,512]{2,1,0:T(8,128)(2,1)S(1)}, bf16[3,256,512]{2,1,0:T(8,128)(2,1)}, u32[]{:S(2)}) copy-start(bf16[3,256,512]{2,1,0:T(8,128)(2,1)} %get-tuple-element.75.kept.refs_13_) | copy-start | bytes 2359300
  312.1 6.3 %collective-permute-start.25 = (bf16[2,128,512]{2,1,0:T(8,128)(2,1)}, bf16[2,128,512]{2,1,0:T(8,128)(2,1)S(1)}, u32[]{:S(2)}, u32[]{:S(2)}) collective-permute-start(bf16[2,128,512]{2,1,0:T(8,128)(2,1)} %get-tuple-element.70), channel_id=1, source_target_pairs={{0,1},{1,0},{2,3},{3,2},{4,5},{5,4},{6,7},{7,6},{8,9},{9,8},{10,11... | collective-permute-start | bytes 786440 | tf_op jit(solution)/shard_map/ppermute | solution.py:27
  313.3 14.7 %copy-start.5 = (s32[3]{0:T(128)S(1)}, s32[3]{0:T(128)}, u32[]{:S(2)}) copy-start(s32[3]{0:T(128)} %pad_add_fusion.place) | copy-start | bytes 40
  313.3 14.7 %copy-start.6 = (s32[8]{0:T(128)S(1)}, s32[8]{0:T(128)}, u32[]{:S(2)}) copy-start(s32[8]{0:T(128)} %order.1) | copy-start | bytes 100
  319.9 4.5 %collective-permute-start.30 = (f32[16,8,128]{2,1,0:T(8,128)S(1)}, f32[16,8,128]{2,1,0:T(8,128)S(1)}, u32[]{:S(2)}, u32[]{:S(2)}) collective-permute-start(f32[16,8,128]{2,1,0:T(8,128)S(1)} %get-tuple-element.79.refs_0_), channel_id=1, source_target_pairs={{0,8},{8,0},{16,24},{24,16},{1,9},{9,1},{17,25},{25,17},{2,10},{10... | collective-permute-start | bytes 196616 | tf_op jit(solution)/shard_map/ppermute | solution.py:27
  322.7 3.7 %collective-permute-start.31 = (f32[16,8,128]{2,1,0:T(8,128)S(1)}, f32[16,8,128]{2,1,0:T(8,128)S(1)}, u32[]{:S(2)}, u32[]{:S(2)}) collective-permute-start(f32[16,8,128]{2,1,0:T(8,128)S(1)} %get-tuple-element.79.refs_0_), channel_id=1, source_target_pairs={{0,16},{8,24},{16,0},{24,8},{1,17},{9,25},{17,1},{25,9},{2,18},{10... | collective-permute-start | bytes 196616 | tf_op jit(solution)/shard_map/ppermute | solution.py:27
  323.7 4.2 %collective-permute-start.32 = (f32[16,8,128]{2,1,0:T(8,128)S(1)}, f32[16,8,128]{2,1,0:T(8,128)S(1)}, u32[]{:S(2)}, u32[]{:S(2)}) collective-permute-start(f32[16,8,128]{2,1,0:T(8,128)S(1)} %get-tuple-element.79.refs_0_), channel_id=1, source_target_pairs={{0,24},{8,16},{16,8},{24,0},{1,25},{9,17},{17,9},{25,1},{2,26},{10... | collective-permute-start | bytes 196616 | tf_op jit(solution)/shard_map/ppermute | solution.py:27
  (12 other events, 38.4 us)
